TPU v7x, 512 devices: a whole 4x4x16 slice. The times are simulated.
512 devices in a mesh: seq: 64 (over y, z), tp: 8 (over x, core).
Axes of the slice: x: 4, y: 4, z: 16, core: 2. Of those that a mesh axis runs over, the one named last changes fastest.
Arguments:
- queries: bfloat16 [16384, 8, 8, 128], P('seq', None, 'tp'), may hold values from -6 to 6
- keys: bfloat16 [16384, 8, 128], P('seq'), may hold values from -6 to 6
- values: bfloat16 [16384, 8, 128], P('seq'), may hold values from -6 to 6
- grad_out: bfloat16 [16384, 8, 8, 128], P('seq', None, 'tp'), may hold values from -6 to 6
- exponents: int32 [128, 8, 8], P('seq', None, 'tp'), may hold values from -2 to 2
- lengths: int32 [128], replicated, may hold values from 1 to 256, 16384 in all
Outputs:
- grad_queries: bfloat16 [16384, 8, 8, 128], P('seq', None, 'tp')
- grad_keys: bfloat16 [16384, 8, 128], P('seq', 'tp')
- grad_values: bfloat16 [16384, 8, 128], P('seq', 'tp')
Inputs may be any that keep to these rules, and one draw needn't show every extreme that they name: No document has more than 256 tokens (at least one has exactly 256); the lengths sum to 16384. `exponents`: one exponent for each block of 128 tokens of one query head.
All inputs are finite; a program needn't handle non-finite values.
Results may differ from a plain program's by a relative error of at most 0.03.
Values may be sent and summed in bfloat16 or wider, within the bound.
No kernel may reach another device: no remote copies, remote signals or barrier semaphores. Data moves between devices by JAX's collectives and lax.ppermute only.
A program may use at most 64 MiB of HBM per device.

v0:
```python
import jax
import jax.numpy as jnp
from jax import lax
from jax.sharding import PartitionSpec as P


def passed_along(block, axis, distance):
    devices = range(lax.axis_size(axis))
    route = [(i - distance, i) for i in devices if i - distance in devices]
    return lax.ppermute(block, axis, route)


def window_docs(lengths, first_row, count):
    positions = first_row + jnp.arange(count, dtype=jnp.int32)
    doc_ends = jnp.cumsum(lengths)
    return (positions, jnp.sum((doc_ends[None, :] <= positions[:, None]).astype(jnp.int32), axis=1))


def group_grads(query_grp, dout_grp, key_window, value_window, allowed, scaling):
    scores = (
        jnp.einsum("qrd,kd->rqk", query_grp, key_window, preferred_element_type=jnp.float32)
        * scaling
    )
    scores = jnp.where(allowed[None], scores, -1e30)
    row_max = jnp.max(scores, axis=-1, keepdims=True)
    shifted = jnp.exp(scores - row_max)
    row_sum = jnp.sum(shifted, axis=-1, keepdims=True)
    attn_w = shifted / row_sum
    attn_low = attn_w.astype(jnp.bfloat16)
    attn_out = jnp.einsum(
        "rqk,kd->qrd", attn_low, value_window, preferred_element_type=jnp.float32
    ).astype(jnp.bfloat16)
    row_delta = jnp.transpose(
        jnp.sum(dout_grp.astype(jnp.float32) * attn_out.astype(jnp.float32), axis=-1)
    )[..., None]
    grad_probs = jnp.einsum(
        "qrd,kd->rqk", dout_grp, value_window, preferred_element_type=jnp.float32
    )
    grad_low = (scaling * attn_w * (grad_probs - row_delta)).astype(jnp.bfloat16)
    grad_query = jnp.einsum(
        "rqk,kd->qrd", grad_low, key_window, preferred_element_type=jnp.float32
    ).astype(jnp.bfloat16)
    return (attn_low, grad_low, grad_query, row_max[..., 0], row_sum[..., 0], row_delta[..., 0])


def core_grads(queries, scaled, keys, values, lengths, scaling):
    row_count = queries.shape[0]
    first_row = lax.axis_index("seq") * row_count
    earlier_keys, earlier_values = passed_along((keys, values), "seq", 1)
    key_window = jnp.moveaxis(jnp.concatenate([earlier_keys, keys], axis=0), 1, 0)
    value_window = jnp.moveaxis(jnp.concatenate([earlier_values, values], axis=0), 1, 0)
    query_pos, query_doc = window_docs(lengths, first_row, row_count)
    key_pos, key_doc = window_docs(lengths, first_row - row_count, 2 * row_count)
    allowed = (
        (query_doc[:, None] == key_doc[None, :])
        & (key_pos[None, :] <= query_pos[:, None])
        & (key_pos[None, :] >= 0)
    )
    query_major = jnp.moveaxis(queries, 1, 0)
    dout_major = jnp.moveaxis(scaled, 1, 0)

    def full_group(inputs):
        query_grp, dout_grp, key_grp, value_grp = inputs
        attn_low, grad_low, grad_query, row_max, row_sum, row_delta = group_grads(
            query_grp, dout_grp, key_grp, value_grp, allowed, scaling
        )
        grad_key = jnp.einsum(
            "rqk,qrd->kd", grad_low, query_grp, preferred_element_type=jnp.float32
        )
        grad_value = jnp.einsum(
            "rqk,qrd->kd", attn_low, dout_grp, preferred_element_type=jnp.float32
        )
        return (grad_query, grad_key, grad_value)

    grad_query, key_terms, value_terms = lax.map(
        full_group, (query_major, dout_major, key_window, value_window)
    )
    back_keys, back_values = (
        passed_along(key_terms[:, :row_count].astype(jnp.bfloat16), "seq", -1).astype(jnp.float32),
        passed_along(value_terms[:, :row_count].astype(jnp.bfloat16), "seq", -1).astype(
            jnp.float32
        ),
    )
    key_total = key_terms[:, row_count:] + back_keys
    value_total = value_terms[:, row_count:] + back_values
    return (grad_query, key_total, value_total)


def per_device(queries, keys, values, grad_out, exponents, lengths):
    row_count, groups, local_heads, head_width = queries.shape
    scaling = head_width ** (-0.5)
    exp_block = row_count // exponents.shape[0]
    factor = jnp.exp2(exponents.astype(jnp.float32)).astype(jnp.bfloat16)
    scaled = (
        grad_out.reshape(row_count // exp_block, exp_block, groups, local_heads, head_width)
        * factor[:, None, :, :, None]
    )
    scaled = scaled.reshape(row_count, groups, local_heads, head_width)
    grad_query, key_total, value_total = core_grads(queries, scaled, keys, values, lengths, scaling)
    summed_keys, summed_values = (
        lax.psum_scatter(key_total, "tp", scatter_dimension=0, tiled=True),
        lax.psum_scatter(value_total, "tp", scatter_dimension=0, tiled=True),
    )
    grad_queries = jnp.moveaxis(grad_query, 0, 1)
    grad_keys = jnp.moveaxis(summed_keys, 0, 1).astype(jnp.bfloat16)
    grad_values = jnp.moveaxis(summed_values, 0, 1).astype(jnp.bfloat16)
    return (grad_queries, grad_keys, grad_values)


def solution(mesh):
    placed = (
        P("seq", None, "tp", None),
        P("seq", None, None),
        P("seq", None, None),
        P("seq", None, "tp", None),
        P("seq", None, "tp"),
        P(),
    )
    return jax.shard_map(
        per_device,
        mesh=mesh,
        in_specs=placed,
        out_specs=(P("seq", None, "tp", None), P("seq", "tp", None), P("seq", "tp", None)),
        check_vma=False,
    )
```

profile of v0, /device:TPU:24, one launch (start us, length us, event | category | flops | bytes accessed | tf_op | source)
XLA Modules:
  0.0 199.5 jit_solution(16353359951570236641)
XLA Ops:
  7.3 1.2 copy.28
  8.4 3.8 %collective-permute-start.1 = (bf16[256,8,128]{2,0,1:T(8,128)(2,1)S(1)}, bf16[256,8,128]{2,0,1:T(8,128)(2,1)}, u32[]{:S(2)}, u32[]{:S(2)}) collective-permute-start(bf16[256,8,128]{2,0,1:T(8,128)(2,1)S(1)} %copy.28), channel_id=1, source_target_pairs={{0,8},{8,16},{16,24},{24,32},{32,40},{40,48},{48,56},{56,64},{64,7... | collective-permute-start | bytes 1572872 | tf_op jit(solution)/shard_map/ppermute | solution.py:10
  12.3 1.1 copy.25
  13.4 3.8 %collective-permute-start = (bf16[256,8,128]{2,0,1:T(8,128)(2,1)S(1)}, bf16[256,8,128]{2,0,1:T(8,128)(2,1)}, u32[]{:S(2)}, u32[]{:S(2)}) collective-permute-start(bf16[256,8,128]{2,0,1:T(8,128)(2,1)S(1)} %copy.25), channel_id=1, source_target_pairs={{0,8},{8,16},{16,24},{24,32},{32,40},{40,48},{48,56},{56,64},{64,7... | collective-permute-start | bytes 1572872 | tf_op jit(solution)/shard_map/ppermute | solution.py:10
  18.1 0.3 copy.30
  18.7 0.8 multiply_bitcast_fusion
  19.5 13.4 %collective-permute-done.1 = bf16[256,8,128]{2,0,1:T(8,128)(2,1)} collective-permute-done((bf16[256,8,128]{2,0,1:T(8,128)(2,1)S(1)}, bf16[256,8,128]{2,0,1:T(8,128)(2,1)}, u32[]{:S(2)}, u32[]{:S(2)}) %collective-permute-start.1) | collective-permute-done | bytes 524320 | tf_op jit(solution)/shard_map/ppermute | solution.py:10
  32.9 1.1 maximum_bitcast_fusion.1
  34.0 9.3 %collective-permute-done = bf16[256,8,128]{2,0,1:T(8,128)(2,1)} collective-permute-done((bf16[256,8,128]{2,0,1:T(8,128)(2,1)S(1)}, bf16[256,8,128]{2,0,1:T(8,128)(2,1)}, u32[]{:S(2)}, u32[]{:S(2)}) %collective-permute-start) | collective-permute-done | bytes 524320 | tf_op jit(solution)/shard_map/ppermute | solution.py:10
  43.3 1.1 maximum_bitcast_fusion
  44.4 49.9 %while.15 = (s32[]{:T(128)}, bf16[8,256,1,128]{1,3,2,0:T(8,128)(2,1)}, f32[8,512,128]{2,1,0:T(8,128)}, f32[8,512,128]{2,1,0:T(8,128)}, bf16[8,512,128]{2,1,0:T(8...) while((s32[]{:T(128)}, ...), condition=%wide.region_7.8_spmd.clone, body=%wide.region_3.7_spmd.clone.sunk | while | flops 204274944 | bytes 4873869 | solution.py:75
  44.4 0.3 fusion.77
  44.9 1.1 fusion.79
  46.0 1.1 fusion.80
  47.1 0.9 fusion.81
  47.9 1.8 fusion.83
  49.7 0.9 fusion.82
  51.1 1.1 fusion.79
  52.2 1.1 fusion.80
  53.3 0.9 fusion.81
  54.2 1.8 fusion.83
  56.0 0.9 fusion.82
  57.3 1.1 fusion.79
  58.4 1.1 fusion.80
  59.5 0.9 fusion.81
  60.4 1.8 fusion.83
  62.2 0.9 fusion.82
  63.5 1.1 fusion.79
  64.7 1.1 fusion.80
  65.7 0.9 fusion.81
  66.6 1.8 fusion.83
  68.4 0.9 fusion.82
  69.8 1.1 fusion.79
  70.9 1.1 fusion.80
  72.0 0.9 fusion.81
  72.9 1.8 fusion.83
  74.7 0.9 fusion.82
  76.1 1.1 fusion.79
  77.2 1.1 fusion.80
  78.3 0.9 fusion.81
  79.1 1.8 fusion.83
  80.9 0.9 fusion.82
  82.3 1.1 fusion.79
  83.4 1.1 fusion.80
  84.5 0.9 fusion.81
  85.4 1.8 fusion.83
  87.2 0.9 fusion.82
  88.5 1.1 fusion.79
  89.7 1.1 fusion.80
  90.7 0.9 fusion.81
  91.6 1.8 fusion.83
  93.4 0.9 fusion.82
  94.3 1.3 slice.25
  95.6 3.8 %collective-permute-start.2 = (bf16[8,256,128]{2,1,0:T(8,128)(2,1)S(1)}, bf16[8,256,128]{2,1,0:T(8,128)(2,1)S(1)}, u32[]{:S(2)}, u32[]{:S(2)}) collective-permute-start(bf16[8,256,128]{2,1,0:T(8,128)(2,1)S(1)} %slice.25), channel_id=1, source_target_pairs={{8,0},{16,8},{24,16},{32,24},{40,32},{48,40},{56,48},{64,56},{72,6... | collective-permute-start | bytes 1572872 | tf_op jit(solution)/shard_map/ppermute | solution.py:10
  99.4 11.4 %collective-permute-done.2 = bf16[8,256,128]{2,1,0:T(8,128)(2,1)S(1)} collective-permute-done((bf16[8,256,128]{2,1,0:T(8,128)(2,1)S(1)}, bf16[8,256,128]{2,1,0:T(8,128)(2,1)S(1)}, u32[]{:S(2)}, u32[]{:S(2)}) %collective-permute-start.2) | collective-permute-done | bytes 524320 | tf_op jit(solution)/shard_map/ppermute | solution.py:10
  110.8 2.3 %convert_add_fusion.1 = f32[8,256,128]{2,1,0:T(8,128)} fusion(bf16[8,256,128]{2,1,0:T(8,128)(2,1)S(1)} %collective-permute-done.2, f32[8,512,128]{2,1,0:T(8,128)} %get-tuple-element.53), kind=kLoop, calls=%fused_computation.56 | loop fusion | flops 524288 | bytes 2621440 | tf_op jit(solution)/shard_map/add | solution.py:84
  113.3 5.5 %collective-permute-start.3 = (bf16[8,256,128]{2,1,0:T(8,128)(2,1)S(1)}, bf16[8,256,128]{2,1,0:T(8,128)(2,1)S(1)}, u32[]{:S(2)}, u32[]{:S(2)}) collective-permute-start(bf16[8,256,128]{2,1,0:T(8,128)(2,1)S(1)} %slice.24), channel_id=1, source_target_pairs={{8,0},{16,8},{24,16},{32,24},{40,32},{48,40},{56,48},{64,56},{72,6... | collective-permute-start | bytes 1572872 | tf_op jit(solution)/shard_map/ppermute | solution.py:10
  118.8 9.4 %collective-permute-done.3 = bf16[8,256,128]{2,1,0:T(8,128)(2,1)S(1)} collective-permute-done((bf16[8,256,128]{2,1,0:T(8,128)(2,1)S(1)}, bf16[8,256,128]{2,1,0:T(8,128)(2,1)S(1)}, u32[]{:S(2)}, u32[]{:S(2)}) %collective-permute-start.3) | collective-permute-done | bytes 524320 | tf_op jit(solution)/shard_map/ppermute | solution.py:10
  128.2 1.1 convert_add_fusion
  129.3 1.1 copy.32
  130.4 19.5 %reduce-scatter.3.cloned.1.call-done = f32[1,256,128]{2,1,0:T(8,128)} async-done(((f32[8,256,128]{2,1,0:T(8,128)}), f32[1,256,128]{2,1,0:T(8,128)}) %reduce-scatter.3.cloned.1.call-update) | async-done | bytes 131088 | tf_op jit(solution)/shard_map/reduce_scatter | solution.py:101
  149.9 1.5 convert_bitcast_fusion.1
  151.4 39.7 %reduce-scatter.5.cloned.1.call-done = f32[1,256,128]{2,1,0:T(8,128)} async-done(((f32[8,256,128]{2,1,0:T(8,128)}), f32[1,256,128]{2,1,0:T(8,128)}) %reduce-scatter.5.cloned.1.call-update) | async-done | bytes 131088 | tf_op jit(solution)/shard_map/reduce_scatter | solution.py:102
  191.1 1.5 convert_bitcast_fusion
  (47 shorter events, 4.5 us)
Async XLA Ops:
  7.2 10.1 %copy-start.4 = (s32[2,8,1]{1,2,0:T(1,128)S(1)}, s32[2,8,1]{1,2,0:T(1,128)}, u32[]{:S(2)}) copy-start(s32[2,8,1]{1,2,0:T(1,128)} %param.12) | copy-start | bytes 196
  7.2 10.2 %copy-start.5 = (s32[128]{0:T(128)S(1)}, s32[128]{0:T(128)}, u32[]{:S(2)}) copy-start(s32[128]{0:T(128)} %param.13) | copy-start | bytes 1540
  7.2 10.8 %copy-start.1 = (bf16[256,8,1,128]{3,1,2,0:T(8,128)(2,1)S(1)}, bf16[256,8,1,128]{3,1,2,0:T(8,128)(2,1)}, u32[]{:S(2)}) copy-start(bf16[256,8,1,128]{3,1,2,0:T(8,128)(2,1)} %param.8) | copy-start | bytes 1572868
  7.2 10.9 %copy-start.2 = (bf16[256,8,1,128]{3,1,2,0:T(8,128)(2,1)S(1)}, bf16[256,8,1,128]{3,1,2,0:T(8,128)(2,1)}, u32[]{:S(2)}) copy-start(bf16[256,8,1,128]{3,1,2,0:T(8,128)(2,1)} %param.11) | copy-start | bytes 1572868
  7.2 142.7 %reduce-scatter.3.cloned.1.call-start = ((), (), s32[]{:S(2)}) async-start(), calls=%async_computation.2 | async-start | bytes 1179648 | tf_op jit(solution)/shard_map/reduce_scatter | solution.py:101
  8.4 24.4 %collective-permute-start.1 = (bf16[256,8,128]{2,0,1:T(8,128)(2,1)S(1)}, bf16[256,8,128]{2,0,1:T(8,128)(2,1)}, u32[]{:S(2)}, u32[]{:S(2)}) collective-permute-start(bf16[256,8,128]{2,0,1:T(8,128)(2,1)S(1)} %copy.28), channel_id=1, source_target_pairs={{0,8},{8,16},{16,24},{24,32},{32,40},{40,48},{48,56},{56,64},{64,7... | collective-permute-start | bytes 1572872 | tf_op jit(solution)/shard_map/ppermute | solution.py:10
  13.4 29.9 %collective-permute-start = (bf16[256,8,128]{2,0,1:T(8,128)(2,1)S(1)}, bf16[256,8,128]{2,0,1:T(8,128)(2,1)}, u32[]{:S(2)}, u32[]{:S(2)}) collective-permute-start(bf16[256,8,128]{2,0,1:T(8,128)(2,1)S(1)} %copy.25), channel_id=1, source_target_pairs={{0,8},{8,16},{16,24},{24,32},{32,40},{40,48},{48,56},{56,64},{64,7... | collective-permute-start | bytes 1572872 | tf_op jit(solution)/shard_map/ppermute | solution.py:10
  95.6 17.5 %copy-start = (f32[8,512,128]{2,1,0:T(8,128)S(1)}, f32[8,512,128]{2,1,0:T(8,128)}, u32[]{:S(2)}) copy-start(f32[8,512,128]{2,1,0:T(8,128)} %get-tuple-element.54) | copy-start | bytes 6291460
  95.6 15.2 %collective-permute-start.2 = (bf16[8,256,128]{2,1,0:T(8,128)(2,1)S(1)}, bf16[8,256,128]{2,1,0:T(8,128)(2,1)S(1)}, u32[]{:S(2)}, u32[]{:S(2)}) collective-permute-start(bf16[8,256,128]{2,1,0:T(8,128)(2,1)S(1)} %slice.25), channel_id=1, source_target_pairs={{8,0},{16,8},{24,16},{32,24},{40,32},{48,40},{56,48},{64,56},{72,6... | collective-permute-start | bytes 1572872 | tf_op jit(solution)/shard_map/ppermute | solution.py:10
  113.1 78.0 %reduce-scatter.5.cloned.1.call-start = ((), (), s32[]{:S(2)}) async-start(), calls=%async_computation.3 | async-start | bytes 1179648 | tf_op jit(solution)/shard_map/reduce_scatter | solution.py:102
  113.3 16.0 %copy-start.3 = (bf16[8,256,1,128]{1,3,2,0:T(8,128)(2,1)S(1)}, bf16[8,256,1,128]{1,3,2,0:T(8,128)(2,1)}, u32[]{:S(2)}) copy-start(bf16[8,256,1,128]{1,3,2,0:T(8,128)(2,1)} %get-tuple-element.52) | copy-start | bytes 1572868
  113.3 14.9 %collective-permute-start.3 = (bf16[8,256,128]{2,1,0:T(8,128)(2,1)S(1)}, bf16[8,256,128]{2,1,0:T(8,128)(2,1)S(1)}, u32[]{:S(2)}, u32[]{:S(2)}) collective-permute-start(bf16[8,256,128]{2,1,0:T(8,128)(2,1)S(1)} %slice.24), channel_id=1, source_target_pairs={{8,0},{16,8},{24,16},{32,24},{40,32},{48,40},{56,48},{64,56},{72,6... | collective-permute-start | bytes 1572872 | tf_op jit(solution)/shard_map/ppermute | solution.py:10
Sparse Core Ops, SparseCore 0:
  113.2 36.6 reduce-scatter.2
  152.7 38.3 reduce-scatter.4
where the time goes:
time: 201 us; the launch traced here: 200 us
  waiting for transfers between devices  103 us (51%)
  matrix products  48.8 us (24%)
  starting transfers between devices  17 us (8%)
  between operations  14.3 us (7%)
  other arithmetic  11.3 us (6%)
  local copies, waits for them, and re-layouts  5.38 us (3%)
    ppermute x4, waiting for transfers between devices, passed_along(): return lax.ppermute(block, axis, route)  43.4 us
    reduce_scatter x1, waiting for transfers between devices, per_device(): lax.psum_scatter(value_total, 'tp', scatter_dimension=0, tiled=True)  39.7 us
    reduce_scatter x1, waiting for transfers between devices, per_device(): lax.psum_scatter(key_total, 'tp', scatter_dimension=0, tiled=True)  19.5 us
    ppermute x4, starting transfers between devices, passed_along(): return lax.ppermute(block, axis, route)  17 us
    dot_general x8, matrix products, full_group(): jnp.einsum('rqk,qrd->kd', attn_low, dout_grp, preferred_element_type=jnp....  14.3 us
    dot_general x8, matrix products, group_grads(): jnp.einsum('rqk,kd->qrd', attn_low, value_window, preferred_element_type=...  8.89 us
    dot_general x8, matrix products, group_grads(): jnp.einsum('qrd,kd->rqk', dout_grp, value_window, preferred_element_type=...  8.56 us
    dot_general x8, matrix products, full_group(): jnp.einsum('rqk,qrd->kd', grad_low, query_grp, preferred_element_type=jnp...  7.49 us
  transfers between devices with their start and end apart: 6, of which 6 were waited for; matrix products, arithmetic and copies ran while one was open for 4% of the time, Pallas kernels for 0%

commit v1 on v0

v1 whole, which is shorter than its diff:
```python
import functools
import math

import jax
import jax.numpy as jnp
from jax import lax
from jax.experimental import pallas as pl
from jax.experimental.pallas import tpu as pltpu
from jax.sharding import PartitionSpec as P

BF16 = jnp.bfloat16
F32 = jnp.float32
MASKED = -1e30
VMEM = pl.BlockSpec(memory_space=pltpu.VMEM)
SMEM = pl.BlockSpec(memory_space=pltpu.SMEM)


def params():
    return pltpu.CompilerParams(vmem_limit_bytes=40 * 1024 * 1024)


def dot_nt(a, b):
    return lax.dot_general(a, b, (((1,), (1,)), ((), ())), preferred_element_type=F32)


def dot_nn(a, b):
    return lax.dot_general(a, b, (((1,), (0,)), ((), ())), preferred_element_type=F32)


def shifted(block, axis, distance):
    size = lax.axis_size(axis)
    route = [(i - distance, i) for i in range(size) if 0 <= i - distance < size]
    return lax.ppermute(block, axis, route)


def fill_bias(bias, lengths_ref, first_row):
    keys, rows = bias.shape
    docs = lengths_ref.shape[1]
    lengths = lengths_ref[...]
    i = lax.broadcasted_iota(jnp.int32, (docs, docs), 0)
    j = lax.broadcasted_iota(jnp.int32, (docs, docs), 1)
    ends = jnp.sum(jnp.where(j <= i, lengths, 0), axis=1, keepdims=True) - first_row
    t = lax.broadcasted_iota(jnp.int32, (docs, rows), 1)
    start = jnp.max(jnp.where(ends <= t, ends, -first_row), axis=0, keepdims=True)
    u = lax.broadcasted_iota(jnp.int32, (keys, rows), 0) - (keys - rows)
    t = lax.broadcasted_iota(jnp.int32, (keys, rows), 1)
    bias[...] = jnp.where((u <= t) & (u >= start), 0.0, MASKED).astype(F32)


def pair_terms(query, dout, key, value, bias, scaling):
    scores = dot_nt(key, query) * (scaling * math.log2(math.e)) + bias
    shifted_exp = jnp.exp2(scores - jnp.max(scores, axis=0, keepdims=True))
    probs = shifted_exp * (1.0 / jnp.sum(shifted_exp, axis=0, keepdims=True))
    grad_probs = dot_nt(value, dout)
    row_delta = jnp.sum(probs * grad_probs, axis=0, keepdims=True)
    return probs.astype(BF16), (probs * (grad_probs - row_delta)).astype(BF16)


def prepare_kernel(query_ref, grad_ref, key_ref, value_ref, exp_ref, qd_ref, kv_ref):
    blocks, groups = exp_ref.shape
    rows = grad_ref.shape[0] // blocks
    kv_ref[0] = jnp.swapaxes(key_ref[...], 0, 1)
    kv_ref[1] = jnp.swapaxes(value_ref[...], 0, 1)
    qd_ref[:, 0] = jnp.swapaxes(query_ref[...], 0, 1)
    factor = jnp.exp2(exp_ref[...].astype(F32)).astype(BF16)
    for b in range(blocks):
        part = pl.ds(b * rows, rows)
        qd_ref[:, 1, part] = jnp.swapaxes(grad_ref[part], 0, 1) * factor[b][:, None, None]


def key_side_kernel(scaling, where_ref, lengths_ref, qd_ref, back_ref, here_ref, cross_ref, own_ref, bias, key, value, dkey, dvalue):
    rows = here_ref.shape[2]
    fill_bias(bias, lengths_ref, where_ref[0])
    key[:rows] = back_ref[0, 0]
    key[rows:] = here_ref[0, 0]
    value[:rows] = back_ref[1, 0]
    value[rows:] = here_ref[1, 0]
    for h in range(qd_ref.shape[0]):
        query, dout = qd_ref[h, 0], qd_ref[h, 1]
        probs, grad_scores = pair_terms(query, dout, key[...], value[...], bias[...], scaling)
        if h == 0:
            dvalue[...] = dot_nn(probs, dout)
            dkey[...] = dot_nn(grad_scores, query)
        else:
            dvalue[...] += dot_nn(probs, dout)
            dkey[...] += dot_nn(grad_scores, query)
    cross_ref[0] = (dkey[:rows] * scaling).astype(BF16)
    cross_ref[1] = dvalue[:rows].astype(BF16)
    own_ref[0] = dkey[rows:] * scaling
    own_ref[1] = dvalue[rows:]


def query_side_kernel(scaling, where_ref, lengths_ref, qd_ref, back_ref, here_ref, out_ref, bias, grads):
    fill_bias(bias, lengths_ref, where_ref[0])
    for g in range(qd_ref.shape[0]):
        key = jnp.concatenate([back_ref[0, g], here_ref[0, g]], axis=0)
        value = jnp.concatenate([back_ref[1, g], here_ref[1, g]], axis=0)
        _, grad_scores = pair_terms(qd_ref[g, 0], qd_ref[g, 1], key, value, bias[...], scaling)
        grads[g] = (dot_nn(key.T, grad_scores) * scaling).astype(BF16).T
    out_ref[...] = jnp.swapaxes(grads[...], 0, 1)


def finish_kernel(own_ref, back_ref, key_ref, value_ref):
    key_ref[...] = (own_ref[0] + back_ref[0].astype(F32)).astype(BF16)
    value_ref[...] = (own_ref[1] + back_ref[1].astype(F32)).astype(BF16)


def per_device(queries, keys, values, grad_out, exponents, lengths):
    rows, groups, _, width = queries.shape
    scaling = width ** (-0.5)
    shape = jax.ShapeDtypeStruct
    where = jnp.stack([lax.axis_index("seq") * rows, lax.axis_index("tp")]).astype(jnp.int32)
    lengths = lengths.reshape(1, -1)
    qd, kv = pl.pallas_call(
        prepare_kernel,
        in_specs=[VMEM] * 5,
        out_specs=[VMEM] * 2,
        out_shape=[shape((groups, 2, rows, width), BF16), shape((2, groups, rows, width), BF16)],
        compiler_params=params(),
    )(
        queries.reshape(rows, groups, width),
        grad_out.reshape(rows, groups, width),
        keys,
        values,
        exponents.reshape(-1, groups),
    )
    kv_back = shifted(kv, "seq", 1)
    qd_group = lax.all_to_all(qd, "tp", split_axis=0, concat_axis=0, tiled=True)
    whole = lambda i, where: (0, 0)
    one_group = pl.BlockSpec((2, 1, rows, width), lambda i, where: (0, where[1], 0, 0))
    pairs = qd.shape[0]
    flops = 2 * 2 * rows * rows * width * pairs
    cross, own = pl.pallas_call(
        functools.partial(key_side_kernel, scaling),
        grid_spec=pltpu.PrefetchScalarGridSpec(
            num_scalar_prefetch=1,
            grid=(1,),
            in_specs=[
                pl.BlockSpec(lengths.shape, whole),
                pl.BlockSpec(qd_group.shape, lambda i, where: (0, 0, 0, 0)),
                one_group,
                one_group,
            ],
            out_specs=[pl.BlockSpec((2, rows, width), lambda i, where: (0, 0, 0))] * 2,
            scratch_shapes=[
                pltpu.VMEM((2 * rows, rows), F32),
                pltpu.VMEM((2 * rows, width), BF16),
                pltpu.VMEM((2 * rows, width), BF16),
                pltpu.VMEM((2 * rows, width), F32),
                pltpu.VMEM((2 * rows, width), F32),
            ],
        ),
        out_shape=[shape((2, rows, width), BF16), shape((2, rows, width), F32)],
        compiler_params=params(),
        cost_estimate=pl.CostEstimate(flops=4 * flops, bytes_accessed=2**21, transcendentals=2 * rows * rows * pairs),
    )(where, lengths, qd_group, kv_back, kv)
    back = shifted(cross, "seq", -1)
    grad_queries = pl.pallas_call(
        functools.partial(query_side_kernel, scaling),
        in_specs=[SMEM] + [VMEM] * 4,
        out_specs=VMEM,
        out_shape=shape((rows, groups, width), BF16),
        scratch_shapes=[pltpu.VMEM((2 * rows, rows), F32), pltpu.VMEM((groups, rows, width), BF16)],
        compiler_params=params(),
        cost_estimate=pl.CostEstimate(flops=3 * flops, bytes_accessed=2**22, transcendentals=2 * rows * rows * pairs),
    )(where, lengths, qd, kv_back, kv)
    grad_keys, grad_values = pl.pallas_call(
        finish_kernel,
        in_specs=[VMEM] * 2,
        out_specs=[VMEM] * 2,
        out_shape=[shape((rows, width), BF16)] * 2,
        compiler_params=params(),
    )(own, back)
    return (
        grad_queries.reshape(queries.shape),
        grad_keys.reshape(rows, 1, width),
        grad_values.reshape(rows, 1, width),
    )


def solution(mesh):
    placed = (
        P("seq", None, "tp", None),
        P("seq", None, None),
        P("seq", None, None),
        P("seq", None, "tp", None),
        P("seq", None, "tp"),
        P(),
    )
    return jax.shard_map(
        per_device,
        mesh=mesh,
        in_specs=placed,
        out_specs=(P("seq", None, "tp", None), P("seq", "tp", None), P("seq", "tp", None)),
        check_vma=False,
    )
```

time: 201 us -> 57.5 us (0.29)
  waiting for transfers between devices: 103 us -> 26.5 us
  matrix products: 48.8 us -> 0 us
  between operations: 14.3 us -> 0.67 us
  Pallas kernels: 0 us -> 13.2 us
  other arithmetic: 11.3 us -> 0.07 us
  starting transfers between devices: 17 us -> 11.8 us
    reduce_scatter x2 -> x0, waiting for transfers between devices: 59.2 us -> none  [the longest x1 39.7 us: per_device(): lax.psum_scatter(value_total, 'tp', scatter_dimension=0, tiled=True)]
    dot_general x48 -> x0, matrix products: 48.8 us -> none  [the longest x8 14.3 us: full_group(): jnp.einsum('rqk,qrd->kd', attn_low, dout_grp, preferred_element_type=jnp....]
    ppermute x4 -> x2, waiting for transfers between devices: 43.4 us -> 10.6 us  [shifted(): return lax.ppermute(block, axis, route)]
    all_to_all x0 -> x1, waiting for transfers between devices: none -> 15.9 us  [per_device(): qd_group = lax.all_to_all(qd, 'tp', split_axis=0, concat_axis=0, tiled=True)]
    pallas_call x0 -> x4, Pallas kernels: none -> 13.2 us  [the longest x1 5.8 us: per_device(): pl.pallas_call(functools.partial(query_side_kernel, scaling), in_specs=[S...]
    ppermute x4 -> x2, starting transfers between devices: 17 us -> 7.45 us  [shifted(): return lax.ppermute(block, axis, route)]
    all_to_all x0 -> x1, starting transfers between devices: none -> 4.31 us  [per_device(): qd_group = lax.all_to_all(qd, 'tp', split_axis=0, concat_axis=0, tiled=True)]
    add x4 -> x0, other arithmetic: 3.38 us -> none  [the longest x1 2.29 us: core_grads(): key_total = key_terms[:, row_count:] + back_keys]
  transfers between devices with their start and end apart: 6 -> 3, of which waited for: 6 -> 2; matrix products, arithmetic and copies ran while one was open for 4% -> 0% of each run, Pallas kernels for 0% -> 10%
where the time goes in v1:
time: 57.5 us; the launch traced here: 57.1 us
  waiting for transfers between devices  26.5 us (46%)
  Pallas kernels  13.2 us (23%)
  starting transfers between devices  11.8 us (21%)
  local copies, waits for them, and re-layouts  4.84 us (8%)
  between operations  0.67 us (1%)
    all_to_all x1, waiting for transfers between devices, per_device(): qd_group = lax.all_to_all(qd, 'tp', split_axis=0, concat_axis=0, tiled=True)  15.9 us
    ppermute x2, waiting for transfers between devices, shifted(): return lax.ppermute(block, axis, route)  10.6 us
    ppermute x2, starting transfers between devices, shifted(): return lax.ppermute(block, axis, route)  7.45 us
    pallas_call x1, Pallas kernels, per_device(): pl.pallas_call(functools.partial(query_side_kernel, scaling), in_specs=[S...  5.8 us
    pallas_call x1, Pallas kernels, per_device(): pl.pallas_call(functools.partial(key_side_kernel, scaling), grid_spec=plt...  5.26 us
    unnamed x12, local copies, waits for them, and re-layouts  4.84 us
    all_to_all x1, starting transfers between devices, per_device(): qd_group = lax.all_to_all(qd, 'tp', split_axis=0, concat_axis=0, tiled=True)  4.31 us
    pallas_call x1, Pallas kernels, per_device(): pl.pallas_call(prepare_kernel, in_specs=[VMEM] * 5, out_specs=[VMEM] * 2,...  1.51 us
  transfers between devices with their start and end apart: 3, of which 2 were waited for; matrix products, arithmetic and copies ran while one was open for 0% of the time, Pallas kernels for 10%

profile of v1, /device:TPU:24, one launch (start us, length us, event | category | flops | bytes accessed | tf_op | source)
XLA Modules:
  0.0 57.1 jit_solution(17689438486154296346)
XLA Ops:
  0.6 0.0 copy-start.4
  0.6 0.7 %copy-done.4 = s32[2,8,1]{1,2,0:T(1,128)S(1)} copy-done((s32[2,8,1]{1,2,0:T(1,128)S(1)}, s32[2,8,1]{1,2,0:T(1,128)}, u32[]{:S(2)}) %copy-start.4) | copy-done | bytes 88
  1.3 0.0 copy-start
  1.3 1.0 %copy-done = bf16[256,8,1,128]{3,1,2,0:T(8,128)(2,1)S(1)} copy-done((bf16[256,8,1,128]{3,1,2,0:T(8,128)(2,1)S(1)}, bf16[256,8,1,128]{3,1,2,0:T(8,128)(2,1)}, u32[]{:S(2)}) %copy-start) | copy-done | bytes 524312
  2.4 0.0 copy-start.1
  2.4 1.0 %copy-done.1 = bf16[256,8,1,128]{3,1,2,0:T(8,128)(2,1)S(1)} copy-done((bf16[256,8,1,128]{3,1,2,0:T(8,128)(2,1)S(1)}, bf16[256,8,1,128]{3,1,2,0:T(8,128)(2,1)}, u32[]{:S(2)}) %copy-start.1) | copy-done | bytes 524312
  3.4 0.0 copy-start.2
  3.4 1.0 %copy-done.2 = bf16[256,8,128]{2,1,0:T(8,128)(2,1)S(1)} copy-done((bf16[256,8,128]{2,1,0:T(8,128)(2,1)S(1)}, bf16[256,8,128]{2,1,0:T(8,128)(2,1)}, u32[]{:S(2)}) %copy-start.2) | copy-done | bytes 524312
  4.4 0.0 copy-start.3
  4.4 1.0 %copy-done.3 = bf16[256,8,128]{2,1,0:T(8,128)(2,1)S(1)} copy-done((bf16[256,8,128]{2,1,0:T(8,128)(2,1)S(1)}, bf16[256,8,128]{2,1,0:T(8,128)(2,1)}, u32[]{:S(2)}) %copy-start.3) | copy-done | bytes 524312
  5.5 1.5 %shard_map.85 = (bf16[8,2,256,128]{3,2,1,0:T(8,128)(2,1)}, bf16[2,8,256,128]{3,2,1,0:T(8,128)(2,1)S(1)}) custom-call(bf16[256,8,128]{2,1,0:T(8,128)(2,1)S(1)} %bitcast.11, bf16[256,8,128]{2,1,0:T(8,128)(2,1)S(1)} %bitcast.12, bf16[256,8,128]{2,1,0:T(8,128)(2,1)S(1)} %copy-done.2, bf16[256,8,128]{2,1,0:T(8,128)(2,1)S(1)} %copy-done.3, s32[2,8]{1,0:T(2,128)S(1)} %bitcast.13), custom_call_target="tpu_custom_call" | custom-call | tf_op jit(solution)/shard_map/pallas_call | solution.py:114
  7.0 3.8 %collective-permute-start = (bf16[2,8,256,128]{3,2,1,0:T(8,128)(2,1)S(1)}, bf16[2,8,256,128]{3,2,1,0:T(8,128)(2,1)S(1)}, u32[]{:S(2)}, u32[]{:S(2)}) collective-permute-start(bf16[2,8,256,128]{3,2,1,0:T(8,128)(2,1)S(1)} %get-tuple-element.10.here_ref), channel_id=1, source_target_pairs={{0,8},{8,16},{16,24},{24,32},{32,40},{40,48},{48,56},{56,64},{64,7... | collective-permute-start | bytes 3145736 | tf_op jit(solution)/shard_map/ppermute | solution.py:33
  10.8 4.3 %all-to-all-start = ((bf16[8,2,256,128]{3,2,1,0:T(8,128)(2,1)}), bf16[8,2,256,128]{3,2,1,0:T(8,128)(2,1)S(1)}, u32[]{:S(2)}, u32[]{:S(2)}) async-start(bf16[8,2,256,128]{3,2,1,0:T(8,128)(2,1)} %get-tuple-element.9.qd_ref), calls=%async_computation | async-start | bytes 2097152 | tf_op jit(solution)/shard_map/all_to_all | solution.py:128
  15.1 0.1 pad_add_fusion.where_ref
  15.2 0.0 copy-start.5
  15.2 15.9 %all-to-all-done.qd_ref = bf16[8,2,256,128]{3,2,1,0:T(8,128)(2,1)S(1)} async-done(((bf16[8,2,256,128]{3,2,1,0:T(8,128)(2,1)}), bf16[8,2,256,128]{3,2,1,0:T(8,128)(2,1)S(1)}, u32[]{:S(2)}, u32[]{:S(2)}) %all-to-all-start) | async-done | bytes 1048608 | tf_op jit(solution)/shard_map/all_to_all | solution.py:128
  31.1 10.6 %collective-permute-done.back_ref = bf16[2,8,256,128]{3,2,1,0:T(8,128)(2,1)S(1)} collective-permute-done((bf16[2,8,256,128]{3,2,1,0:T(8,128)(2,1)S(1)}, bf16[2,8,256,128]{3,2,1,0:T(8,128)(2,1)S(1)}, u32[]{:S(2)}, u32[]{:S(2)}) %collective-permute-start) | collective-permute-done | bytes 1048608 | tf_op jit(solution)/shard_map/ppermute | solution.py:33
  41.7 0.0 copy-done.5
  41.7 5.3 %shard_map.87 = (bf16[2,256,128]{2,1,0:T(8,128)(2,1)S(1)}, f32[2,256,128]{2,1,0:T(8,128)S(1)}) custom-call(s32[2]{0:T(128)S(1)} %pad_add_fusion.where_ref, s32[1,128]{1,0:T(1,128)S(1)} %bitcast.14, bf16[8,2,256,128]{3,2,1,0:T(8,128)(2,1)S(1)} %all-to-all-done.qd_ref, bf16[2,8,256,128]{3,2,1,0:T(8,128)(2,1)S(1)} %collective-permute-done.back_ref, ...), custom_call_target="tpu_custom_call" | custom-call | flops 1073741824 | bytes 2097152 | tf_op jit(solution)/shard_map/pallas_call | solution.py:133
  47.0 3.6 %collective-permute-start.1 = (bf16[2,256,128]{2,1,0:T(8,128)(2,1)S(1)}, bf16[2,256,128]{2,1,0:T(8,128)(2,1)S(1)}, u32[]{:S(2)}, u32[]{:S(2)}) collective-permute-start(bf16[2,256,128]{2,1,0:T(8,128)(2,1)S(1)} %get-tuple-element.12), channel_id=1, source_target_pairs={{8,0},{16,8},{24,16},{32,24},{40,32},{48,40},{56,48},{64,56},{72,6... | collective-permute-start | bytes 393224 | tf_op jit(solution)/shard_map/ppermute | solution.py:33
  50.6 5.8 %shard_map.86 = bf16[256,8,128]{2,1,0:T(8,128)(2,1)} custom-call(s32[2]{0:T(128)S(1)} %pad_add_fusion.where_ref, s32[1,128]{1,0:T(1,128)S(1)} %bitcast.15, bf16[8,2,256,128]{3,2,1,0:T(8,128)(2,1)} %get-tuple-element.9.qd_ref, bf16[2,8,256,128]{3,2,1,0:T(8,128)(2,1)S(1)} %collective-permute-done.back_ref, bf16[2,8,256,128]{3,2,1,0:T(8,128)(2,1)S(1)} %get-tuple-element.10.here_ref), custom_call_target="tpu_custom_call" | custom-call | flops 805306368 | bytes 4194304 | tf_op jit(solution)/shard_map/pallas_call | solution.py:158
  56.4 0.0 collective-permute-done.1.back_ref
  56.4 0.7 %shard_map.88 = (bf16[256,128]{1,0:T(8,128)(2,1)}, bf16[256,128]{1,0:T(8,128)(2,1)}) custom-call(f32[2,256,128]{2,1,0:T(8,128)S(1)} %get-tuple-element.11.own_ref, bf16[2,256,128]{2,1,0:T(8,128)(2,1)S(1)} %collective-permute-done.1.back_ref), custom_call_target="tpu_custom_call" | custom-call | tf_op jit(solution)/shard_map/pallas_call | solution.py:167
Async XLA Ops:
  0.6 0.7 %copy-start.4 = (s32[2,8,1]{1,2,0:T(1,128)S(1)}, s32[2,8,1]{1,2,0:T(1,128)}, u32[]{:S(2)}) copy-start(s32[2,8,1]{1,2,0:T(1,128)} %param.10) | copy-start | bytes 196
  1.3 1.0 %copy-start = (bf16[256,8,1,128]{3,1,2,0:T(8,128)(2,1)S(1)}, bf16[256,8,1,128]{3,1,2,0:T(8,128)(2,1)}, u32[]{:S(2)}) copy-start(bf16[256,8,1,128]{3,1,2,0:T(8,128)(2,1)} %param.6) | copy-start | bytes 1572868
  2.4 1.0 %copy-start.1 = (bf16[256,8,1,128]{3,1,2,0:T(8,128)(2,1)S(1)}, bf16[256,8,1,128]{3,1,2,0:T(8,128)(2,1)}, u32[]{:S(2)}) copy-start(bf16[256,8,1,128]{3,1,2,0:T(8,128)(2,1)} %param.9) | copy-start | bytes 1572868
  3.4 1.0 %copy-start.2 = (bf16[256,8,128]{2,1,0:T(8,128)(2,1)S(1)}, bf16[256,8,128]{2,1,0:T(8,128)(2,1)}, u32[]{:S(2)}) copy-start(bf16[256,8,128]{2,1,0:T(8,128)(2,1)} %key_ref.1) | copy-start | bytes 1572868
  4.4 1.0 %copy-start.3 = (bf16[256,8,128]{2,1,0:T(8,128)(2,1)S(1)}, bf16[256,8,128]{2,1,0:T(8,128)(2,1)}, u32[]{:S(2)}) copy-start(bf16[256,8,128]{2,1,0:T(8,128)(2,1)} %value_ref.1) | copy-start | bytes 1572868
  7.0 34.7 %collective-permute-start = (bf16[2,8,256,128]{3,2,1,0:T(8,128)(2,1)S(1)}, bf16[2,8,256,128]{3,2,1,0:T(8,128)(2,1)S(1)}, u32[]{:S(2)}, u32[]{:S(2)}) collective-permute-start(bf16[2,8,256,128]{3,2,1,0:T(8,128)(2,1)S(1)} %get-tuple-element.10.here_ref), channel_id=1, source_target_pairs={{0,8},{8,16},{16,24},{24,32},{32,40},{40,48},{48,56},{56,64},{64,7... | collective-permute-start | bytes 3145736 | tf_op jit(solution)/shard_map/ppermute | solution.py:33
  10.8 20.3 %all-to-all-start = ((bf16[8,2,256,128]{3,2,1,0:T(8,128)(2,1)}), bf16[8,2,256,128]{3,2,1,0:T(8,128)(2,1)S(1)}, u32[]{:S(2)}, u32[]{:S(2)}) async-start(bf16[8,2,256,128]{3,2,1,0:T(8,128)(2,1)} %get-tuple-element.9.qd_ref), calls=%async_computation | async-start | bytes 2097152 | tf_op jit(solution)/shard_map/all_to_all | solution.py:128
  15.2 26.5 %copy-start.5 = (s32[128]{0:T(128)S(1)}, s32[128]{0:T(128)}, u32[]{:S(2)}) copy-start(s32[128]{0:T(128)} %param.11) | copy-start | bytes 1540
  47.0 9.4 %collective-permute-start.1 = (bf16[2,256,128]{2,1,0:T(8,128)(2,1)S(1)}, bf16[2,256,128]{2,1,0:T(8,128)(2,1)S(1)}, u32[]{:S(2)}, u32[]{:S(2)}) collective-permute-start(bf16[2,256,128]{2,1,0:T(8,128)(2,1)S(1)} %get-tuple-element.12), channel_id=1, source_target_pairs={{8,0},{16,8},{24,16},{32,24},{40,32},{48,40},{56,48},{64,56},{72,6... | collective-permute-start | bytes 393224 | tf_op jit(solution)/shard_map/ppermute | solution.py:33

commit v2 on v1

v2 whole, which is shorter than its diff:
```python
import functools
import math

import jax
import jax.numpy as jnp
from jax import lax
from jax.experimental import pallas as pl
from jax.experimental.pallas import tpu as pltpu
from jax.sharding import PartitionSpec as P

BF16 = jnp.bfloat16
F32 = jnp.float32
MASKED = -1e30
VMEM = pl.BlockSpec(memory_space=pltpu.VMEM)
SMEM = pl.BlockSpec(memory_space=pltpu.SMEM)


def params():
    return pltpu.CompilerParams(vmem_limit_bytes=40 * 1024 * 1024)


def dot_nt(a, b):
    return lax.dot_general(a, b, (((1,), (1,)), ((), ())), preferred_element_type=F32)


def dot_nn(a, b):
    return lax.dot_general(a, b, (((1,), (0,)), ((), ())), preferred_element_type=F32)


def shifted(block, axis, distance):
    size = lax.axis_size(axis)
    route = [(i - distance, i) for i in range(size) if 0 <= i - distance < size]
    return lax.ppermute(block, axis, route)


def fill_bias(bias, lengths_ref, first_row):
    keys, rows = bias.shape
    half = rows // 2
    docs = lengths_ref.shape[1]
    lengths = lengths_ref[...]
    i = lax.broadcasted_iota(jnp.int32, (docs, docs), 0)
    j = lax.broadcasted_iota(jnp.int32, (docs, docs), 1)
    ends = jnp.sum(jnp.where(j <= i, lengths, 0), axis=1, keepdims=True) - first_row
    t = lax.broadcasted_iota(jnp.int32, (docs, rows), 1)
    start = jnp.max(jnp.where(ends <= t, ends, -first_row), axis=0, keepdims=True)
    row = lax.broadcasted_iota(jnp.int32, (keys, rows), 0)
    t = lax.broadcasted_iota(jnp.int32, (keys, rows), 1)
    u = jnp.where((row >= rows) & (t < half), row - 2 * rows, row - half)
    bias[...] = jnp.where((u <= t) & (u >= start), 0.0, MASKED).astype(F32)


def window_dots(keys, queries):
    rows = queries.shape[0]
    half = rows // 2
    middle = dot_nt(keys[half : half + rows], queries)
    corners = jnp.concatenate(
        [dot_nt(keys[:half], queries[:half]), dot_nt(keys[half + rows :], queries[half:])], axis=1
    )
    return middle, corners


def pair_terms(query, dout, key, value, bias, scaling):
    rows = query.shape[0]
    fold = scaling * math.log2(math.e)
    middle, corners = window_dots(key, query)
    middle = middle * fold + bias[:rows]
    corners = corners * fold + bias[rows:]
    row_max = jnp.maximum(jnp.max(middle, axis=0, keepdims=True), jnp.max(corners, axis=0, keepdims=True))
    middle = jnp.exp2(middle - row_max)
    corners = jnp.exp2(corners - row_max)
    inverse = 1.0 / (jnp.sum(middle, axis=0, keepdims=True) + jnp.sum(corners, axis=0, keepdims=True))
    middle = middle * inverse
    corners = corners * inverse
    grad_middle, grad_corners = window_dots(value, dout)
    row_delta = jnp.sum(middle * grad_middle, axis=0, keepdims=True) + jnp.sum(
        corners * grad_corners, axis=0, keepdims=True
    )
    return (
        middle.astype(BF16),
        corners.astype(BF16),
        (middle * (grad_middle - row_delta)).astype(BF16),
        (corners * (grad_corners - row_delta)).astype(BF16),
    )


def query_prepare_kernel(query_ref, grad_ref, exp_ref, qd_ref):
    blocks, groups = exp_ref.shape
    rows = grad_ref.shape[0] // blocks
    qd_ref[:, 0] = jnp.swapaxes(query_ref[...], 0, 1)
    factor = jnp.exp2(exp_ref[...].astype(F32)).astype(BF16)
    for b in range(blocks):
        part = pl.ds(b * rows, rows)
        qd_ref[:, 1, part] = jnp.swapaxes(grad_ref[part], 0, 1) * factor[b][:, None, None]


def key_prepare_kernel(key_ref, value_ref, kv_ref):
    kv_ref[0] = jnp.swapaxes(key_ref[...], 0, 1)
    kv_ref[1] = jnp.swapaxes(value_ref[...], 0, 1)


def window_prepare_kernel(where_ref, here_ref, other_ref, kv_ref):
    core = where_ref[1] % 2
    kv_ref[core] = jnp.swapaxes(here_ref[...], 0, 1)
    kv_ref[1 - core] = jnp.swapaxes(other_ref[...], 0, 1)


def query_side_kernel(scaling, where_ref, lengths_ref, qd_ref, back_ref, here_ref, out_ref, bias, grads):
    fill_bias(bias, lengths_ref, where_ref[0])
    rows = qd_ref.shape[2]
    half = rows // 2
    for g in range(qd_ref.shape[0]):
        key = jnp.concatenate([back_ref[0, g], here_ref[0, g]], axis=0)
        value = jnp.concatenate([back_ref[1, g], here_ref[1, g]], axis=0)
        _, _, middle, corners = pair_terms(qd_ref[g, 0], qd_ref[g, 1], key, value, bias[...], scaling)
        key_t = key.T
        total = dot_nn(key_t[:, half : half + rows], middle) + jnp.concatenate(
            [dot_nn(key_t[:, :half], corners[:, :half]), dot_nn(key_t[:, half + rows :], corners[:, half:])],
            axis=1,
        )
        grads[g] = (total * scaling).astype(BF16).T
    out_ref[...] = jnp.swapaxes(grads[...], 0, 1)


def key_side_kernel(scaling, where_ref, lengths_ref, qd_ref, back_ref, here_ref, cross_ref, own_ref, bias, mid_terms, left_terms, right_terms):
    heads, _, rows, width = qd_ref.shape
    half = rows // 2
    fill_bias(bias, lengths_ref, where_ref[0])
    key = jnp.concatenate([back_ref[0, 0], here_ref[0, 0]], axis=0)
    value = jnp.concatenate([back_ref[1, 0], here_ref[1, 0]], axis=0)
    for h in range(heads):
        probs, probs_c, grads, grads_c = pair_terms(qd_ref[h, 0], qd_ref[h, 1], key, value, bias[...], scaling)
        at, at_half = pl.ds(h * rows, rows), pl.ds(h * half, half)
        mid_terms[0, :, at] = grads
        mid_terms[1, :, at] = probs
        left_terms[0, :, at_half] = grads_c[:, :half]
        left_terms[1, :, at_half] = probs_c[:, :half]
        right_terms[0, :, at_half] = grads_c[:, half:]
        right_terms[1, :, at_half] = probs_c[:, half:]
    for i, factor in ((0, scaling), (1, 1.0)):
        both = qd_ref[:, i].reshape(heads * rows, width)
        early = qd_ref[:, i, :half].reshape(heads * half, width)
        late = qd_ref[:, i, half:].reshape(heads * half, width)
        middle = dot_nn(mid_terms[i], both) * factor
        cross_ref[i, :half] = (dot_nn(left_terms[i], early) * factor).astype(BF16)
        cross_ref[i, half:] = middle[:half].astype(BF16)
        own_ref[i, :half] = middle[half:]
        own_ref[i, half:] = dot_nn(right_terms[i], late) * factor


def finish_kernel(own_ref, back_ref, key_ref, value_ref):
    key_ref[...] = (own_ref[0] + back_ref[0].astype(F32)).astype(BF16)
    value_ref[...] = (own_ref[1] + back_ref[1].astype(F32)).astype(BF16)


def per_device(queries, keys, values, grad_out, exponents, lengths):
    rows, groups, _, width = queries.shape
    scaling = width ** (-0.5)
    shape = jax.ShapeDtypeStruct
    device = lax.axis_index("tp")
    where = jnp.stack([lax.axis_index("seq") * rows, device]).astype(jnp.int32)
    lengths = lengths.reshape(1, -1)
    pairs = 8
    flops = 2 * 2 * rows * rows * width * pairs
    bias = pltpu.VMEM((rows + rows // 2, rows), F32)

    def call(kernel, operands, out_shape, scratch=(), scalars=0, dots=0):
        many = isinstance(out_shape, list)
        return pl.pallas_call(
            kernel,
            in_specs=[SMEM] * scalars + [VMEM] * (len(operands) - scalars),
            out_specs=[VMEM] * len(out_shape) if many else VMEM,
            out_shape=out_shape,
            scratch_shapes=list(scratch),
            compiler_params=params(),
            cost_estimate=pl.CostEstimate(flops=flops * dots + 10**6, bytes_accessed=2**20, transcendentals=0),
            name=(kernel.func if isinstance(kernel, functools.partial) else kernel).__name__,
        )(*operands)

    half_kv = jnp.where(device % 2 == 0, keys, values)
    half_back = shifted(half_kv, "seq", 1)
    queries_3d = queries.reshape(rows, groups, width)
    queries_3d, half_kv = lax.optimization_barrier((queries_3d, half_kv))
    qd = call(
        query_prepare_kernel,
        (queries_3d, grad_out.reshape(rows, groups, width), exponents.reshape(-1, groups)),
        shape((groups, 2, rows, width), BF16),
    )
    qd_group = lax.all_to_all(qd, "tp", split_axis=0, concat_axis=0, tiled=True)
    kv_shape = shape((2, groups, rows, width), BF16)
    kv = call(key_prepare_kernel, (keys, values), kv_shape)
    other_half = lax.ppermute(half_back, "tp", [(d, d ^ 1) for d in range(lax.axis_size("tp"))])
    kv_back = call(window_prepare_kernel, (where, half_back, other_half), kv_shape, scalars=1)
    grad_queries = call(
        functools.partial(query_side_kernel, scaling),
        (where, lengths, qd, kv_back, kv),
        shape((rows, groups, width), BF16),
        [bias, pltpu.VMEM((groups, rows, width), BF16)],
        scalars=1,
        dots=3,
    )
    grad_queries, kv_back = lax.optimization_barrier((grad_queries, kv_back))
    whole = lambda i, where: (0, 0)
    one_group = pl.BlockSpec((2, 1, rows, width), lambda i, where: (0, where[1], 0, 0))
    cross, own = pl.pallas_call(
        functools.partial(key_side_kernel, scaling),
        grid_spec=pltpu.PrefetchScalarGridSpec(
            num_scalar_prefetch=1,
            grid=(1,),
            in_specs=[
                pl.BlockSpec(lengths.shape, whole),
                pl.BlockSpec(qd_group.shape, lambda i, where: (0, 0, 0, 0)),
                one_group,
                one_group,
            ],
            out_specs=[pl.BlockSpec((2, rows, width), lambda i, where: (0, 0, 0))] * 2,
            scratch_shapes=[
                bias,
                pltpu.VMEM((2, rows, pairs * rows), BF16),
                pltpu.VMEM((2, rows // 2, pairs * rows // 2), BF16),
                pltpu.VMEM((2, rows // 2, pairs * rows // 2), BF16),
            ],
        ),
        out_shape=[shape((2, rows, width), BF16), shape((2, rows, width), F32)],
        compiler_params=params(),
        cost_estimate=pl.CostEstimate(flops=4 * flops, bytes_accessed=2**21, transcendentals=0),
        name="key_side_kernel",
    )(where, lengths, qd_group, kv_back, kv)
    back = shifted(cross, "seq", -1)
    grad_keys, grad_values = call(finish_kernel, (own, back), [shape((rows, width), BF16)] * 2)
    return (
        grad_queries.reshape(queries.shape),
        grad_keys.reshape(rows, 1, width),
        grad_values.reshape(rows, 1, width),
    )


def solution(mesh):
    placed = (
        P("seq", None, "tp", None),
        P("seq", None, None),
        P("seq", None, None),
        P("seq", None, "tp", None),
        P("seq", None, "tp"),
        P(),
    )
    return jax.shard_map(
        per_device,
        mesh=mesh,
        in_specs=placed,
        out_specs=(P("seq", None, "tp", None), P("seq", "tp", None), P("seq", "tp", None)),
        check_vma=False,
    )
```

time: 57.5 us -> 49.2 us (0.86)
  waiting for transfers between devices: 26.5 us -> 19.1 us
  local copies, waits for them, and re-layouts: 4.84 us -> 1.32 us
  starting transfers between devices: 11.8 us -> 13.8 us
  other arithmetic: 0.07 us -> 1.27 us
  Pallas kernels: 13.2 us -> 12.6 us
    all_to_all x1, waiting for transfers between devices: 15.9 us -> 0.01 us  [per_device(): qd_group = lax.all_to_all(qd, 'tp', split_axis=0, concat_axis=0, tiled=True)]
    ppermute x2, waiting for transfers between devices: 10.6 us -> 17.1 us  [shifted(): return lax.ppermute(block, axis, route)]
    unnamed x12, local copies, waits for them, and re-layouts: 4.84 us -> 1.32 us
    ppermute x0 -> x1, waiting for transfers between devices: none -> 1.94 us  [per_device(): lax.ppermute(half_back, 'tp', [(d, d ^ 1) for d in range(lax.axis_size('t...]
    ppermute x0 -> x1, starting transfers between devices: none -> 1.91 us  [per_device(): lax.ppermute(half_back, 'tp', [(d, d ^ 1) for d in range(lax.axis_size('t...]
    pallas_call x1, Pallas kernels: 5.26 us -> 3.5 us  [per_device(): pl.pallas_call(functools.partial(key_side_kernel, scaling), grid_spec=plt...]
    select_n x0 -> x1, other arithmetic: none -> 1.19 us  [per_device(): half_kv = jnp.where(device % 2 == 0, keys, values)]
    pallas_call x3 -> x5, Pallas kernels: 7.97 us -> 9.14 us  [call(): pl.pallas_call(kernel, in_specs=[SMEM] * scalars + [VMEM] * (len(operands...]
  transfers between devices with their start and end apart: 3 -> 4, of which waited for: 2 -> 3; matrix products, arithmetic and copies ran while one was open for 0% -> 0% of each run, Pallas kernels for 10% -> 17%
where the time goes in v2:
time: 49.2 us; the launch traced here: 48.9 us
  waiting for transfers between devices  19.1 us (39%)
  starting transfers between devices  13.8 us (28%)
  Pallas kernels  12.6 us (26%)
  local copies, waits for them, and re-layouts  1.32 us (3%)
  other arithmetic  1.27 us (3%)
  between operations  0.77 us (2%)
    ppermute x2, waiting for transfers between devices, shifted(): return lax.ppermute(block, axis, route)  17.1 us
    pallas_call x5, Pallas kernels, call(): pl.pallas_call(kernel, in_specs=[SMEM] * scalars + [VMEM] * (len(operands...  9.14 us
    ppermute x2, starting transfers between devices, shifted(): return lax.ppermute(block, axis, route)  7.48 us
    all_to_all x1, starting transfers between devices, per_device(): qd_group = lax.all_to_all(qd, 'tp', split_axis=0, concat_axis=0, tiled=True)  4.43 us
    pallas_call x1, Pallas kernels, per_device(): pl.pallas_call(functools.partial(key_side_kernel, scaling), grid_spec=plt...  3.5 us
    ppermute x1, waiting for transfers between devices, per_device(): lax.ppermute(half_back, 'tp', [(d, d ^ 1) for d in range(lax.axis_size('t...  1.94 us
    ppermute x1, starting transfers between devices, per_device(): lax.ppermute(half_back, 'tp', [(d, d ^ 1) for d in range(lax.axis_size('t...  1.91 us
    unnamed x12, local copies, waits for them, and re-layouts  1.32 us
  transfers between devices with their start and end apart: 4, of which 3 were waited for; matrix products, arithmetic and copies ran while one was open for 0% of the time, Pallas kernels for 17%

profile of v2, /device:TPU:24, one launch (start us, length us, event | category | flops | bytes accessed | tf_op | source)
XLA Modules:
  0.0 48.9 jit_solution(4231159396290828104)
XLA Ops:
  0.6 0.0 copy-start.2
  0.7 0.0 copy-start.3
  0.7 1.2 %broadcast_select_fusion = bf16[256,8,128]{2,1,0:T(8,128)(2,1)S(1)} fusion(bf16[256,8,128]{2,1,0:T(8,128)(2,1)} %key_ref.1, bf16[256,8,128]{2,1,0:T(8,128)(2,1)} %value_ref.1, pred[]{:T(512)S(6)} %eq.5), kind=kLoop, calls=%fused_computation | loop fusion | flops 262144 | bytes 1572865 | tf_op jit(solution)/shard_map/jit(_where)/select_n | solution.py:179
  1.9 3.8 %collective-permute-start = (bf16[256,8,128]{2,1,0:T(8,128)(2,1)S(1)}, bf16[256,8,128]{2,1,0:T(8,128)(2,1)}, u32[]{:S(2)}, u32[]{:S(2)}) collective-permute-start(bf16[256,8,128]{2,1,0:T(8,128)(2,1)S(1)} %broadcast_select_fusion), channel_id=1, source_target_pairs={{0,8},{8,16},{16,24},{24,32},{32,40},{40,48},{48,56},{56,64},{64,7... | collective-permute-start | bytes 1572872 | tf_op jit(solution)/shard_map/ppermute | solution.py:33
  5.7 0.0 copy-start.4
  5.7 0.0 copy-done.2
  5.7 0.0 copy-done.3
  5.7 0.7 %copy-done.4 = s32[2,8,1]{1,2,0:T(1,128)S(1)} copy-done((s32[2,8,1]{1,2,0:T(1,128)S(1)}, s32[2,8,1]{1,2,0:T(1,128)}, u32[]{:S(2)}) %copy-start.4) | copy-done | bytes 88
  6.4 1.3 %query_prepare_kernel.1.qd_ref = bf16[8,2,256,128]{3,2,1,0:T(8,128)(2,1)} custom-call(bf16[256,8,128]{2,1,0:T(8,128)(2,1)S(1)} %bitcast.11, bf16[256,8,128]{2,1,0:T(8,128)(2,1)S(1)} %bitcast.12, s32[2,8]{1,0:T(2,128)S(1)} %bitcast.13), custom_call_target="tpu_custom_call" | custom-call | flops 1000000 | bytes 1048576 | tf_op jit(solution)/shard_map/query_prepare_kernel/pallas_call | solution.py:168
  7.7 0.0 copy-start
  7.7 0.0 copy-start.1
  7.7 4.4 %all-to-all-start = ((bf16[8,2,256,128]{3,2,1,0:T(8,128)(2,1)}), bf16[8,2,256,128]{3,2,1,0:T(8,128)(2,1)S(1)}, u32[]{:S(2)}, u32[]{:S(2)}) async-start(bf16[8,2,256,128]{3,2,1,0:T(8,128)(2,1)} %query_prepare_kernel.1.qd_ref), calls=%async_computation | async-start | bytes 2097152 | tf_op jit(solution)/shard_map/all_to_all | solution.py:188
  12.1 13.3 %collective-permute-done.here_ref = bf16[256,8,128]{2,1,0:T(8,128)(2,1)} collective-permute-done((bf16[256,8,128]{2,1,0:T(8,128)(2,1)S(1)}, bf16[256,8,128]{2,1,0:T(8,128)(2,1)}, u32[]{:S(2)}, u32[]{:S(2)}) %collective-permute-start) | collective-permute-done | bytes 524320 | tf_op jit(solution)/shard_map/ppermute | solution.py:33
  25.5 1.9 %collective-permute-start.1 = (bf16[256,8,128]{2,1,0:T(8,128)(2,1)}, bf16[256,8,128]{2,1,0:T(8,128)(2,1)}, u32[]{:S(2)}, u32[]{:S(2)}) collective-permute-start(bf16[256,8,128]{2,1,0:T(8,128)(2,1)} %collective-permute-done.here_ref), channel_id=1, source_target_pairs={{0,1},{1,0},{2,3},{3,2},{4,5},{5,4},{6,7},{7,6},{8,9},{9,8},{10,11... | collective-permute-start | bytes 1572872 | tf_op jit(solution)/shard_map/ppermute | solution.py:191
  27.4 0.0 copy-done
  27.4 0.0 copy-done.1
  27.4 0.2 key_prepare_kernel.1.here_ref
  27.6 0.1 pad_add_fusion.where_ref
  27.7 1.9 %collective-permute-done.1.other_ref = bf16[256,8,128]{2,1,0:T(8,128)(2,1)} collective-permute-done((bf16[256,8,128]{2,1,0:T(8,128)(2,1)}, bf16[256,8,128]{2,1,0:T(8,128)(2,1)}, u32[]{:S(2)}, u32[]{:S(2)}) %collective-permute-start.1) | collective-permute-done | bytes 524320 | tf_op jit(solution)/shard_map/ppermute | solution.py:191
  29.6 1.4 %window_prepare_kernel.1.back_ref = bf16[2,8,256,128]{3,2,1,0:T(8,128)(2,1)S(1)} custom-call(s32[2]{0:T(128)S(1)} %pad_add_fusion.where_ref, bf16[256,8,128]{2,1,0:T(8,128)(2,1)} %collective-permute-done.here_ref, bf16[256,8,128]{2,1,0:T(8,128)(2,1)} %collective-permute-done.1.other_ref), custom_call_target="tpu_custom_call" | custom-call | flops 1000000 | bytes 1048576 | tf_op jit(solution)/shard_map/window_prepare_kernel/pallas_call | solution.py:168
  31.0 0.0 copy-start.5
  31.0 0.6 %copy-done.5 = s32[128]{0:T(128)S(1)} copy-done((s32[128]{0:T(128)S(1)}, s32[128]{0:T(128)}, u32[]{:S(2)}) %copy-start.5) | copy-done | bytes 536
  31.6 5.6 %query_side_kernel.1 = bf16[256,8,128]{2,1,0:T(8,128)(2,1)} custom-call(s32[2]{0:T(128)S(1)} %pad_add_fusion.where_ref, s32[1,128]{1,0:T(1,128)S(1)} %bitcast.14, bf16[8,2,256,128]{3,2,1,0:T(8,128)(2,1)} %query_prepare_kernel.1.qd_ref, bf16[2,8,256,128]{3,2,1,0:T(8,128)(2,1)S(1)} %window_prepare_kernel.1.back_ref, ...), custom_call_target="tpu_custom_call" | custom-call | flops 806306368 | bytes 1048576 | tf_op jit(solution)/shard_map/query_side_kernel/pallas_call | solution.py:168
  37.3 0.0 all-to-all-done.qd_ref
  37.3 3.5 %key_side_kernel.1 = (bf16[2,256,128]{2,1,0:T(8,128)(2,1)S(1)}, f32[2,256,128]{2,1,0:T(8,128)S(1)}) custom-call(s32[2]{0:T(128)S(1)} %pad_add_fusion.where_ref, s32[1,128]{1,0:T(1,128)S(1)} %bitcast.15, bf16[8,2,256,128]{3,2,1,0:T(8,128)(2,1)S(1)} %all-to-all-done.qd_ref, bf16[2,8,256,128]{3,2,1,0:T(8,128)(2,1)S(1)} %window_prepare_kernel.1.back_ref, ...), custom_call_target="tpu_custom_call" | custom-call | flops 1073741824 | bytes 2097152 | tf_op jit(solution)/shard_map/key_side_kernel/pallas_call | solution.py:204
  40.8 3.7 %collective-permute-start.2 = (bf16[2,256,128]{2,1,0:T(8,128)(2,1)S(1)}, bf16[2,256,128]{2,1,0:T(8,128)(2,1)S(1)}, u32[]{:S(2)}, u32[]{:S(2)}) collective-permute-start(bf16[2,256,128]{2,1,0:T(8,128)(2,1)S(1)} %get-tuple-element.14), channel_id=1, source_target_pairs={{8,0},{16,8},{24,16},{32,24},{40,32},{48,40},{56,48},{64,56},{72,6... | collective-permute-start | bytes 393224 | tf_op jit(solution)/shard_map/ppermute | solution.py:33
  44.4 3.8 %collective-permute-done.2.back_ref = bf16[2,256,128]{2,1,0:T(8,128)(2,1)S(1)} collective-permute-done((bf16[2,256,128]{2,1,0:T(8,128)(2,1)S(1)}, bf16[2,256,128]{2,1,0:T(8,128)(2,1)S(1)}, u32[]{:S(2)}, u32[]{:S(2)}) %collective-permute-start.2) | collective-permute-done | bytes 131104 | tf_op jit(solution)/shard_map/ppermute | solution.py:33
  48.2 0.7 %finish_kernel.1 = (bf16[256,128]{1,0:T(8,128)(2,1)}, bf16[256,128]{1,0:T(8,128)(2,1)}) custom-call(f32[2,256,128]{2,1,0:T(8,128)S(1)} %get-tuple-element.13.own_ref, bf16[2,256,128]{2,1,0:T(8,128)(2,1)S(1)} %collective-permute-done.2.back_ref), custom_call_target="tpu_custom_call" | custom-call | flops 1000000 | bytes 1048576 | tf_op jit(solution)/shard_map/finish_kernel/pallas_call | solution.py:168
Async XLA Ops:
  0.6 5.1 %copy-start.2 = (bf16[256,8,1,128]{3,1,2,0:T(8,128)(2,1)S(1)}, bf16[256,8,1,128]{3,1,2,0:T(8,128)(2,1)}, u32[]{:S(2)}) copy-start(bf16[256,8,1,128]{3,1,2,0:T(8,128)(2,1)} %param.6) | copy-start | bytes 1572868
  0.7 5.1 %copy-start.3 = (bf16[256,8,1,128]{3,1,2,0:T(8,128)(2,1)S(1)}, bf16[256,8,1,128]{3,1,2,0:T(8,128)(2,1)}, u32[]{:S(2)}) copy-start(bf16[256,8,1,128]{3,1,2,0:T(8,128)(2,1)} %param.9) | copy-start | bytes 1572868
  1.9 23.6 %collective-permute-start = (bf16[256,8,128]{2,1,0:T(8,128)(2,1)S(1)}, bf16[256,8,128]{2,1,0:T(8,128)(2,1)}, u32[]{:S(2)}, u32[]{:S(2)}) collective-permute-start(bf16[256,8,128]{2,1,0:T(8,128)(2,1)S(1)} %broadcast_select_fusion), channel_id=1, source_target_pairs={{0,8},{8,16},{16,24},{24,32},{32,40},{40,48},{48,56},{56,64},{64,7... | collective-permute-start | bytes 1572872 | tf_op jit(solution)/shard_map/ppermute | solution.py:33
  5.7 0.7 %copy-start.4 = (s32[2,8,1]{1,2,0:T(1,128)S(1)}, s32[2,8,1]{1,2,0:T(1,128)}, u32[]{:S(2)}) copy-start(s32[2,8,1]{1,2,0:T(1,128)} %param.10) | copy-start | bytes 196
  7.7 19.7 %copy-start = (bf16[256,8,128]{2,1,0:T(8,128)(2,1)S(1)}, bf16[256,8,128]{2,1,0:T(8,128)(2,1)}, u32[]{:S(2)}) copy-start(bf16[256,8,128]{2,1,0:T(8,128)(2,1)} %key_ref.1) | copy-start | bytes 1572868
  7.7 19.7 %copy-start.1 = (bf16[256,8,128]{2,1,0:T(8,128)(2,1)S(1)}, bf16[256,8,128]{2,1,0:T(8,128)(2,1)}, u32[]{:S(2)}) copy-start(bf16[256,8,128]{2,1,0:T(8,128)(2,1)} %value_ref.1) | copy-start | bytes 1572868
  7.7 29.6 %all-to-all-start = ((bf16[8,2,256,128]{3,2,1,0:T(8,128)(2,1)}), bf16[8,2,256,128]{3,2,1,0:T(8,128)(2,1)S(1)}, u32[]{:S(2)}, u32[]{:S(2)}) async-start(bf16[8,2,256,128]{3,2,1,0:T(8,128)(2,1)} %query_prepare_kernel.1.qd_ref), calls=%async_computation | async-start | bytes 2097152 | tf_op jit(solution)/shard_map/all_to_all | solution.py:188
  25.5 4.1 %collective-permute-start.1 = (bf16[256,8,128]{2,1,0:T(8,128)(2,1)}, bf16[256,8,128]{2,1,0:T(8,128)(2,1)}, u32[]{:S(2)}, u32[]{:S(2)}) collective-permute-start(bf16[256,8,128]{2,1,0:T(8,128)(2,1)} %collective-permute-done.here_ref), channel_id=1, source_target_pairs={{0,1},{1,0},{2,3},{3,2},{4,5},{5,4},{6,7},{7,6},{8,9},{9,8},{10,11... | collective-permute-start | bytes 1572872 | tf_op jit(solution)/shard_map/ppermute | solution.py:191
  31.0 0.7 %copy-start.5 = (s32[128]{0:T(128)S(1)}, s32[128]{0:T(128)}, u32[]{:S(2)}) copy-start(s32[128]{0:T(128)} %param.11) | copy-start | bytes 1540
  40.8 7.4 %collective-permute-start.2 = (bf16[2,256,128]{2,1,0:T(8,128)(2,1)S(1)}, bf16[2,256,128]{2,1,0:T(8,128)(2,1)S(1)}, u32[]{:S(2)}, u32[]{:S(2)}) collective-permute-start(bf16[2,256,128]{2,1,0:T(8,128)(2,1)S(1)} %get-tuple-element.14), channel_id=1, source_target_pairs={{8,0},{16,8},{24,16},{32,24},{40,32},{48,40},{56,48},{64,56},{72,6... | collective-permute-start | bytes 393224 | tf_op jit(solution)/shard_map/ppermute | solution.py:33

commit v3 on v2

--- a/solution.py
+++ b/solution.py
@@ -16,7 +16,7 @@
 
 
 def params():
-    return pltpu.CompilerParams(vmem_limit_bytes=40 * 1024 * 1024)
+    return pltpu.CompilerParams(vmem_limit_bytes=16 * 1024 * 1024)
 
 
 def dot_nt(a, b):
@@ -83,48 +83,59 @@
     )
 
 
-def query_prepare_kernel(query_ref, grad_ref, exp_ref, qd_ref):
+def query_prepare_kernel(exp_ref, query_ref, grad_ref, qd_ref):
+    qd_ref[:, 0] = jnp.swapaxes(query_ref[...], 0, 1)
     blocks, groups = exp_ref.shape
     rows = grad_ref.shape[0] // blocks
-    qd_ref[:, 0] = jnp.swapaxes(query_ref[...], 0, 1)
     factor = jnp.exp2(exp_ref[...].astype(F32)).astype(BF16)
     for b in range(blocks):
         part = pl.ds(b * rows, rows)
         qd_ref[:, 1, part] = jnp.swapaxes(grad_ref[part], 0, 1) * factor[b][:, None, None]
 
 
-def key_prepare_kernel(key_ref, value_ref, kv_ref):
+def key_prepare_kernel(where_ref, lengths_ref, key_ref, value_ref, kv_ref, bias_ref):
+    fill_bias(bias_ref, lengths_ref, where_ref[0])
     kv_ref[0] = jnp.swapaxes(key_ref[...], 0, 1)
     kv_ref[1] = jnp.swapaxes(value_ref[...], 0, 1)
 
 
-def window_prepare_kernel(where_ref, here_ref, other_ref, kv_ref):
-    core = where_ref[1] % 2
-    kv_ref[core] = jnp.swapaxes(here_ref[...], 0, 1)
-    kv_ref[1 - core] = jnp.swapaxes(other_ref[...], 0, 1)
-
-
-def query_side_kernel(scaling, where_ref, lengths_ref, qd_ref, back_ref, here_ref, out_ref, bias, grads):
-    fill_bias(bias, lengths_ref, where_ref[0])
+def query_grads(scaling, g, qd_ref, back_ref, kv_ref, bias_ref):
     rows = qd_ref.shape[2]
     half = rows // 2
-    for g in range(qd_ref.shape[0]):
-        key = jnp.concatenate([back_ref[0, g], here_ref[0, g]], axis=0)
-        value = jnp.concatenate([back_ref[1, g], here_ref[1, g]], axis=0)
-        _, _, middle, corners = pair_terms(qd_ref[g, 0], qd_ref[g, 1], key, value, bias[...], scaling)
-        key_t = key.T
-        total = dot_nn(key_t[:, half : half + rows], middle) + jnp.concatenate(
-            [dot_nn(key_t[:, :half], corners[:, :half]), dot_nn(key_t[:, half + rows :], corners[:, half:])],
-            axis=1,
-        )
-        grads[g] = (total * scaling).astype(BF16).T
+    key = jnp.concatenate([back_ref[0, g], kv_ref[0, g]], axis=0)
+    value = jnp.concatenate([back_ref[1, g], kv_ref[1, g]], axis=0)
+    _, _, middle, corners = pair_terms(qd_ref[g, 0], qd_ref[g, 1], key, value, bias_ref[...], scaling)
+    key_t = key.T
+    total = dot_nn(key_t[:, half : half + rows], middle) + jnp.concatenate(
+        [dot_nn(key_t[:, :half], corners[:, :half]), dot_nn(key_t[:, half + rows :], corners[:, half:])],
+        axis=1,
+    )
+    return (total * scaling).astype(BF16).T
+
+
+def early_query_kernel(scaling, where_ref, bias_ref, here_ref, other_ref, kv_ref, qd_ref, out_ref, back_ref):
+    even = where_ref[1] % 2 == 0
+    for g in range(here_ref.shape[0]):
+        here, other = here_ref[g], other_ref[g]
+        back_ref[0, g] = jnp.where(even, here, other)
+        back_ref[1, g] = jnp.where(even, other, here)
+    for g in range(out_ref.shape[0]):
+        out_ref[g] = query_grads(scaling, g, qd_ref, back_ref, kv_ref, bias_ref)
+
+
+def late_query_kernel(scaling, bias_ref, back_ref, kv_ref, early_ref, qd_ref, out_ref, grads):
+    first, last = early_ref.shape[0], qd_ref.shape[0]
+    grads[:first] = early_ref[...]
+    for g in range(first, last):
+        grads[g] = query_grads(scaling, g, qd_ref, back_ref, kv_ref, bias_ref)
     out_ref[...] = jnp.swapaxes(grads[...], 0, 1)
 
 
-def key_side_kernel(scaling, where_ref, lengths_ref, qd_ref, back_ref, here_ref, cross_ref, own_ref, bias, mid_terms, left_terms, right_terms):
+def key_side_kernel(
+    scaling, where_ref, bias, qd_ref, back_ref, here_ref, cross_ref, own_ref, mid_terms, left_terms, right_terms
+):
     heads, _, rows, width = qd_ref.shape
     half = rows // 2
-    fill_bias(bias, lengths_ref, where_ref[0])
     key = jnp.concatenate([back_ref[0, 0], here_ref[0, 0]], axis=0)
     value = jnp.concatenate([back_ref[1, 0], here_ref[1, 0]], axis=0)
     for h in range(heads):
@@ -161,13 +172,12 @@
     lengths = lengths.reshape(1, -1)
     pairs = 8
     flops = 2 * 2 * rows * rows * width * pairs
-    bias = pltpu.VMEM((rows + rows // 2, rows), F32)
-
-    def call(kernel, operands, out_shape, scratch=(), scalars=0, dots=0):
+
+    def call(kernel, operands, out_shape, scratch=(), first=VMEM, dots=0):
         many = isinstance(out_shape, list)
         return pl.pallas_call(
             kernel,
-            in_specs=[SMEM] * scalars + [VMEM] * (len(operands) - scalars),
+            in_specs=[first] + [VMEM] * (len(operands) - 1),
             out_specs=[VMEM] * len(out_shape) if many else VMEM,
             out_shape=out_shape,
             scratch_shapes=list(scratch),
@@ -176,30 +186,31 @@
             name=(kernel.func if isinstance(kernel, functools.partial) else kernel).__name__,
         )(*operands)
 
-    half_kv = jnp.where(device % 2 == 0, keys, values)
-    half_back = shifted(half_kv, "seq", 1)
-    queries_3d = queries.reshape(rows, groups, width)
-    queries_3d, half_kv = lax.optimization_barrier((queries_3d, half_kv))
+    half_kv = jnp.swapaxes(jnp.where(device % 2 == 0, keys, values), 0, 1)
+    exponents = exponents.reshape(-1, groups)
+    here = shifted(half_kv, "seq", 1)
+    queries, half_kv = lax.optimization_barrier((queries, half_kv))
     qd = call(
         query_prepare_kernel,
-        (queries_3d, grad_out.reshape(rows, groups, width), exponents.reshape(-1, groups)),
+        (exponents, queries.reshape(rows, groups, width), grad_out.reshape(rows, groups, width)),
         shape((groups, 2, rows, width), BF16),
     )
     qd_group = lax.all_to_all(qd, "tp", split_axis=0, concat_axis=0, tiled=True)
     kv_shape = shape((2, groups, rows, width), BF16)
-    kv = call(key_prepare_kernel, (keys, values), kv_shape)
-    other_half = lax.ppermute(half_back, "tp", [(d, d ^ 1) for d in range(lax.axis_size("tp"))])
-    kv_back = call(window_prepare_kernel, (where, half_back, other_half), kv_shape, scalars=1)
-    grad_queries = call(
-        functools.partial(query_side_kernel, scaling),
-        (where, lengths, qd, kv_back, kv),
-        shape((rows, groups, width), BF16),
-        [bias, pltpu.VMEM((groups, rows, width), BF16)],
-        scalars=1,
-        dots=3,
-    )
-    grad_queries, kv_back = lax.optimization_barrier((grad_queries, kv_back))
-    whole = lambda i, where: (0, 0)
+    kv, bias = call(
+        key_prepare_kernel,
+        (where, lengths, keys, values),
+        [kv_shape, shape((rows + rows // 2, rows), F32)],
+        first=SMEM,
+    )
+    other = lax.ppermute(here, "tp", [(d, d ^ 1) for d in range(lax.axis_size("tp"))])
+    early, back_kv = call(
+        functools.partial(early_query_kernel, scaling),
+        (where, bias, here, other, kv, qd),
+        [shape((3, rows, width), BF16), kv_shape],
+        dots=1,
+        first=SMEM,
+    )
     one_group = pl.BlockSpec((2, 1, rows, width), lambda i, where: (0, where[1], 0, 0))
     cross, own = pl.pallas_call(
         functools.partial(key_side_kernel, scaling),
@@ -207,14 +218,13 @@
             num_scalar_prefetch=1,
             grid=(1,),
             in_specs=[
-                pl.BlockSpec(lengths.shape, whole),
+                pl.BlockSpec(bias.shape, lambda i, where: (0, 0)),
                 pl.BlockSpec(qd_group.shape, lambda i, where: (0, 0, 0, 0)),
                 one_group,
                 one_group,
             ],
             out_specs=[pl.BlockSpec((2, rows, width), lambda i, where: (0, 0, 0))] * 2,
             scratch_shapes=[
-                bias,
                 pltpu.VMEM((2, rows, pairs * rows), BF16),
                 pltpu.VMEM((2, rows // 2, pairs * rows // 2), BF16),
                 pltpu.VMEM((2, rows // 2, pairs * rows // 2), BF16),
@@ -224,8 +234,15 @@
         compiler_params=params(),
         cost_estimate=pl.CostEstimate(flops=4 * flops, bytes_accessed=2**21, transcendentals=0),
         name="key_side_kernel",
-    )(where, lengths, qd_group, kv_back, kv)
+    )(where, bias, qd_group, back_kv, kv)
     back = shifted(cross, "seq", -1)
+    grad_queries = call(
+        functools.partial(late_query_kernel, scaling),
+        (bias, back_kv, kv, early, qd),
+        shape((rows, groups, width), BF16),
+        [pltpu.VMEM((groups, rows, width), BF16)],
+        dots=3,
+    )
     grad_keys, grad_values = call(finish_kernel, (own, back), [shape((rows, width), BF16)] * 2)
     return (
         grad_queries.reshape(queries.shape),

time: 49.2 us -> 46.9 us (0.953)
  waiting for transfers between devices: 19.1 us -> 13.9 us
  Pallas kernels: 12.6 us -> 13.9 us
  starting transfers between devices: 13.8 us -> 14.5 us
  local copies, waits for them, and re-layouts: 1.32 us -> 2 us
    ppermute x2, waiting for transfers between devices: 17.1 us -> 13.3 us  [shifted(): return lax.ppermute(block, axis, route)]
    transpose x0 -> x1, other arithmetic: none -> 1.45 us  [per_device(): half_kv = jnp.swapaxes(jnp.where(device % 2 == 0, keys, values), 0, 1)]
    ppermute x1, waiting for transfers between devices: 1.94 us -> 0.57 us  [per_device(): lax.ppermute(here, 'tp', [(d, d ^ 1) for d in range(lax.axis_size('tp'))])]
    pallas_call x5, Pallas kernels: 9.14 us -> 10.4 us  [call(): pl.pallas_call(kernel, in_specs=[first] + [VMEM] * (len(operands) - 1), o...]
    select_n x1 -> x0, other arithmetic: 1.19 us -> none  [per_device(): half_kv = jnp.where(device % 2 == 0, keys, values)]
    unnamed x12 -> x16, local copies, waits for them, and re-layouts: 1.32 us -> 2 us
    ppermute x2, starting transfers between devices: 7.48 us -> 8.15 us  [shifted(): return lax.ppermute(block, axis, route)]
  transfers between devices with their start and end apart: 4 -> 4, of which waited for: 3 -> 2; matrix products, arithmetic and copies ran while one was open for 0% -> 0% of each run, Pallas kernels for 17% -> 21%
where the time goes in v3:
time: 46.9 us; the launch traced here: 46.6 us
  starting transfers between devices  14.5 us (31%)
  Pallas kernels  13.9 us (30%)
  waiting for transfers between devices  13.9 us (30%)
  local copies, waits for them, and re-layouts  2 us (4%)
  other arithmetic  1.53 us (3%)
  between operations  0.76 us (2%)
    ppermute x2, waiting for transfers between devices, shifted(): return lax.ppermute(block, axis, route)  13.3 us
    pallas_call x5, Pallas kernels, call(): pl.pallas_call(kernel, in_specs=[first] + [VMEM] * (len(operands) - 1), o...  10.4 us
    ppermute x2, starting transfers between devices, shifted(): return lax.ppermute(block, axis, route)  8.15 us
    all_to_all x1, starting transfers between devices, per_device(): qd_group = lax.all_to_all(qd, 'tp', split_axis=0, concat_axis=0, tiled=True)  4.43 us
    pallas_call x1, Pallas kernels, per_device(): pl.pallas_call(functools.partial(key_side_kernel, scaling), grid_spec=plt...  3.49 us
    unnamed x16, local copies, waits for them, and re-layouts  2 us
    ppermute x1, starting transfers between devices, per_device(): lax.ppermute(here, 'tp', [(d, d ^ 1) for d in range(lax.axis_size('tp'))])  1.91 us
    transpose x1, other arithmetic, per_device(): half_kv = jnp.swapaxes(jnp.where(device % 2 == 0, keys, values), 0, 1)  1.45 us
  transfers between devices with their start and end apart: 4, of which 2 were waited for; matrix products, arithmetic and copies ran while one was open for 0% of the time, Pallas kernels for 21%

profile of v3, /device:TPU:24, one launch (start us, length us, event | category | flops | bytes accessed | tf_op | source)
XLA Modules:
  0.0 46.6 jit_solution(11505985187412442305)
XLA Ops:
  0.6 0.0 copy-start.2
  0.7 0.0 copy-start.3
  0.7 1.4 %fusion = bf16[8,256,128]{2,1,0:T(8,128)(2,1)S(1)} fusion(bf16[256,8,128]{2,1,0:T(8,128)(2,1)} %value_ref.1, bf16[256,8,128]{2,1,0:T(8,128)(2,1)} %key_ref.1, pred[]{:T(512)S(6)} %eq.5), kind=kLoop, calls=%fused_computation.1 | loop fusion | flops 262144 | bytes 1572865 | tf_op jit(solution)/shard_map/transpose | solution.py:189
  2.1 3.8 %collective-permute-start = (bf16[8,256,128]{2,1,0:T(8,128)(2,1)S(1)}, bf16[8,256,128]{2,1,0:T(8,128)(2,1)}, u32[]{:S(2)}, u32[]{:S(2)}) collective-permute-start(bf16[8,256,128]{2,1,0:T(8,128)(2,1)S(1)} %fusion), channel_id=1, source_target_pairs={{0,8},{8,16},{16,24},{24,32},{32,40},{40,48},{48,56},{56,64},{64,7... | collective-permute-start | bytes 1572872 | tf_op jit(solution)/shard_map/ppermute | solution.py:33
  5.9 0.0 copy-start.6
  6.0 0.0 copy-done.2
  6.0 0.0 copy-done.3
  6.0 0.7 %copy-done.6 = s32[2,8,1]{1,2,0:T(1,128)S(1)} copy-done((s32[2,8,1]{1,2,0:T(1,128)S(1)}, s32[2,8,1]{1,2,0:T(1,128)}, u32[]{:S(2)}) %copy-start.6) | copy-done | bytes 88
  6.6 1.3 %query_prepare_kernel.1.qd_ref = bf16[8,2,256,128]{3,2,1,0:T(8,128)(2,1)} custom-call(s32[2,8]{1,0:T(2,128)S(1)} %bitcast.15, bf16[256,8,128]{2,1,0:T(8,128)(2,1)S(1)} %bitcast.13, bf16[256,8,128]{2,1,0:T(8,128)(2,1)S(1)} %bitcast.14), custom_call_target="tpu_custom_call" | custom-call | flops 1000000 | bytes 1048576 | tf_op jit(solution)/shard_map/query_prepare_kernel/pallas_call | solution.py:178
  8.0 0.0 copy-start
  8.0 0.0 copy-start.1
  8.0 4.4 %all-to-all-start = ((bf16[8,2,256,128]{3,2,1,0:T(8,128)(2,1)}), bf16[8,2,256,128]{3,2,1,0:T(8,128)(2,1)S(1)}, u32[]{:S(2)}, u32[]{:S(2)}) async-start(bf16[8,2,256,128]{3,2,1,0:T(8,128)(2,1)} %query_prepare_kernel.1.qd_ref), calls=%async_computation | async-start | bytes 2097152 | tf_op jit(solution)/shard_map/all_to_all | solution.py:198
  12.4 13.3 %collective-permute-done.here_ref = bf16[8,256,128]{2,1,0:T(8,128)(2,1)} collective-permute-done((bf16[8,256,128]{2,1,0:T(8,128)(2,1)S(1)}, bf16[8,256,128]{2,1,0:T(8,128)(2,1)}, u32[]{:S(2)}, u32[]{:S(2)}) %collective-permute-start) | collective-permute-done | bytes 524320 | tf_op jit(solution)/shard_map/ppermute | solution.py:33
  25.7 1.9 %collective-permute-start.1 = (bf16[8,256,128]{2,1,0:T(8,128)(2,1)}, bf16[8,256,128]{2,1,0:T(8,128)(2,1)}, u32[]{:S(2)}, u32[]{:S(2)}) collective-permute-start(bf16[8,256,128]{2,1,0:T(8,128)(2,1)} %collective-permute-done.here_ref), channel_id=1, source_target_pairs={{0,1},{1,0},{2,3},{3,2},{4,5},{5,4},{6,7},{7,6},{8,9},{9,8},{10,11... | collective-permute-start | bytes 1572872 | tf_op jit(solution)/shard_map/ppermute | solution.py:206
  27.6 0.1 pad_add_fusion.where_ref
  27.7 0.0 copy-start.7
  27.7 0.0 copy-done
  27.7 0.0 copy-done.1
  27.7 0.6 %copy-done.7 = s32[128]{0:T(128)S(1)} copy-done((s32[128]{0:T(128)S(1)}, s32[128]{0:T(128)}, u32[]{:S(2)}) %copy-start.7) | copy-done | bytes 536
  28.4 0.9 %key_prepare_kernel.1 = (bf16[2,8,256,128]{3,2,1,0:T(8,128)(2,1)S(1)}, f32[384,256]{1,0:T(8,128)S(1)}) custom-call(s32[2]{0:T(128)S(1)} %pad_add_fusion.where_ref, s32[1,128]{1,0:T(1,128)S(1)} %bitcast.16, bf16[256,8,128]{2,1,0:T(8,128)(2,1)S(1)} %copy-done, bf16[256,8,128]{2,1,0:T(8,128)(2,1)S(1)} %copy-done.1), custom_call_target="tpu_custom_call" | custom-call | flops 1000000 | bytes 1048576 | tf_op jit(solution)/shard_map/key_prepare_kernel/pallas_call | solution.py:178
  29.3 0.6 %collective-permute-done.1.other_ref = bf16[8,256,128]{2,1,0:T(8,128)(2,1)} collective-permute-done((bf16[8,256,128]{2,1,0:T(8,128)(2,1)}, bf16[8,256,128]{2,1,0:T(8,128)(2,1)}, u32[]{:S(2)}, u32[]{:S(2)}) %collective-permute-start.1) | collective-permute-done | bytes 524320 | tf_op jit(solution)/shard_map/ppermute | solution.py:206
  29.9 3.2 %early_query_kernel.1 = (bf16[3,256,128]{2,1,0:T(8,128)(2,1)S(1)}, bf16[2,8,256,128]{3,2,1,0:T(8,128)(2,1)S(1)}) custom-call(s32[2]{0:T(128)S(1)} %pad_add_fusion.where_ref, f32[384,256]{1,0:T(8,128)S(1)} %get-tuple-element.12.bias_ref.bias, bf16[8,256,128]{2,1,0:T(8,128)(2,1)} %collective-permute-done.here_ref, ...), custom_call_target="tpu_custom_call" | custom-call | flops 269435456 | bytes 1048576 | tf_op jit(solution)/shard_map/early_query_kernel/pallas_call | solution.py:178
  33.0 0.0 copy-start.4
  33.0 0.7 %copy-done.4 = bf16[3,256,128]{2,1,0:T(8,128)(2,1)} copy-done((bf16[3,256,128]{2,1,0:T(8,128)(2,1)}, bf16[3,256,128]{2,1,0:T(8,128)(2,1)S(1)}, u32[]{:S(2)}) %copy-start.4) | copy-done | bytes 196632
  33.7 0.0 all-to-all-done.qd_ref
  33.7 0.0 copy-start.5
  33.7 3.5 %key_side_kernel.1 = (bf16[2,256,128]{2,1,0:T(8,128)(2,1)S(1)}, f32[2,256,128]{2,1,0:T(8,128)S(1)}) custom-call(s32[2]{0:T(128)S(1)} %pad_add_fusion.where_ref, f32[384,256]{1,0:T(8,128)S(1)} %get-tuple-element.12.bias_ref.bias, bf16[8,2,256,128]{3,2,1,0:T(8,128)(2,1)S(1)} %all-to-all-done.qd_ref, bf16[2,8,256,128]{3,2,1,0:T(8,128)(2,1)S(1)} %get-tuple-element.15.back_ref, ...), custom_call_target="tpu_custom_call" | custom-call | flops 1073741824 | bytes 2097152 | tf_op jit(solution)/shard_map/key_side_kernel/pallas_call | solution.py:215
  37.2 4.3 %collective-permute-start.2 = (bf16[2,256,128]{2,1,0:T(8,128)(2,1)S(1)}, bf16[2,256,128]{2,1,0:T(8,128)(2,1)S(1)}, u32[]{:S(2)}, u32[]{:S(2)}) collective-permute-start(bf16[2,256,128]{2,1,0:T(8,128)(2,1)S(1)} %get-tuple-element.18), channel_id=1, source_target_pairs={{8,0},{16,8},{24,16},{32,24},{40,32},{48,40},{56,48},{64,56},{72,6... | collective-permute-start | bytes 393224 | tf_op jit(solution)/shard_map/ppermute | solution.py:33
  41.5 0.0 copy-done.5
  41.5 4.3 %late_query_kernel.1 = bf16[256,8,128]{2,1,0:T(8,128)(2,1)} custom-call(f32[384,256]{1,0:T(8,128)S(1)} %get-tuple-element.12.bias_ref.bias, bf16[2,8,256,128]{3,2,1,0:T(8,128)(2,1)S(1)} %get-tuple-element.15.back_ref, bf16[2,8,256,128]{3,2,1,0:T(8,128)(2,1)S(1)} %get-tuple-element.13.kv_ref.here_ref, bf16[3,256,128]{2,1,0:T(8,128)(2,1)S(1)} %copy-done.5, ...), custom_call_target="tpu_custom_call" | custom-call | flops 806306368 | bytes 1048576 | tf_op jit(solution)/shard_map/late_query_kernel/pallas_call | solution.py:178
  45.9 0.0 collective-permute-done.2.back_ref
  45.9 0.7 %finish_kernel.1 = (bf16[256,128]{1,0:T(8,128)(2,1)}, bf16[256,128]{1,0:T(8,128)(2,1)}) custom-call(f32[2,256,128]{2,1,0:T(8,128)S(1)} %get-tuple-element.17.own_ref, bf16[2,256,128]{2,1,0:T(8,128)(2,1)S(1)} %collective-permute-done.2.back_ref), custom_call_target="tpu_custom_call" | custom-call | flops 1000000 | bytes 1048576 | tf_op jit(solution)/shard_map/finish_kernel/pallas_call | solution.py:178
Async XLA Ops:
  0.6 5.3 %copy-start.2 = (bf16[256,8,1,128]{3,1,2,0:T(8,128)(2,1)S(1)}, bf16[256,8,1,128]{3,1,2,0:T(8,128)(2,1)}, u32[]{:S(2)}) copy-start(bf16[256,8,1,128]{3,1,2,0:T(8,128)(2,1)} %param.6) | copy-start | bytes 1572868
  0.7 5.3 %copy-start.3 = (bf16[256,8,1,128]{3,1,2,0:T(8,128)(2,1)S(1)}, bf16[256,8,1,128]{3,1,2,0:T(8,128)(2,1)}, u32[]{:S(2)}) copy-start(bf16[256,8,1,128]{3,1,2,0:T(8,128)(2,1)} %param.9) | copy-start | bytes 1572868
  2.1 23.6 %collective-permute-start = (bf16[8,256,128]{2,1,0:T(8,128)(2,1)S(1)}, bf16[8,256,128]{2,1,0:T(8,128)(2,1)}, u32[]{:S(2)}, u32[]{:S(2)}) collective-permute-start(bf16[8,256,128]{2,1,0:T(8,128)(2,1)S(1)} %fusion), channel_id=1, source_target_pairs={{0,8},{8,16},{16,24},{24,32},{32,40},{40,48},{48,56},{56,64},{64,7... | collective-permute-start | bytes 1572872 | tf_op jit(solution)/shard_map/ppermute | solution.py:33
  5.9 0.7 %copy-start.6 = (s32[2,8,1]{1,2,0:T(1,128)S(1)}, s32[2,8,1]{1,2,0:T(1,128)}, u32[]{:S(2)}) copy-start(s32[2,8,1]{1,2,0:T(1,128)} %param.10) | copy-start | bytes 196
  8.0 19.8 %copy-start = (bf16[256,8,128]{2,1,0:T(8,128)(2,1)S(1)}, bf16[256,8,128]{2,1,0:T(8,128)(2,1)}, u32[]{:S(2)}) copy-start(bf16[256,8,128]{2,1,0:T(8,128)(2,1)} %key_ref.1) | copy-start | bytes 1572868
  8.0 19.8 %copy-start.1 = (bf16[256,8,128]{2,1,0:T(8,128)(2,1)S(1)}, bf16[256,8,128]{2,1,0:T(8,128)(2,1)}, u32[]{:S(2)}) copy-start(bf16[256,8,128]{2,1,0:T(8,128)(2,1)} %value_ref.1) | copy-start | bytes 1572868
  8.0 25.8 %all-to-all-start = ((bf16[8,2,256,128]{3,2,1,0:T(8,128)(2,1)}), bf16[8,2,256,128]{3,2,1,0:T(8,128)(2,1)S(1)}, u32[]{:S(2)}, u32[]{:S(2)}) async-start(bf16[8,2,256,128]{3,2,1,0:T(8,128)(2,1)} %query_prepare_kernel.1.qd_ref), calls=%async_computation | async-start | bytes 2097152 | tf_op jit(solution)/shard_map/all_to_all | solution.py:198
  25.7 4.1 %collective-permute-start.1 = (bf16[8,256,128]{2,1,0:T(8,128)(2,1)}, bf16[8,256,128]{2,1,0:T(8,128)(2,1)}, u32[]{:S(2)}, u32[]{:S(2)}) collective-permute-start(bf16[8,256,128]{2,1,0:T(8,128)(2,1)} %collective-permute-done.here_ref), channel_id=1, source_target_pairs={{0,1},{1,0},{2,3},{3,2},{4,5},{5,4},{6,7},{7,6},{8,9},{9,8},{10,11... | collective-permute-start | bytes 1572872 | tf_op jit(solution)/shard_map/ppermute | solution.py:206
  27.7 0.7 %copy-start.7 = (s32[128]{0:T(128)S(1)}, s32[128]{0:T(128)}, u32[]{:S(2)}) copy-start(s32[128]{0:T(128)} %param.11) | copy-start | bytes 1540
  33.0 0.7 %copy-start.4 = (bf16[3,256,128]{2,1,0:T(8,128)(2,1)}, bf16[3,256,128]{2,1,0:T(8,128)(2,1)S(1)}, u32[]{:S(2)}) copy-start(bf16[3,256,128]{2,1,0:T(8,128)(2,1)S(1)} %get-tuple-element.16.early_ref) | copy-start | bytes 589828
  33.7 7.8 %copy-start.5 = (bf16[3,256,128]{2,1,0:T(8,128)(2,1)S(1)}, bf16[3,256,128]{2,1,0:T(8,128)(2,1)}, u32[]{:S(2)}) copy-start(bf16[3,256,128]{2,1,0:T(8,128)(2,1)} %copy-done.4) | copy-start | bytes 589828
  37.2 8.7 %collective-permute-start.2 = (bf16[2,256,128]{2,1,0:T(8,128)(2,1)S(1)}, bf16[2,256,128]{2,1,0:T(8,128)(2,1)S(1)}, u32[]{:S(2)}, u32[]{:S(2)}) collective-permute-start(bf16[2,256,128]{2,1,0:T(8,128)(2,1)S(1)} %get-tuple-element.18), channel_id=1, source_target_pairs={{8,0},{16,8},{24,16},{32,24},{40,32},{48,40},{56,48},{64,56},{72,6... | collective-permute-start | bytes 393224 | tf_op jit(solution)/shard_map/ppermute | solution.py:33

commit v4 on v3

--- a/solution.py
+++ b/solution.py
@@ -93,18 +93,17 @@
         qd_ref[:, 1, part] = jnp.swapaxes(grad_ref[part], 0, 1) * factor[b][:, None, None]
 
 
-def key_prepare_kernel(where_ref, lengths_ref, key_ref, value_ref, kv_ref, bias_ref):
-    fill_bias(bias_ref, lengths_ref, where_ref[0])
+def key_prepare_kernel(where_ref, lengths_ref, key_ref, value_ref, kv_ref, bias_ref, bias):
+    fill_bias(bias, lengths_ref, where_ref[0])
+    bias_ref[...] = bias[...].astype(BF16)
     kv_ref[0] = jnp.swapaxes(key_ref[...], 0, 1)
     kv_ref[1] = jnp.swapaxes(value_ref[...], 0, 1)
 
 
-def query_grads(scaling, g, qd_ref, back_ref, kv_ref, bias_ref):
-    rows = qd_ref.shape[2]
+def query_grads(scaling, query, dout, key, value, bias):
+    rows = query.shape[0]
     half = rows // 2
-    key = jnp.concatenate([back_ref[0, g], kv_ref[0, g]], axis=0)
-    value = jnp.concatenate([back_ref[1, g], kv_ref[1, g]], axis=0)
-    _, _, middle, corners = pair_terms(qd_ref[g, 0], qd_ref[g, 1], key, value, bias_ref[...], scaling)
+    _, _, middle, corners = pair_terms(query, dout, key, value, bias, scaling)
     key_t = key.T
     total = dot_nn(key_t[:, half : half + rows], middle) + jnp.concatenate(
         [dot_nn(key_t[:, :half], corners[:, :half]), dot_nn(key_t[:, half + rows :], corners[:, half:])],
@@ -113,33 +112,58 @@
     return (total * scaling).astype(BF16).T
 
 
-def early_query_kernel(scaling, where_ref, bias_ref, here_ref, other_ref, kv_ref, qd_ref, out_ref, back_ref):
-    even = where_ref[1] % 2 == 0
-    for g in range(here_ref.shape[0]):
+def early_query_kernel(scaling, where_ref, bias_ref, here_ref, other_ref, kv_ref, qd_ref, stash_ref):
+    d = where_ref[1]
+    even = d % 2 == 0
+    groups = here_ref.shape[0]
+    early = (4 + 4 * groups - stash_ref.shape[0]) // 3
+    bias = bias_ref[...].astype(F32)
+
+    def window(g):
         here, other = here_ref[g], other_ref[g]
-        back_ref[0, g] = jnp.where(even, here, other)
-        back_ref[1, g] = jnp.where(even, other, here)
-    for g in range(out_ref.shape[0]):
-        out_ref[g] = query_grads(scaling, g, qd_ref, back_ref, kv_ref, bias_ref)
-
-
-def late_query_kernel(scaling, bias_ref, back_ref, kv_ref, early_ref, qd_ref, out_ref, grads):
-    first, last = early_ref.shape[0], qd_ref.shape[0]
-    grads[:first] = early_ref[...]
-    for g in range(first, last):
-        grads[g] = query_grads(scaling, g, qd_ref, back_ref, kv_ref, bias_ref)
+        return jnp.where(even, here, other), kv_ref[0, g], jnp.where(even, other, here), kv_ref[1, g]
+
+    for i, part in enumerate(window(d)):
+        stash_ref[i] = part
+    for g in range(early, groups):
+        for i, part in enumerate(window(g)):
+            stash_ref[4 + early + 4 * (g - early) + i] = part
+    for g in range(early):
+        key_back, key, value_back, value = window(g)
+        stash_ref[4 + g] = query_grads(
+            scaling,
+            qd_ref[g, 0],
+            qd_ref[g, 1],
+            jnp.concatenate([key_back, key], axis=0),
+            jnp.concatenate([value_back, value], axis=0),
+            bias,
+        )
+
+
+def late_query_kernel(scaling, bias_ref, stash_ref, qd_ref, out_ref, grads):
+    groups, rows, _ = grads.shape
+    late = qd_ref.shape[0]
+    early = groups - late
+    grads[:early] = stash_ref[4 : 4 + early]
+    bias = bias_ref[...].astype(F32)
+    for i in range(late):
+        at = 4 + early + 4 * i
+        key = stash_ref[at : at + 2].reshape(2 * rows, -1)
+        value = stash_ref[at + 2 : at + 4].reshape(2 * rows, -1)
+        grads[early + i] = query_grads(scaling, qd_ref[i, 0], qd_ref[i, 1], key, value, bias)
     out_ref[...] = jnp.swapaxes(grads[...], 0, 1)
 
 
 def key_side_kernel(
-    scaling, where_ref, bias, qd_ref, back_ref, here_ref, cross_ref, own_ref, mid_terms, left_terms, right_terms
+    scaling, bias_ref, qd_ref, window_ref, cross_ref, own_ref, mid_terms, left_terms, right_terms
 ):
     heads, _, rows, width = qd_ref.shape
     half = rows // 2
-    key = jnp.concatenate([back_ref[0, 0], here_ref[0, 0]], axis=0)
-    value = jnp.concatenate([back_ref[1, 0], here_ref[1, 0]], axis=0)
+    key = window_ref[:2].reshape(2 * rows, width)
+    value = window_ref[2:].reshape(2 * rows, width)
+    bias = bias_ref[...].astype(F32)
     for h in range(heads):
-        probs, probs_c, grads, grads_c = pair_terms(qd_ref[h, 0], qd_ref[h, 1], key, value, bias[...], scaling)
+        probs, probs_c, grads, grads_c = pair_terms(qd_ref[h, 0], qd_ref[h, 1], key, value, bias, scaling)
         at, at_half = pl.ds(h * rows, rows), pl.ds(h * half, half)
         mid_terms[0, :, at] = grads
         mid_terms[1, :, at] = probs
@@ -197,52 +221,59 @@
     )
     qd_group = lax.all_to_all(qd, "tp", split_axis=0, concat_axis=0, tiled=True)
     kv_shape = shape((2, groups, rows, width), BF16)
+    bias_shape = (rows + rows // 2, rows)
     kv, bias = call(
         key_prepare_kernel,
         (where, lengths, keys, values),
-        [kv_shape, shape((rows + rows // 2, rows), F32)],
+        [kv_shape, shape(bias_shape, BF16)],
+        [pltpu.VMEM(bias_shape, F32)],
         first=SMEM,
     )
     other = lax.ppermute(here, "tp", [(d, d ^ 1) for d in range(lax.axis_size("tp"))])
-    early, back_kv = call(
+    late = 2
+    early = groups - late
+    stash = call(
         functools.partial(early_query_kernel, scaling),
         (where, bias, here, other, kv, qd),
-        [shape((3, rows, width), BF16), kv_shape],
+        shape((4 + early + 4 * late, rows, width), BF16),
         dots=1,
         first=SMEM,
     )
-    one_group = pl.BlockSpec((2, 1, rows, width), lambda i, where: (0, where[1], 0, 0))
     cross, own = pl.pallas_call(
         functools.partial(key_side_kernel, scaling),
-        grid_spec=pltpu.PrefetchScalarGridSpec(
-            num_scalar_prefetch=1,
-            grid=(1,),
-            in_specs=[
-                pl.BlockSpec(bias.shape, lambda i, where: (0, 0)),
-                pl.BlockSpec(qd_group.shape, lambda i, where: (0, 0, 0, 0)),
-                one_group,
-                one_group,
-            ],
-            out_specs=[pl.BlockSpec((2, rows, width), lambda i, where: (0, 0, 0))] * 2,
-            scratch_shapes=[
-                pltpu.VMEM((2, rows, pairs * rows), BF16),
-                pltpu.VMEM((2, rows // 2, pairs * rows // 2), BF16),
-                pltpu.VMEM((2, rows // 2, pairs * rows // 2), BF16),
-            ],
-        ),
+        grid=(1,),
+        in_specs=[
+            pl.BlockSpec(bias.shape, lambda i: (0, 0)),
+            pl.BlockSpec(qd_group.shape, lambda i: (0, 0, 0, 0)),
+            pl.BlockSpec((4, rows, width), lambda i: (0, 0, 0)),
+        ],
+        out_specs=[pl.BlockSpec((2, rows, width), lambda i: (0, 0, 0))] * 2,
         out_shape=[shape((2, rows, width), BF16), shape((2, rows, width), F32)],
+        scratch_shapes=[
+            pltpu.VMEM((2, rows, pairs * rows), BF16),
+            pltpu.VMEM((2, rows // 2, pairs * rows // 2), BF16),
+            pltpu.VMEM((2, rows // 2, pairs * rows // 2), BF16),
+        ],
         compiler_params=params(),
         cost_estimate=pl.CostEstimate(flops=4 * flops, bytes_accessed=2**21, transcendentals=0),
         name="key_side_kernel",
-    )(where, bias, qd_group, back_kv, kv)
+    )(bias, qd_group, stash)
     back = shifted(cross, "seq", -1)
-    grad_queries = call(
+    grad_queries = pl.pallas_call(
         functools.partial(late_query_kernel, scaling),
-        (bias, back_kv, kv, early, qd),
-        shape((rows, groups, width), BF16),
-        [pltpu.VMEM((groups, rows, width), BF16)],
-        dots=3,
-    )
+        grid=(1,),
+        in_specs=[
+            pl.BlockSpec(bias.shape, lambda i: (0, 0)),
+            pl.BlockSpec(stash.shape, lambda i: (0, 0, 0)),
+            pl.BlockSpec((late, 2, rows, width), lambda i: (groups // late - 1, 0, 0, 0)),
+        ],
+        out_specs=pl.BlockSpec((rows, groups, width), lambda i: (0, 0, 0)),
+        out_shape=shape((rows, groups, width), BF16),
+        scratch_shapes=[pltpu.VMEM((groups, rows, width), BF16)],
+        compiler_params=params(),
+        cost_estimate=pl.CostEstimate(flops=3 * flops, bytes_accessed=2**20, transcendentals=0),
+        name="late_query_kernel",
+    )(bias, stash, qd)
     grad_keys, grad_values = call(finish_kernel, (own, back), [shape((rows, width), BF16)] * 2)
     return (
         grad_queries.reshape(queries.shape),

time: 46.9 us -> 44.8 us (0.955)
  local copies, waits for them, and re-layouts: 2 us -> 0.02 us
  waiting for transfers between devices: 13.9 us -> 15.4 us
  Pallas kernels: 13.9 us -> 12.8 us
    pallas_call x5 -> x4, Pallas kernels: 10.4 us -> 6.94 us  [call(): pl.pallas_call(kernel, in_specs=[first] + [VMEM] * (len(operands) - 1), o...]
    pallas_call x1 -> x2, Pallas kernels: 3.49 us -> 5.84 us  [the longest x1 2.95 us: per_device(): pl.pallas_call(functools.partial(key_side_kernel, scaling), grid=(1,), in...]
    unnamed x16 -> x12, local copies, waits for them, and re-layouts: 2 us -> 0.02 us
    ppermute x2, waiting for transfers between devices: 13.3 us -> 14.5 us  [shifted(): return lax.ppermute(block, axis, route)]
  transfers between devices with their start and end apart: 4 -> 4, of which waited for: 2 -> 3; matrix products, arithmetic and copies ran while one was open for 0% -> 0% of each run, Pallas kernels for 21% -> 21%
where the time goes in v4:
time: 44.8 us; the launch traced here: 44.5 us
  waiting for transfers between devices  15.4 us (34%)
  starting transfers between devices  14.1 us (31%)
  Pallas kernels  12.8 us (29%)
  other arithmetic  1.52 us (3%)
  between operations  0.75 us (2%)
    ppermute x2, waiting for transfers between devices, shifted(): return lax.ppermute(block, axis, route)  14.5 us
    ppermute x2, starting transfers between devices, shifted(): return lax.ppermute(block, axis, route)  7.74 us
    pallas_call x4, Pallas kernels, call(): pl.pallas_call(kernel, in_specs=[first] + [VMEM] * (len(operands) - 1), o...  6.94 us
    all_to_all x1, starting transfers between devices, per_device(): qd_group = lax.all_to_all(qd, 'tp', split_axis=0, concat_axis=0, tiled=True)  4.43 us
    pallas_call x1, Pallas kernels, per_device(): pl.pallas_call(functools.partial(key_side_kernel, scaling), grid=(1,), in...  2.95 us
    pallas_call x1, Pallas kernels, per_device(): pl.pallas_call(functools.partial(late_query_kernel, scaling), grid=(1,),...  2.88 us
    ppermute x1, starting transfers between devices, per_device(): lax.ppermute(here, 'tp', [(d, d ^ 1) for d in range(lax.axis_size('tp'))])  1.91 us
    transpose x1, other arithmetic, per_device(): half_kv = jnp.swapaxes(jnp.where(device % 2 == 0, keys, values), 0, 1)  1.45 us
  transfers between devices with their start and end apart: 4, of which 3 were waited for; matrix products, arithmetic and copies ran while one was open for 0% of the time, Pallas kernels for 21%

profile of v4, /device:TPU:24, one launch (start us, length us, event | category | flops | bytes accessed | tf_op | source)
XLA Modules:
  0.0 44.5 jit_solution(7088219476358373352)
XLA Ops:
  0.6 0.0 copy-start.2
  0.6 0.0 copy-start.4
  0.7 0.0 copy-start.3
  0.7 1.4 %fusion = bf16[8,256,128]{2,1,0:T(8,128)(2,1)S(1)} fusion(bf16[256,8,128]{2,1,0:T(8,128)(2,1)} %value_ref.1, bf16[256,8,128]{2,1,0:T(8,128)(2,1)} %key_ref.1, pred[]{:T(512)S(6)} %eq.5), kind=kLoop, calls=%fused_computation.1 | loop fusion | flops 262144 | bytes 1572865 | tf_op jit(solution)/shard_map/transpose | solution.py:213
  2.1 3.8 %collective-permute-start = (bf16[8,256,128]{2,1,0:T(8,128)(2,1)S(1)}, bf16[8,256,128]{2,1,0:T(8,128)(2,1)S(1)}, u32[]{:S(2)}, u32[]{:S(2)}) collective-permute-start(bf16[8,256,128]{2,1,0:T(8,128)(2,1)S(1)} %fusion), channel_id=1, source_target_pairs={{0,8},{8,16},{16,24},{24,32},{32,40},{40,48},{48,56},{56,64},{64,7... | collective-permute-start | bytes 1572872 | tf_op jit(solution)/shard_map/ppermute | solution.py:33
  6.0 0.0 copy-done.2
  6.0 0.0 copy-done.4
  6.0 0.0 copy-done.3
  6.0 1.3 %query_prepare_kernel.1.qd_ref = bf16[8,2,256,128]{3,2,1,0:T(8,128)(2,1)} custom-call(s32[2,8]{1,0:T(2,128)S(1)} %bitcast.15, bf16[256,8,128]{2,1,0:T(8,128)(2,1)S(1)} %bitcast.13, bf16[256,8,128]{2,1,0:T(8,128)(2,1)S(1)} %bitcast.14), custom_call_target="tpu_custom_call" | custom-call | flops 1000000 | bytes 1048576 | tf_op jit(solution)/shard_map/query_prepare_kernel/pallas_call | solution.py:202
  7.3 0.0 copy-start
  7.3 0.0 copy-start.1
  7.3 0.0 copy-start.5
  7.3 4.4 %all-to-all-start = ((bf16[8,2,256,128]{3,2,1,0:T(8,128)(2,1)}), bf16[8,2,256,128]{3,2,1,0:T(8,128)(2,1)S(1)}, u32[]{:S(2)}, u32[]{:S(2)}) async-start(bf16[8,2,256,128]{3,2,1,0:T(8,128)(2,1)} %query_prepare_kernel.1.qd_ref), calls=%async_computation | async-start | bytes 2097152 | tf_op jit(solution)/shard_map/all_to_all | solution.py:222
  11.7 13.9 %collective-permute-done.here_ref = bf16[8,256,128]{2,1,0:T(8,128)(2,1)S(1)} collective-permute-done((bf16[8,256,128]{2,1,0:T(8,128)(2,1)S(1)}, bf16[8,256,128]{2,1,0:T(8,128)(2,1)S(1)}, u32[]{:S(2)}, u32[]{:S(2)}) %collective-permute-start) | collective-permute-done | bytes 524320 | tf_op jit(solution)/shard_map/ppermute | solution.py:33
  25.6 1.9 %collective-permute-start.1 = (bf16[8,256,128]{2,1,0:T(8,128)(2,1)S(1)}, bf16[8,256,128]{2,1,0:T(8,128)(2,1)S(1)}, u32[]{:S(2)}, u32[]{:S(2)}) collective-permute-start(bf16[8,256,128]{2,1,0:T(8,128)(2,1)S(1)} %collective-permute-done.here_ref), channel_id=1, source_target_pairs={{0,1},{1,0},{2,3},{3,2},{4,5},{5,4},{6,7},{7,6},{8,9},{9,8},{10,11... | collective-permute-start | bytes 1572872 | tf_op jit(solution)/shard_map/ppermute | solution.py:232
  27.5 0.1 pad_add_fusion.where_ref
  27.6 0.0 copy-done
  27.6 0.0 copy-done.1
  27.6 0.0 copy-done.5
  27.6 0.9 %key_prepare_kernel.1 = (bf16[2,8,256,128]{3,2,1,0:T(8,128)(2,1)S(1)}, bf16[384,256]{1,0:T(8,128)(2,1)S(1)}) custom-call(s32[2]{0:T(128)S(1)} %pad_add_fusion.where_ref, s32[1,128]{1,0:T(1,128)S(1)} %bitcast.16, bf16[256,8,128]{2,1,0:T(8,128)(2,1)S(1)} %copy-done, bf16[256,8,128]{2,1,0:T(8,128)(2,1)S(1)} %copy-done.1), custom_call_target="tpu_custom_call" | custom-call | flops 1000000 | bytes 1048576 | tf_op jit(solution)/shard_map/key_prepare_kernel/pallas_call | solution.py:202
  28.6 0.9 %collective-permute-done.1.other_ref = bf16[8,256,128]{2,1,0:T(8,128)(2,1)S(1)} collective-permute-done((bf16[8,256,128]{2,1,0:T(8,128)(2,1)S(1)}, bf16[8,256,128]{2,1,0:T(8,128)(2,1)S(1)}, u32[]{:S(2)}, u32[]{:S(2)}) %collective-permute-start.1) | collective-permute-done | bytes 524320 | tf_op jit(solution)/shard_map/ppermute | solution.py:232
  29.4 4.0 %early_query_kernel.1.stash_ref.window_ref = bf16[18,256,128]{2,1,0:T(8,128)(2,1)S(1)} custom-call(s32[2]{0:T(128)S(1)} %pad_add_fusion.where_ref, bf16[384,256]{1,0:T(8,128)(2,1)S(1)} %get-tuple-element.10.bias_ref, bf16[8,256,128]{2,1,0:T(8,128)(2,1)S(1)} %collective-permute-done.here_ref, bf16[8,256,128]{2,1,0:T(8,128)(2,1)S(1)} %collective-permute-done.1.other_ref, ...), custom_call_target="tpu_custom_call" | custom-call | flops 269435456 | bytes 1048576 | tf_op jit(solution)/shard_map/early_query_kernel/pallas_call | solution.py:202
  33.5 0.0 all-to-all-done.qd_ref
  33.5 3.0 %key_side_kernel.1 = (bf16[2,256,128]{2,1,0:T(8,128)(2,1)S(1)}, f32[2,256,128]{2,1,0:T(8,128)S(1)}) custom-call(bf16[384,256]{1,0:T(8,128)(2,1)S(1)} %get-tuple-element.10.bias_ref, bf16[8,2,256,128]{3,2,1,0:T(8,128)(2,1)S(1)} %all-to-all-done.qd_ref, bf16[18,256,128]{2,1,0:T(8,128)(2,1)S(1)} %early_query_kernel.1.stash_ref.window_ref), custom_call_target="tpu_custom_call" | custom-call | flops 1073741824 | bytes 2097152 | tf_op jit(solution)/shard_map/key_side_kernel/pallas_call | solution.py:242
  36.4 3.9 %collective-permute-start.2 = (bf16[2,256,128]{2,1,0:T(8,128)(2,1)S(1)}, bf16[2,256,128]{2,1,0:T(8,128)(2,1)S(1)}, u32[]{:S(2)}, u32[]{:S(2)}) collective-permute-start(bf16[2,256,128]{2,1,0:T(8,128)(2,1)S(1)} %get-tuple-element.14), channel_id=1, source_target_pairs={{8,0},{16,8},{24,16},{32,24},{40,32},{48,40},{56,48},{64,56},{72,6... | collective-permute-start | bytes 393224 | tf_op jit(solution)/shard_map/ppermute | solution.py:33
  40.3 2.9 %late_query_kernel.1 = bf16[256,8,128]{2,1,0:T(8,128)(2,1)} custom-call(bf16[384,256]{1,0:T(8,128)(2,1)S(1)} %get-tuple-element.10.bias_ref, bf16[18,256,128]{2,1,0:T(8,128)(2,1)S(1)} %early_query_kernel.1.stash_ref.window_ref, bf16[8,2,256,128]{3,2,1,0:T(8,128)(2,1)} %query_prepare_kernel.1.qd_ref), custom_call_target="tpu_custom_call" | custom-call | flops 805306368 | bytes 1048576 | tf_op jit(solution)/shard_map/late_query_kernel/pallas_call | solution.py:262
  43.2 0.6 %collective-permute-done.2.back_ref = bf16[2,256,128]{2,1,0:T(8,128)(2,1)S(1)} collective-permute-done((bf16[2,256,128]{2,1,0:T(8,128)(2,1)S(1)}, bf16[2,256,128]{2,1,0:T(8,128)(2,1)S(1)}, u32[]{:S(2)}, u32[]{:S(2)}) %collective-permute-start.2) | collective-permute-done | bytes 131104 | tf_op jit(solution)/shard_map/ppermute | solution.py:33
  43.9 0.7 %finish_kernel.1 = (bf16[256,128]{1,0:T(8,128)(2,1)}, bf16[256,128]{1,0:T(8,128)(2,1)}) custom-call(f32[2,256,128]{2,1,0:T(8,128)S(1)} %get-tuple-element.13.own_ref, bf16[2,256,128]{2,1,0:T(8,128)(2,1)S(1)} %collective-permute-done.2.back_ref), custom_call_target="tpu_custom_call" | custom-call | flops 1000000 | bytes 1048576 | tf_op jit(solution)/shard_map/finish_kernel/pallas_call | solution.py:202
Async XLA Ops:
  0.6 5.3 %copy-start.2 = (bf16[256,8,1,128]{3,1,2,0:T(8,128)(2,1)S(1)}, bf16[256,8,1,128]{3,1,2,0:T(8,128)(2,1)}, u32[]{:S(2)}) copy-start(bf16[256,8,1,128]{3,1,2,0:T(8,128)(2,1)} %param.6) | copy-start | bytes 1572868
  0.6 5.3 %copy-start.4 = (s32[2,8,1]{1,2,0:T(1,128)S(1)}, s32[2,8,1]{1,2,0:T(1,128)}, u32[]{:S(2)}) copy-start(s32[2,8,1]{1,2,0:T(1,128)} %param.10) | copy-start | bytes 196
  0.7 5.3 %copy-start.3 = (bf16[256,8,1,128]{3,1,2,0:T(8,128)(2,1)S(1)}, bf16[256,8,1,128]{3,1,2,0:T(8,128)(2,1)}, u32[]{:S(2)}) copy-start(bf16[256,8,1,128]{3,1,2,0:T(8,128)(2,1)} %param.9) | copy-start | bytes 1572868
  2.1 23.5 %collective-permute-start = (bf16[8,256,128]{2,1,0:T(8,128)(2,1)S(1)}, bf16[8,256,128]{2,1,0:T(8,128)(2,1)S(1)}, u32[]{:S(2)}, u32[]{:S(2)}) collective-permute-start(bf16[8,256,128]{2,1,0:T(8,128)(2,1)S(1)} %fusion), channel_id=1, source_target_pairs={{0,8},{8,16},{16,24},{24,32},{32,40},{40,48},{48,56},{56,64},{64,7... | collective-permute-start | bytes 1572872 | tf_op jit(solution)/shard_map/ppermute | solution.py:33
  7.3 20.3 %copy-start = (bf16[256,8,128]{2,1,0:T(8,128)(2,1)S(1)}, bf16[256,8,128]{2,1,0:T(8,128)(2,1)}, u32[]{:S(2)}) copy-start(bf16[256,8,128]{2,1,0:T(8,128)(2,1)} %key_ref.1) | copy-start | bytes 1572868
  7.3 20.3 %copy-start.1 = (bf16[256,8,128]{2,1,0:T(8,128)(2,1)S(1)}, bf16[256,8,128]{2,1,0:T(8,128)(2,1)}, u32[]{:S(2)}) copy-start(bf16[256,8,128]{2,1,0:T(8,128)(2,1)} %value_ref.1) | copy-start | bytes 1572868
  7.3 20.3 %copy-start.5 = (s32[128]{0:T(128)S(1)}, s32[128]{0:T(128)}, u32[]{:S(2)}) copy-start(s32[128]{0:T(128)} %param.11) | copy-start | bytes 1540
  7.3 26.2 %all-to-all-start = ((bf16[8,2,256,128]{3,2,1,0:T(8,128)(2,1)}), bf16[8,2,256,128]{3,2,1,0:T(8,128)(2,1)S(1)}, u32[]{:S(2)}, u32[]{:S(2)}) async-start(bf16[8,2,256,128]{3,2,1,0:T(8,128)(2,1)} %query_prepare_kernel.1.qd_ref), calls=%async_computation | async-start | bytes 2097152 | tf_op jit(solution)/shard_map/all_to_all | solution.py:222
  25.6 3.8 %collective-permute-start.1 = (bf16[8,256,128]{2,1,0:T(8,128)(2,1)S(1)}, bf16[8,256,128]{2,1,0:T(8,128)(2,1)S(1)}, u32[]{:S(2)}, u32[]{:S(2)}) collective-permute-start(bf16[8,256,128]{2,1,0:T(8,128)(2,1)S(1)} %collective-permute-done.here_ref), channel_id=1, source_target_pairs={{0,1},{1,0},{2,3},{3,2},{4,5},{5,4},{6,7},{7,6},{8,9},{9,8},{10,11... | collective-permute-start | bytes 1572872 | tf_op jit(solution)/shard_map/ppermute | solution.py:232
  36.4 7.4 %collective-permute-start.2 = (bf16[2,256,128]{2,1,0:T(8,128)(2,1)S(1)}, bf16[2,256,128]{2,1,0:T(8,128)(2,1)S(1)}, u32[]{:S(2)}, u32[]{:S(2)}) collective-permute-start(bf16[2,256,128]{2,1,0:T(8,128)(2,1)S(1)} %get-tuple-element.14), channel_id=1, source_target_pairs={{8,0},{16,8},{24,16},{32,24},{40,32},{48,40},{56,48},{64,56},{72,6... | collective-permute-start | bytes 393224 | tf_op jit(solution)/shard_map/ppermute | solution.py:33

commit v5 on v4

--- a/solution.py
+++ b/solution.py
@@ -12,7 +12,7 @@
 F32 = jnp.float32
 MASKED = -1e30
 VMEM = pl.BlockSpec(memory_space=pltpu.VMEM)
-SMEM = pl.BlockSpec(memory_space=pltpu.SMEM)
+HBM = pl.BlockSpec(memory_space=pl.ANY)
 
 
 def params():
@@ -93,8 +93,8 @@
         qd_ref[:, 1, part] = jnp.swapaxes(grad_ref[part], 0, 1) * factor[b][:, None, None]
 
 
-def key_prepare_kernel(where_ref, lengths_ref, key_ref, value_ref, kv_ref, bias_ref, bias):
-    fill_bias(bias, lengths_ref, where_ref[0])
+def key_prepare_kernel(lengths_ref, key_ref, value_ref, kv_ref, bias_ref, bias):
+    fill_bias(bias, lengths_ref, lax.axis_index("seq") * bias.shape[1])
     bias_ref[...] = bias[...].astype(BF16)
     kv_ref[0] = jnp.swapaxes(key_ref[...], 0, 1)
     kv_ref[1] = jnp.swapaxes(value_ref[...], 0, 1)
@@ -112,55 +112,72 @@
     return (total * scaling).astype(BF16).T
 
 
-def early_query_kernel(scaling, where_ref, bias_ref, here_ref, other_ref, kv_ref, qd_ref, stash_ref):
-    d = where_ref[1]
-    even = d % 2 == 0
-    groups = here_ref.shape[0]
-    early = (4 + 4 * groups - stash_ref.shape[0]) // 3
+def early_query_kernel(scaling, bias_ref, here_ref, kv_ref, qd_all_ref, stash_ref, qd_ref, done):
+    d = lax.axis_index("tp")
+    half = here_ref.shape[0] // 2
+    first = (d & 1) * half
+    late = half - first
+    fetch = pltpu.make_async_copy(qd_all_ref.at[pl.ds(first, half)], qd_ref, done)
+    fetch.start()
     bias = bias_ref[...].astype(F32)
-
-    def window(g):
-        here, other = here_ref[g], other_ref[g]
-        return jnp.where(even, here, other), kv_ref[0, g], jnp.where(even, other, here), kv_ref[1, g]
-
-    for i, part in enumerate(window(d)):
-        stash_ref[i] = part
-    for g in range(early, groups):
-        for i, part in enumerate(window(g)):
-            stash_ref[4 + early + 4 * (g - early) + i] = part
-    for g in range(early):
-        key_back, key, value_back, value = window(g)
-        stash_ref[4 + g] = query_grads(
+    for i in range(2):
+        stash_ref[2 * i] = here_ref[half * i + (d & (half - 1))]
+        stash_ref[2 * i + 1] = kv_ref[i, d]
+        for y in range(half):
+            stash_ref[4 + half + 2 * y + i] = kv_ref[i, late + y]
+    fetch.wait()
+    for y in range(half):
+        stash_ref[4 + y] = query_grads(
             scaling,
-            qd_ref[g, 0],
-            qd_ref[g, 1],
-            jnp.concatenate([key_back, key], axis=0),
-            jnp.concatenate([value_back, value], axis=0),
+            qd_ref[y, 0],
+            qd_ref[y, 1],
+            jnp.concatenate([here_ref[y], kv_ref[0, first + y]], axis=0),
+            jnp.concatenate([here_ref[half + y], kv_ref[1, first + y]], axis=0),
             bias,
         )
 
 
-def late_query_kernel(scaling, bias_ref, stash_ref, qd_ref, out_ref, grads):
-    groups, rows, _ = grads.shape
-    late = qd_ref.shape[0]
-    early = groups - late
-    grads[:early] = stash_ref[4 : 4 + early]
+def late_query_kernel(scaling, bias_ref, other_ref, stash_ref, qd_ref, out_ref, grads, swapped, done):
+    half = other_ref.shape[0] // 2
+    first = (lax.axis_index("tp") & 1) * half
+    late = half - first
     bias = bias_ref[...].astype(F32)
-    for i in range(late):
-        at = 4 + early + 4 * i
-        key = stash_ref[at : at + 2].reshape(2 * rows, -1)
-        value = stash_ref[at + 2 : at + 4].reshape(2 * rows, -1)
-        grads[early + i] = query_grads(scaling, qd_ref[i, 0], qd_ref[i, 1], key, value, bias)
-    out_ref[...] = jnp.swapaxes(grads[...], 0, 1)
+    for y in range(half):
+        grads[first + y] = stash_ref[4 + y]
+        at = 4 + half + 2 * y
+        grads[late + y] = query_grads(
+            scaling,
+            qd_ref[y, 0],
+            qd_ref[y, 1],
+            jnp.concatenate([other_ref[y], stash_ref[at]], axis=0),
+            jnp.concatenate([other_ref[half + y], stash_ref[at + 1]], axis=0),
+            bias,
+        )
+    chunks = done.shape[0]
+    rows = swapped.shape[0] // chunks
+    copies = []
+    for i in range(chunks):
+        part = pl.ds(i * rows, rows)
+        swapped[part] = jnp.swapaxes(grads[:, part], 0, 1)
+        copies.append(pltpu.make_async_copy(swapped.at[part], out_ref.at[part], done.at[i]))
+        copies[-1].start()
+    for copy in copies:
+        copy.wait()
 
 
 def key_side_kernel(
-    scaling, bias_ref, qd_ref, window_ref, cross_ref, own_ref, mid_terms, left_terms, right_terms
+    scaling, bias_ref, qd_ref, window_ref, other_ref, qd_here_ref, cross_ref, own_ref, late_ref, mid_terms, left_terms, right_terms, done
 ):
     heads, _, rows, width = qd_ref.shape
     half = rows // 2
-    key = window_ref[:2].reshape(2 * rows, width)
-    value = window_ref[2:].reshape(2 * rows, width)
+    d = lax.axis_index("tp")
+    count = other_ref.shape[0] // 2
+    fetch = pltpu.make_async_copy(qd_here_ref.at[pl.ds((1 - (d & 1)) * count, count)], late_ref, done)
+    fetch.start()
+    came_here = (d >= count) == ((d & 1) == 1)
+    back = [jnp.where(came_here, window_ref[2 * i], other_ref[count * i + (d & (count - 1))]) for i in range(2)]
+    key = jnp.concatenate([back[0], window_ref[1]], axis=0)
+    value = jnp.concatenate([back[1], window_ref[3]], axis=0)
     bias = bias_ref[...].astype(F32)
     for h in range(heads):
         probs, probs_c, grads, grads_c = pair_terms(qd_ref[h, 0], qd_ref[h, 1], key, value, bias, scaling)
@@ -180,6 +197,7 @@
         cross_ref[i, half:] = middle[:half].astype(BF16)
         own_ref[i, :half] = middle[half:]
         own_ref[i, half:] = dot_nn(right_terms[i], late) * factor
+    fetch.wait()
 
 
 def finish_kernel(own_ref, back_ref, key_ref, value_ref):
@@ -192,17 +210,16 @@
     scaling = width ** (-0.5)
     shape = jax.ShapeDtypeStruct
     device = lax.axis_index("tp")
-    where = jnp.stack([lax.axis_index("seq") * rows, device]).astype(jnp.int32)
     lengths = lengths.reshape(1, -1)
     pairs = 8
     flops = 2 * 2 * rows * rows * width * pairs
 
-    def call(kernel, operands, out_shape, scratch=(), first=VMEM, dots=0):
+    def call(kernel, operands, out_shape, scratch=(), last=VMEM, out=VMEM, dots=0):
         many = isinstance(out_shape, list)
         return pl.pallas_call(
             kernel,
-            in_specs=[first] + [VMEM] * (len(operands) - 1),
-            out_specs=[VMEM] * len(out_shape) if many else VMEM,
+            in_specs=[VMEM] * (len(operands) - 1) + [last],
+            out_specs=[out] * len(out_shape) if many else out,
             out_shape=out_shape,
             scratch_shapes=list(scratch),
             compiler_params=params(),
@@ -210,7 +227,9 @@
             name=(kernel.func if isinstance(kernel, functools.partial) else kernel).__name__,
         )(*operands)
 
-    half_kv = jnp.swapaxes(jnp.where(device % 2 == 0, keys, values), 0, 1)
+    half = groups // 2
+    half_kv = [lax.dynamic_slice(block, (0, (device & 1) * half, 0), (rows, half, width)) for block in (keys, values)]
+    half_kv = jnp.swapaxes(jnp.concatenate(half_kv, axis=1), 0, 1)
     exponents = exponents.reshape(-1, groups)
     here = shifted(half_kv, "seq", 1)
     queries, half_kv = lax.optimization_barrier((queries, half_kv))
@@ -224,56 +243,47 @@
     bias_shape = (rows + rows // 2, rows)
     kv, bias = call(
         key_prepare_kernel,
-        (where, lengths, keys, values),
+        (lengths, keys, values),
         [kv_shape, shape(bias_shape, BF16)],
         [pltpu.VMEM(bias_shape, F32)],
-        first=SMEM,
+        dots=20,
     )
     other = lax.ppermute(here, "tp", [(d, d ^ 1) for d in range(lax.axis_size("tp"))])
-    late = 2
-    early = groups - late
+    fetch = [pltpu.VMEM((half, 2, rows, width), BF16), pltpu.SemaphoreType.DMA(())]
     stash = call(
         functools.partial(early_query_kernel, scaling),
-        (where, bias, here, other, kv, qd),
-        shape((4 + early + 4 * late, rows, width), BF16),
+        (bias, here, kv, qd),
+        shape((4 + 3 * half, rows, width), BF16),
+        fetch,
+        last=HBM,
         dots=1,
-        first=SMEM,
-    )
-    cross, own = pl.pallas_call(
+    )
+    cross, own, late_qd = call(
         functools.partial(key_side_kernel, scaling),
-        grid=(1,),
-        in_specs=[
-            pl.BlockSpec(bias.shape, lambda i: (0, 0)),
-            pl.BlockSpec(qd_group.shape, lambda i: (0, 0, 0, 0)),
-            pl.BlockSpec((4, rows, width), lambda i: (0, 0, 0)),
-        ],
-        out_specs=[pl.BlockSpec((2, rows, width), lambda i: (0, 0, 0))] * 2,
-        out_shape=[shape((2, rows, width), BF16), shape((2, rows, width), F32)],
-        scratch_shapes=[
+        (bias, qd_group, stash, other, qd),
+        [shape((2, rows, width), BF16), shape((2, rows, width), F32), shape((half, 2, rows, width), BF16)],
+        [
             pltpu.VMEM((2, rows, pairs * rows), BF16),
             pltpu.VMEM((2, rows // 2, pairs * rows // 2), BF16),
             pltpu.VMEM((2, rows // 2, pairs * rows // 2), BF16),
+            pltpu.SemaphoreType.DMA(()),
         ],
-        compiler_params=params(),
-        cost_estimate=pl.CostEstimate(flops=4 * flops, bytes_accessed=2**21, transcendentals=0),
-        name="key_side_kernel",
-    )(bias, qd_group, stash)
+        last=HBM,
+        dots=4,
+    )
     back = shifted(cross, "seq", -1)
-    grad_queries = pl.pallas_call(
+    grad_queries = call(
         functools.partial(late_query_kernel, scaling),
-        grid=(1,),
-        in_specs=[
-            pl.BlockSpec(bias.shape, lambda i: (0, 0)),
-            pl.BlockSpec(stash.shape, lambda i: (0, 0, 0)),
-            pl.BlockSpec((late, 2, rows, width), lambda i: (groups // late - 1, 0, 0, 0)),
+        (bias, other, stash, late_qd),
+        shape((rows, groups, width), BF16),
+        [
+            pltpu.VMEM((groups, rows, width), BF16),
+            pltpu.VMEM((rows, groups, width), BF16),
+            pltpu.SemaphoreType.DMA((4,)),
         ],
-        out_specs=pl.BlockSpec((rows, groups, width), lambda i: (0, 0, 0)),
-        out_shape=shape((rows, groups, width), BF16),
-        scratch_shapes=[pltpu.VMEM((groups, rows, width), BF16)],
-        compiler_params=params(),
-        cost_estimate=pl.CostEstimate(flops=3 * flops, bytes_accessed=2**20, transcendentals=0),
-        name="late_query_kernel",
-    )(bias, stash, qd)
+        out=HBM,
+        dots=3,
+    )
     grad_keys, grad_values = call(finish_kernel, (own, back), [shape((rows, width), BF16)] * 2)
     return (
         grad_queries.reshape(queries.shape),

time: 44.8 us -> 45.1 us (level)
  starting transfers between devices: 14.1 us -> 17.4 us
  local copies, waits for them, and re-layouts: 0.02 us -> 2.23 us
  waiting for transfers between devices: 15.4 us -> 13.2 us
  Pallas kernels: 12.8 us -> 11 us
  other arithmetic: 1.52 us -> 0.05 us
    ppermute x2, starting transfers between devices: 7.74 us -> 11.1 us  [shifted(): return lax.ppermute(block, axis, route)]
    pallas_call x6, Pallas kernels: 12.8 us -> 11 us  [call(): pl.pallas_call(kernel, in_specs=[VMEM] * (len(operands) - 1) + [last], ou...]
    dynamic_slice x0 -> x1, local copies, waits for them, and re-layouts: none -> 1.48 us  [per_device(): lax.dynamic_slice(block, (0, (device & 1) * half, 0), (rows, half, width))]
    transpose x1, other arithmetic: 1.45 us -> 0.05 us  [per_device(): half_kv = jnp.swapaxes(jnp.concatenate(half_kv, axis=1), 0, 1)]
    ppermute x2, waiting for transfers between devices: 14.5 us -> 13.2 us  [shifted(): return lax.ppermute(block, axis, route)]
    ppermute x1, waiting for transfers between devices: 0.85 us -> 0.01 us  [per_device(): lax.ppermute(here, 'tp', [(d, d ^ 1) for d in range(lax.axis_size('tp'))])]
    unnamed x12 -> x14, local copies, waits for them, and re-layouts: 0.02 us -> 0.75 us
  transfers between devices with their start and end apart: 4 -> 4, of which waited for: 3 -> 1; matrix products, arithmetic and copies ran while one was open for 0% -> 0% of each run, Pallas kernels for 21% -> 16%
where the time goes in v5:
time: 45.1 us; the launch traced here: 44.8 us
  starting transfers between devices  17.4 us (39%)
  waiting for transfers between devices  13.2 us (29%)
  Pallas kernels  11 us (24%)
  local copies, waits for them, and re-layouts  2.23 us (5%)
  between operations  0.81 us (2%)
    ppermute x2, waiting for transfers between devices, shifted(): return lax.ppermute(block, axis, route)  13.2 us
    ppermute x2, starting transfers between devices, shifted(): return lax.ppermute(block, axis, route)  11.1 us
    pallas_call x6, Pallas kernels, call(): pl.pallas_call(kernel, in_specs=[VMEM] * (len(operands) - 1) + [last], ou...  11 us
    all_to_all x1, starting transfers between devices, per_device(): qd_group = lax.all_to_all(qd, 'tp', split_axis=0, concat_axis=0, tiled=True)  4.43 us
    ppermute x1, starting transfers between devices, per_device(): lax.ppermute(here, 'tp', [(d, d ^ 1) for d in range(lax.axis_size('tp'))])  1.91 us
    dynamic_slice x1, local copies, waits for them, and re-layouts, per_device(): lax.dynamic_slice(block, (0, (device & 1) * half, 0), (rows, half, width))  1.48 us
  transfers between devices with their start and end apart: 4, of which 1 were waited for; matrix products, arithmetic and copies ran while one was open for 0% of the time, Pallas kernels for 16%

profile of v5, /device:TPU:24, one launch (start us, length us, event | category | flops | bytes accessed | tf_op | source)
XLA Modules:
  0.0 44.8 jit_solution(10464346111907034968)
XLA Ops:
  0.6 1.5 %constant_dynamic-slice_fusion = (bf16[256,4,128]{2,1,0:T(4,128)(2,1)S(1)}, bf16[256,4,128]{2,1,0:T(4,128)(2,1)S(1)}) fusion(bf16[256,8,128]{2,1,0:T(8,128)(2,1)} %value_ref.1, s32[]{:T(128)S(6)} %select_n.4, bf16[256,8,128]{2,1,0:T(8,128)(2,1)} %key_ref.1), kind=kLoop, calls=%fused_computation.1 | loop fusion | bytes 1048580 | tf_op jit(solution)/shard_map/dynamic_slice | solution.py:231
  2.2 0.0 copy-start
  2.2 0.0 copy-start.1
  2.3 4.0 %collective-permute-start = (bf16[8,256,128]{2,1,0:T(8,128)(2,1)S(1)}, bf16[8,256,128]{2,1,0:T(8,128)(2,1)S(1)}, u32[]{:S(2)}, u32[]{:S(2)}) collective-permute-start(bf16[8,256,128]{2,1,0:T(8,128)(2,1)S(1)} %maximum_bitcast_fusion), channel_id=1, source_target_pairs={{0,8},{8,16},{16,24},{24,32},{32,40},{40,48},{48,56},{56,64},{64,7... | collective-permute-start | bytes 1572872 | tf_op jit(solution)/shard_map/ppermute | solution.py:33
  6.3 0.0 copy-start.4
  6.3 0.0 copy-done
  6.3 0.0 copy-done.1
  6.3 0.7 %copy-done.4 = s32[2,8,1]{1,2,0:T(1,128)S(1)} copy-done((s32[2,8,1]{1,2,0:T(1,128)S(1)}, s32[2,8,1]{1,2,0:T(1,128)}, u32[]{:S(2)}) %copy-start.4) | copy-done | bytes 88
  6.9 1.3 %query_prepare_kernel.1.qd_all_ref.qd_here_ref = bf16[8,2,256,128]{3,2,1,0:T(8,128)(2,1)} custom-call(s32[2,8]{1,0:T(2,128)S(1)} %bitcast.13, bf16[256,8,128]{2,1,0:T(8,128)(2,1)S(1)} %bitcast.11, bf16[256,8,128]{2,1,0:T(8,128)(2,1)S(1)} %bitcast.12), custom_call_target="tpu_custom_call" | custom-call | flops 1000000 | bytes 1048576 | tf_op jit(solution)/shard_map/query_prepare_kernel/pallas_call | solution.py:219
  8.3 0.0 copy-start.2
  8.3 0.0 copy-start.3
  8.3 4.4 %all-to-all-start = ((bf16[8,2,256,128]{3,2,1,0:T(8,128)(2,1)}), bf16[8,2,256,128]{3,2,1,0:T(8,128)(2,1)S(1)}, u32[]{:S(2)}, u32[]{:S(2)}) async-start(bf16[8,2,256,128]{3,2,1,0:T(8,128)(2,1)} %query_prepare_kernel.1.qd_all_ref.qd_here_ref), calls=%async_computation | async-start | bytes 2097152 | tf_op jit(solution)/shard_map/all_to_all | solution.py:241
  12.7 0.0 copy-start.5
  12.7 13.2 %collective-permute-done.here_ref = bf16[8,256,128]{2,1,0:T(8,128)(2,1)S(1)} collective-permute-done((bf16[8,256,128]{2,1,0:T(8,128)(2,1)S(1)}, bf16[8,256,128]{2,1,0:T(8,128)(2,1)S(1)}, u32[]{:S(2)}, u32[]{:S(2)}) %collective-permute-start) | collective-permute-done | bytes 524320 | tf_op jit(solution)/shard_map/ppermute | solution.py:33
  25.9 1.9 %collective-permute-start.1 = (bf16[8,256,128]{2,1,0:T(8,128)(2,1)S(1)}, bf16[8,256,128]{2,1,0:T(8,128)(2,1)S(1)}, u32[]{:S(2)}, u32[]{:S(2)}) collective-permute-start(bf16[8,256,128]{2,1,0:T(8,128)(2,1)S(1)} %collective-permute-done.here_ref), channel_id=1, source_target_pairs={{0,1},{1,0},{2,3},{3,2},{4,5},{5,4},{6,7},{7,6},{8,9},{9,8},{10,11... | collective-permute-start | bytes 1572872 | tf_op jit(solution)/shard_map/ppermute | solution.py:251
  27.8 0.0 copy-done.2
  27.8 0.0 copy-done.3
  27.9 0.0 copy-done.5
  27.9 0.4 key_prepare_kernel.1
  28.3 2.9 %early_query_kernel.1.window_ref.stash_ref = bf16[16,256,128]{2,1,0:T(8,128)(2,1)S(1)} custom-call(bf16[384,256]{1,0:T(8,128)(2,1)S(1)} %get-tuple-element.11.bias_ref, bf16[8,256,128]{2,1,0:T(8,128)(2,1)S(1)} %collective-permute-done.here_ref, bf16[2,8,256,128]{3,2,1,0:T(8,128)(2,1)S(1)} %get-tuple-element.12.kv_ref, ...), custom_call_target="tpu_custom_call" | custom-call | flops 269435456 | bytes 1048576 | tf_op jit(solution)/shard_map/early_query_kernel/pallas_call | solution.py:219
  31.2 0.0 all-to-all-done.qd_ref
  31.2 0.0 collective-permute-done.1.other_ref
  31.2 3.0 %key_side_kernel.1 = (bf16[2,256,128]{2,1,0:T(8,128)(2,1)S(1)}, f32[2,256,128]{2,1,0:T(8,128)S(1)}, bf16[4,2,256,128]{3,2,1,0:T(8,128)(2,1)S(1)}) custom-call(bf16[384,256]{1,0:T(8,128)(2,1)S(1)} %get-tuple-element.11.bias_ref, bf16[8,2,256,128]{3,2,1,0:T(8,128)(2,1)S(1)} %all-to-all-done.qd_ref, ...), custom_call_target="tpu_custom_call" | custom-call | flops 1074741760 | bytes 1048576 | tf_op jit(solution)/shard_map/key_side_kernel/pallas_call | solution.py:219
  34.2 7.1 %collective-permute-start.2 = (bf16[2,256,128]{2,1,0:T(8,128)(2,1)S(1)}, bf16[2,256,128]{2,1,0:T(8,128)(2,1)S(1)}, u32[]{:S(2)}, u32[]{:S(2)}) collective-permute-start(bf16[2,256,128]{2,1,0:T(8,128)(2,1)S(1)} %get-tuple-element.16), channel_id=1, source_target_pairs={{8,0},{16,8},{24,16},{32,24},{40,32},{48,40},{56,48},{64,56},{72,6... | collective-permute-start | bytes 393224 | tf_op jit(solution)/shard_map/ppermute | solution.py:33
  41.3 2.7 %late_query_kernel.1 = bf16[256,8,128]{2,1,0:T(8,128)(2,1)} custom-call(bf16[384,256]{1,0:T(8,128)(2,1)S(1)} %get-tuple-element.11.bias_ref, bf16[8,256,128]{2,1,0:T(8,128)(2,1)S(1)} %collective-permute-done.1.other_ref, bf16[16,256,128]{2,1,0:T(8,128)(2,1)S(1)} %early_query_kernel.1.window_ref.stash_ref, bf16[4,2,256,128]{3,2,1,0:T(8,128)(2,1)S(1)} %get-tuple-element.14.qd_ref), custom_call_target="tpu_custom_call" | custom-call | flops 806306368 | bytes 1048576 | tf_op jit(solution)/shard_map/late_query_kernel/pallas_call | solution.py:219
  44.1 0.0 collective-permute-done.2.back_ref
  44.1 0.7 %finish_kernel.1 = (bf16[256,128]{1,0:T(8,128)(2,1)}, bf16[256,128]{1,0:T(8,128)(2,1)}) custom-call(f32[2,256,128]{2,1,0:T(8,128)S(1)} %get-tuple-element.15.own_ref, bf16[2,256,128]{2,1,0:T(8,128)(2,1)S(1)} %collective-permute-done.2.back_ref), custom_call_target="tpu_custom_call" | custom-call | flops 1000000 | bytes 1048576 | tf_op jit(solution)/shard_map/finish_kernel/pallas_call | solution.py:219
  (3 shorter events, 0.1 us)
Async XLA Ops:
  2.2 4.1 %copy-start = (bf16[256,8,1,128]{3,1,2,0:T(8,128)(2,1)S(1)}, bf16[256,8,1,128]{3,1,2,0:T(8,128)(2,1)}, u32[]{:S(2)}) copy-start(bf16[256,8,1,128]{3,1,2,0:T(8,128)(2,1)} %param.6) | copy-start | bytes 1572868
  2.2 4.1 %copy-start.1 = (bf16[256,8,1,128]{3,1,2,0:T(8,128)(2,1)S(1)}, bf16[256,8,1,128]{3,1,2,0:T(8,128)(2,1)}, u32[]{:S(2)}) copy-start(bf16[256,8,1,128]{3,1,2,0:T(8,128)(2,1)} %param.9) | copy-start | bytes 1572868
  2.3 23.6 %collective-permute-start = (bf16[8,256,128]{2,1,0:T(8,128)(2,1)S(1)}, bf16[8,256,128]{2,1,0:T(8,128)(2,1)S(1)}, u32[]{:S(2)}, u32[]{:S(2)}) collective-permute-start(bf16[8,256,128]{2,1,0:T(8,128)(2,1)S(1)} %maximum_bitcast_fusion), channel_id=1, source_target_pairs={{0,8},{8,16},{16,24},{24,32},{32,40},{40,48},{48,56},{56,64},{64,7... | collective-permute-start | bytes 1572872 | tf_op jit(solution)/shard_map/ppermute | solution.py:33
  6.3 0.7 %copy-start.4 = (s32[2,8,1]{1,2,0:T(1,128)S(1)}, s32[2,8,1]{1,2,0:T(1,128)}, u32[]{:S(2)}) copy-start(s32[2,8,1]{1,2,0:T(1,128)} %param.10) | copy-start | bytes 196
  8.3 19.6 %copy-start.2 = (bf16[256,8,128]{2,1,0:T(8,128)(2,1)S(1)}, bf16[256,8,128]{2,1,0:T(8,128)(2,1)}, u32[]{:S(2)}) copy-start(bf16[256,8,128]{2,1,0:T(8,128)(2,1)} %key_ref.1) | copy-start | bytes 1572868
  8.3 19.6 %copy-start.3 = (bf16[256,8,128]{2,1,0:T(8,128)(2,1)S(1)}, bf16[256,8,128]{2,1,0:T(8,128)(2,1)}, u32[]{:S(2)}) copy-start(bf16[256,8,128]{2,1,0:T(8,128)(2,1)} %value_ref.1) | copy-start | bytes 1572868
  8.3 22.9 %all-to-all-start = ((bf16[8,2,256,128]{3,2,1,0:T(8,128)(2,1)}), bf16[8,2,256,128]{3,2,1,0:T(8,128)(2,1)S(1)}, u32[]{:S(2)}, u32[]{:S(2)}) async-start(bf16[8,2,256,128]{3,2,1,0:T(8,128)(2,1)} %query_prepare_kernel.1.qd_all_ref.qd_here_ref), calls=%async_computation | async-start | bytes 2097152 | tf_op jit(solution)/shard_map/all_to_all | solution.py:241
  12.7 15.2 %copy-start.5 = (s32[128]{0:T(128)S(1)}, s32[128]{0:T(128)}, u32[]{:S(2)}) copy-start(s32[128]{0:T(128)} %param.11) | copy-start | bytes 1540
  25.9 5.3 %collective-permute-start.1 = (bf16[8,256,128]{2,1,0:T(8,128)(2,1)S(1)}, bf16[8,256,128]{2,1,0:T(8,128)(2,1)S(1)}, u32[]{:S(2)}, u32[]{:S(2)}) collective-permute-start(bf16[8,256,128]{2,1,0:T(8,128)(2,1)S(1)} %collective-permute-done.here_ref), channel_id=1, source_target_pairs={{0,1},{1,0},{2,3},{3,2},{4,5},{5,4},{6,7},{7,6},{8,9},{9,8},{10,11... | collective-permute-start | bytes 1572872 | tf_op jit(solution)/shard_map/ppermute | solution.py:251
  34.2 9.9 %collective-permute-start.2 = (bf16[2,256,128]{2,1,0:T(8,128)(2,1)S(1)}, bf16[2,256,128]{2,1,0:T(8,128)(2,1)S(1)}, u32[]{:S(2)}, u32[]{:S(2)}) collective-permute-start(bf16[2,256,128]{2,1,0:T(8,128)(2,1)S(1)} %get-tuple-element.16), channel_id=1, source_target_pairs={{8,0},{16,8},{24,16},{32,24},{40,32},{48,40},{56,48},{64,56},{72,6... | collective-permute-start | bytes 393224 | tf_op jit(solution)/shard_map/ppermute | solution.py:33

commit v6 on v5

--- a/solution.py
+++ b/solution.py
@@ -112,22 +112,17 @@
     return (total * scaling).astype(BF16).T
 
 
-def early_query_kernel(scaling, bias_ref, here_ref, kv_ref, qd_all_ref, stash_ref, qd_ref, done):
-    d = lax.axis_index("tp")
+def early_query_kernel(scaling, bias_ref, here_ref, kv_ref, qd_all_ref, out_ref, next_ref, qd_ref, done):
     half = here_ref.shape[0] // 2
-    first = (d & 1) * half
-    late = half - first
-    fetch = pltpu.make_async_copy(qd_all_ref.at[pl.ds(first, half)], qd_ref, done)
+    first = (lax.axis_index("tp") & 1) * half
+    fetch = pltpu.make_async_copy(qd_all_ref.at[pl.ds(first, half)], qd_ref, done.at[0])
     fetch.start()
+    fetch_next = pltpu.make_async_copy(qd_all_ref.at[pl.ds(half - first, next_ref.shape[0])], next_ref, done.at[1])
+    fetch_next.start()
     bias = bias_ref[...].astype(F32)
-    for i in range(2):
-        stash_ref[2 * i] = here_ref[half * i + (d & (half - 1))]
-        stash_ref[2 * i + 1] = kv_ref[i, d]
-        for y in range(half):
-            stash_ref[4 + half + 2 * y + i] = kv_ref[i, late + y]
     fetch.wait()
     for y in range(half):
-        stash_ref[4 + y] = query_grads(
+        out_ref[y] = query_grads(
             scaling,
             qd_ref[y, 0],
             qd_ref[y, 1],
@@ -135,26 +130,53 @@
             jnp.concatenate([here_ref[half + y], kv_ref[1, first + y]], axis=0),
             bias,
         )
-
-
-def late_query_kernel(scaling, bias_ref, other_ref, stash_ref, qd_ref, out_ref, grads, swapped, done):
-    half = other_ref.shape[0] // 2
+    fetch_next.wait()
+
+
+def middle_query_kernel(scaling, bias_ref, here_ref, other_ref, kv_ref, early_ref, qd_ref, stash_ref):
+    d = lax.axis_index("tp")
+    half = here_ref.shape[0] // 2
+    count = qd_ref.shape[0]
+    late = half - (d & 1) * half
+    bias = bias_ref[...].astype(F32)
+    for i in range(2):
+        at = half * i + (d & (half - 1))
+        stash_ref[3 * i] = here_ref[at]
+        stash_ref[3 * i + 1] = other_ref[at]
+        stash_ref[3 * i + 2] = kv_ref[i, d]
+        for y in range(count, half):
+            at = 6 + half + count + 4 * (y - count) + 2 * i
+            stash_ref[at] = other_ref[half * i + y]
+            stash_ref[at + 1] = kv_ref[i, late + y]
+    stash_ref[6 : 6 + half] = early_ref[...]
+    for y in range(count):
+        stash_ref[6 + half + y] = query_grads(
+            scaling,
+            qd_ref[y, 0],
+            qd_ref[y, 1],
+            jnp.concatenate([other_ref[y], kv_ref[0, late + y]], axis=0),
+            jnp.concatenate([other_ref[half + y], kv_ref[1, late + y]], axis=0),
+            bias,
+        )
+
+
+def late_query_kernel(scaling, bias_ref, stash_ref, qd_ref, out_ref, grads, swapped, done):
+    groups, window, _ = grads.shape
+    half, left = groups // 2, qd_ref.shape[0]
     first = (lax.axis_index("tp") & 1) * half
     late = half - first
     bias = bias_ref[...].astype(F32)
     for y in range(half):
-        grads[first + y] = stash_ref[4 + y]
-        at = 4 + half + 2 * y
-        grads[late + y] = query_grads(
-            scaling,
-            qd_ref[y, 0],
-            qd_ref[y, 1],
-            jnp.concatenate([other_ref[y], stash_ref[at]], axis=0),
-            jnp.concatenate([other_ref[half + y], stash_ref[at + 1]], axis=0),
-            bias,
-        )
+        grads[first + y] = stash_ref[6 + y]
+    for y in range(half - left):
+        grads[late + y] = stash_ref[6 + half + y]
+    for i in range(left):
+        at = 6 + groups - left + 4 * i
+        key = stash_ref[at : at + 2].reshape(2 * window, -1)
+        value = stash_ref[at + 2 : at + 4].reshape(2 * window, -1)
+        grads[late + half - left + i] = query_grads(scaling, qd_ref[i, 0], qd_ref[i, 1], key, value, bias)
     chunks = done.shape[0]
-    rows = swapped.shape[0] // chunks
+    rows = window // chunks
     copies = []
     for i in range(chunks):
         part = pl.ds(i * rows, rows)
@@ -166,18 +188,20 @@
 
 
 def key_side_kernel(
-    scaling, bias_ref, qd_ref, window_ref, other_ref, qd_here_ref, cross_ref, own_ref, late_ref, mid_terms, left_terms, right_terms, done
+    scaling, bias_ref, qd_ref, stash_ref, qd_here_ref, cross_ref, own_ref, late_ref, mid_terms, left_terms, right_terms, done
 ):
     heads, _, rows, width = qd_ref.shape
     half = rows // 2
+    left = late_ref.shape[0]
+    first = (heads // 2) * (1 - (lax.axis_index("tp") & 1)) + heads // 2 - left
+    fetch = pltpu.make_async_copy(qd_here_ref.at[pl.ds(first, left)], late_ref, done)
+    fetch.start()
     d = lax.axis_index("tp")
-    count = other_ref.shape[0] // 2
-    fetch = pltpu.make_async_copy(qd_here_ref.at[pl.ds((1 - (d & 1)) * count, count)], late_ref, done)
-    fetch.start()
-    came_here = (d >= count) == ((d & 1) == 1)
-    back = [jnp.where(came_here, window_ref[2 * i], other_ref[count * i + (d & (count - 1))]) for i in range(2)]
-    key = jnp.concatenate([back[0], window_ref[1]], axis=0)
-    value = jnp.concatenate([back[1], window_ref[3]], axis=0)
+    came_here = (d >= heads // 2) == ((d & 1) == 1)
+    key, value = (
+        jnp.concatenate([jnp.where(came_here, stash_ref[at], stash_ref[at + 1]), stash_ref[at + 2]], axis=0)
+        for at in (0, 3)
+    )
     bias = bias_ref[...].astype(F32)
     for h in range(heads):
         probs, probs_c, grads, grads_c = pair_terms(qd_ref[h, 0], qd_ref[h, 1], key, value, bias, scaling)
@@ -249,19 +273,25 @@
         dots=20,
     )
     other = lax.ppermute(here, "tp", [(d, d ^ 1) for d in range(lax.axis_size("tp"))])
-    fetch = [pltpu.VMEM((half, 2, rows, width), BF16), pltpu.SemaphoreType.DMA(())]
-    stash = call(
+    middle = 2
+    early, next_qd = call(
         functools.partial(early_query_kernel, scaling),
         (bias, here, kv, qd),
-        shape((4 + 3 * half, rows, width), BF16),
-        fetch,
+        [shape((half, rows, width), BF16), shape((middle, 2, rows, width), BF16)],
+        [pltpu.VMEM((half, 2, rows, width), BF16), pltpu.SemaphoreType.DMA((2,))],
         last=HBM,
         dots=1,
     )
+    stash = call(
+        functools.partial(middle_query_kernel, scaling),
+        (bias, here, other, kv, early, next_qd),
+        shape((6 + half + middle + 4 * (half - middle), rows, width), BF16),
+        dots=1,
+    )
     cross, own, late_qd = call(
         functools.partial(key_side_kernel, scaling),
-        (bias, qd_group, stash, other, qd),
-        [shape((2, rows, width), BF16), shape((2, rows, width), F32), shape((half, 2, rows, width), BF16)],
+        (bias, qd_group, stash, qd),
+        [shape((2, rows, width), BF16), shape((2, rows, width), F32), shape((half - middle, 2, rows, width), BF16)],
         [
             pltpu.VMEM((2, rows, pairs * rows), BF16),
             pltpu.VMEM((2, rows // 2, pairs * rows // 2), BF16),
@@ -274,7 +304,7 @@
     back = shifted(cross, "seq", -1)
     grad_queries = call(
         functools.partial(late_query_kernel, scaling),
-        (bias, other, stash, late_qd),
+        (bias, stash, late_qd),
         shape((rows, groups, width), BF16),
         [
             pltpu.VMEM((groups, rows, width), BF16),

time: 45.1 us -> 44.2 us (0.980)
  starting transfers between devices: 17.4 us -> 15.7 us
  waiting for transfers between devices: 13.2 us -> 14.4 us
  local copies, waits for them, and re-layouts: 2.23 us -> 1.58 us
    ppermute x2, starting transfers between devices: 11.1 us -> 9.31 us  [shifted(): return lax.ppermute(block, axis, route)]
    ppermute x2, waiting for transfers between devices: 13.2 us -> 14.4 us  [shifted(): return lax.ppermute(block, axis, route)]
    unnamed x14, local copies, waits for them, and re-layouts: 0.75 us -> 0.1 us
    pallas_call x6 -> x7, Pallas kernels: 11 us -> 11.4 us  [call(): pl.pallas_call(kernel, in_specs=[VMEM] * (len(operands) - 1) + [last], ou...]
  transfers between devices with their start and end apart: 4 -> 4, of which waited for: 1 -> 2; matrix products, arithmetic and copies ran while one was open for 0% -> 0% of each run, Pallas kernels for 16% -> 18%
where the time goes in v6:
time: 44.2 us; the launch traced here: 43.9 us
  starting transfers between devices  15.7 us (36%)
  waiting for transfers between devices  14.4 us (33%)
  Pallas kernels  11.4 us (26%)
  local copies, waits for them, and re-layouts  1.58 us (4%)
  between operations  0.81 us (2%)
    ppermute x2, waiting for transfers between devices, shifted(): return lax.ppermute(block, axis, route)  14.4 us
    pallas_call x7, Pallas kernels, call(): pl.pallas_call(kernel, in_specs=[VMEM] * (len(operands) - 1) + [last], ou...  11.4 us
    ppermute x2, starting transfers between devices, shifted(): return lax.ppermute(block, axis, route)  9.31 us
    all_to_all x1, starting transfers between devices, per_device(): qd_group = lax.all_to_all(qd, 'tp', split_axis=0, concat_axis=0, tiled=True)  4.43 us
    ppermute x1, starting transfers between devices, per_device(): lax.ppermute(here, 'tp', [(d, d ^ 1) for d in range(lax.axis_size('tp'))])  1.91 us
    dynamic_slice x1, local copies, waits for them, and re-layouts, per_device(): lax.dynamic_slice(block, (0, (device & 1) * half, 0), (rows, half, width))  1.48 us
  transfers between devices with their start and end apart: 4, of which 2 were waited for; matrix products, arithmetic and copies ran while one was open for 0% of the time, Pallas kernels for 18%

profile of v6, /device:TPU:24, one launch (start us, length us, event | category | flops | bytes accessed | tf_op | source)
XLA Modules:
  0.0 43.9 jit_solution(4506202760794603797)
XLA Ops:
  0.6 1.5 %constant_dynamic-slice_fusion = (bf16[256,4,128]{2,1,0:T(4,128)(2,1)S(1)}, bf16[256,4,128]{2,1,0:T(4,128)(2,1)S(1)}) fusion(bf16[256,8,128]{2,1,0:T(8,128)(2,1)} %value_ref.1, s32[]{:T(128)S(6)} %select_n.4, bf16[256,8,128]{2,1,0:T(8,128)(2,1)} %key_ref.1), kind=kLoop, calls=%fused_computation.1 | loop fusion | bytes 1048580 | tf_op jit(solution)/shard_map/dynamic_slice | solution.py:255
  2.1 0.0 copy-start
  2.1 0.0 copy-start.1
  2.1 0.0 copy-start.4
  2.3 4.0 %collective-permute-start = (bf16[8,256,128]{2,1,0:T(8,128)(2,1)S(1)}, bf16[8,256,128]{2,1,0:T(8,128)(2,1)S(1)}, u32[]{:S(2)}, u32[]{:S(2)}) collective-permute-start(bf16[8,256,128]{2,1,0:T(8,128)(2,1)S(1)} %maximum_bitcast_fusion), channel_id=1, source_target_pairs={{0,8},{8,16},{16,24},{24,32},{32,40},{40,48},{48,56},{56,64},{64,7... | collective-permute-start | bytes 1572872 | tf_op jit(solution)/shard_map/ppermute | solution.py:33
  6.3 0.0 copy-done
  6.3 0.0 copy-done.1
  6.3 0.0 copy-done.4
  6.3 1.3 %query_prepare_kernel.1.qd_all_ref.qd_here_ref = bf16[8,2,256,128]{3,2,1,0:T(8,128)(2,1)} custom-call(s32[2,8]{1,0:T(2,128)S(1)} %bitcast.13, bf16[256,8,128]{2,1,0:T(8,128)(2,1)S(1)} %bitcast.11, bf16[256,8,128]{2,1,0:T(8,128)(2,1)S(1)} %bitcast.12), custom_call_target="tpu_custom_call" | custom-call | flops 1000000 | bytes 1048576 | tf_op jit(solution)/shard_map/query_prepare_kernel/pallas_call | solution.py:243
  7.6 0.0 copy-start.2
  7.6 0.0 copy-start.3
  7.6 0.0 copy-start.5
  7.6 4.4 %all-to-all-start = ((bf16[8,2,256,128]{3,2,1,0:T(8,128)(2,1)}), bf16[8,2,256,128]{3,2,1,0:T(8,128)(2,1)S(1)}, u32[]{:S(2)}, u32[]{:S(2)}) async-start(bf16[8,2,256,128]{3,2,1,0:T(8,128)(2,1)} %query_prepare_kernel.1.qd_all_ref.qd_here_ref), calls=%async_computation | async-start | bytes 2097152 | tf_op jit(solution)/shard_map/all_to_all | solution.py:265
  12.1 13.9 %collective-permute-done.here_ref = bf16[8,256,128]{2,1,0:T(8,128)(2,1)S(1)} collective-permute-done((bf16[8,256,128]{2,1,0:T(8,128)(2,1)S(1)}, bf16[8,256,128]{2,1,0:T(8,128)(2,1)S(1)}, u32[]{:S(2)}, u32[]{:S(2)}) %collective-permute-start) | collective-permute-done | bytes 524320 | tf_op jit(solution)/shard_map/ppermute | solution.py:33
  25.9 1.9 %collective-permute-start.1 = (bf16[8,256,128]{2,1,0:T(8,128)(2,1)S(1)}, bf16[8,256,128]{2,1,0:T(8,128)(2,1)S(1)}, u32[]{:S(2)}, u32[]{:S(2)}) collective-permute-start(bf16[8,256,128]{2,1,0:T(8,128)(2,1)S(1)} %collective-permute-done.here_ref), channel_id=1, source_target_pairs={{0,1},{1,0},{2,3},{3,2},{4,5},{5,4},{6,7},{7,6},{8,9},{9,8},{10,11... | collective-permute-start | bytes 1572872 | tf_op jit(solution)/shard_map/ppermute | solution.py:275
  27.8 0.0 copy-done.2
  27.9 0.0 copy-done.3
  27.9 0.0 copy-done.5
  27.9 0.4 key_prepare_kernel.1
  28.3 2.9 %early_query_kernel.1 = (bf16[4,256,128]{2,1,0:T(8,128)(2,1)S(1)}, bf16[2,2,256,128]{3,2,1,0:T(8,128)(2,1)S(1)}) custom-call(bf16[384,256]{1,0:T(8,128)(2,1)S(1)} %get-tuple-element.13.bias_ref, bf16[8,256,128]{2,1,0:T(8,128)(2,1)S(1)} %collective-permute-done.here_ref, bf16[2,8,256,128]{3,2,1,0:T(8,128)(2,1)S(1)} %get-tuple-element.14.kv_ref, ...), custom_call_target="tpu_custom_call" | custom-call | flops 269435456 | bytes 1048576 | tf_op jit(solution)/shard_map/early_query_kernel/pallas_call | solution.py:243
  31.2 0.0 collective-permute-done.1.other_ref
  31.2 1.1 %middle_query_kernel.1.stash_ref = bf16[20,256,128]{2,1,0:T(8,128)(2,1)S(1)} custom-call(bf16[384,256]{1,0:T(8,128)(2,1)S(1)} %get-tuple-element.13.bias_ref, bf16[8,256,128]{2,1,0:T(8,128)(2,1)S(1)} %collective-permute-done.here_ref, bf16[8,256,128]{2,1,0:T(8,128)(2,1)S(1)} %collective-permute-done.1.other_ref, ...), custom_call_target="tpu_custom_call" | custom-call | flops 269435456 | bytes 1048576 | tf_op jit(solution)/shard_map/middle_query_kernel/pallas_call | solution.py:243
  32.3 0.0 all-to-all-done.qd_ref
  32.3 3.0 %key_side_kernel.1 = (bf16[2,256,128]{2,1,0:T(8,128)(2,1)S(1)}, f32[2,256,128]{2,1,0:T(8,128)S(1)}, bf16[2,2,256,128]{3,2,1,0:T(8,128)(2,1)S(1)}) custom-call(bf16[384,256]{1,0:T(8,128)(2,1)S(1)} %get-tuple-element.13.bias_ref, bf16[8,2,256,128]{3,2,1,0:T(8,128)(2,1)S(1)} %all-to-all-done.qd_ref, bf16[20,256,128]{2,1,0:T(8,128)(2,1)S(1)} %middle_query_kernel.1.stash_ref, ...), custom_call_target="tpu_custom_call" | custom-call | flops 1074741760 | bytes 1048576 | tf_op jit(solution)/shard_map/key_side_kernel/pallas_call | solution.py:243
  35.3 5.4 %collective-permute-start.2 = (bf16[2,256,128]{2,1,0:T(8,128)(2,1)S(1)}, bf16[2,256,128]{2,1,0:T(8,128)(2,1)S(1)}, u32[]{:S(2)}, u32[]{:S(2)}) collective-permute-start(bf16[2,256,128]{2,1,0:T(8,128)(2,1)S(1)} %get-tuple-element.20), channel_id=1, source_target_pairs={{8,0},{16,8},{24,16},{32,24},{40,32},{48,40},{56,48},{64,56},{72,6... | collective-permute-start | bytes 393224 | tf_op jit(solution)/shard_map/ppermute | solution.py:33
  40.7 2.0 %late_query_kernel.1 = bf16[256,8,128]{2,1,0:T(8,128)(2,1)} custom-call(bf16[384,256]{1,0:T(8,128)(2,1)S(1)} %get-tuple-element.13.bias_ref, bf16[20,256,128]{2,1,0:T(8,128)(2,1)S(1)} %middle_query_kernel.1.stash_ref, bf16[2,2,256,128]{3,2,1,0:T(8,128)(2,1)S(1)} %get-tuple-element.18.qd_ref), custom_call_target="tpu_custom_call" | custom-call | flops 806306368 | bytes 1048576 | tf_op jit(solution)/shard_map/late_query_kernel/pallas_call | solution.py:243
  42.7 0.5 %collective-permute-done.2.back_ref = bf16[2,256,128]{2,1,0:T(8,128)(2,1)S(1)} collective-permute-done((bf16[2,256,128]{2,1,0:T(8,128)(2,1)S(1)}, bf16[2,256,128]{2,1,0:T(8,128)(2,1)S(1)}, u32[]{:S(2)}, u32[]{:S(2)}) %collective-permute-start.2) | collective-permute-done | bytes 131104 | tf_op jit(solution)/shard_map/ppermute | solution.py:33
  43.2 0.7 %finish_kernel.1 = (bf16[256,128]{1,0:T(8,128)(2,1)}, bf16[256,128]{1,0:T(8,128)(2,1)}) custom-call(f32[2,256,128]{2,1,0:T(8,128)S(1)} %get-tuple-element.19.own_ref, bf16[2,256,128]{2,1,0:T(8,128)(2,1)S(1)} %collective-permute-done.2.back_ref), custom_call_target="tpu_custom_call" | custom-call | flops 1000000 | bytes 1048576 | tf_op jit(solution)/shard_map/finish_kernel/pallas_call | solution.py:243
  (3 shorter events, 0.1 us)
Async XLA Ops:
  2.1 4.2 %copy-start = (bf16[256,8,1,128]{3,1,2,0:T(8,128)(2,1)S(1)}, bf16[256,8,1,128]{3,1,2,0:T(8,128)(2,1)}, u32[]{:S(2)}) copy-start(bf16[256,8,1,128]{3,1,2,0:T(8,128)(2,1)} %param.6) | copy-start | bytes 1572868
  2.1 4.1 %copy-start.1 = (bf16[256,8,1,128]{3,1,2,0:T(8,128)(2,1)S(1)}, bf16[256,8,1,128]{3,1,2,0:T(8,128)(2,1)}, u32[]{:S(2)}) copy-start(bf16[256,8,1,128]{3,1,2,0:T(8,128)(2,1)} %param.9) | copy-start | bytes 1572868
  2.1 4.1 %copy-start.4 = (s32[2,8,1]{1,2,0:T(1,128)S(1)}, s32[2,8,1]{1,2,0:T(1,128)}, u32[]{:S(2)}) copy-start(s32[2,8,1]{1,2,0:T(1,128)} %param.10) | copy-start | bytes 196
  2.3 23.6 %collective-permute-start = (bf16[8,256,128]{2,1,0:T(8,128)(2,1)S(1)}, bf16[8,256,128]{2,1,0:T(8,128)(2,1)S(1)}, u32[]{:S(2)}, u32[]{:S(2)}) collective-permute-start(bf16[8,256,128]{2,1,0:T(8,128)(2,1)S(1)} %maximum_bitcast_fusion), channel_id=1, source_target_pairs={{0,8},{8,16},{16,24},{24,32},{32,40},{40,48},{48,56},{56,64},{64,7... | collective-permute-start | bytes 1572872 | tf_op jit(solution)/shard_map/ppermute | solution.py:33
  7.6 20.2 %copy-start.2 = (bf16[256,8,128]{2,1,0:T(8,128)(2,1)S(1)}, bf16[256,8,128]{2,1,0:T(8,128)(2,1)}, u32[]{:S(2)}) copy-start(bf16[256,8,128]{2,1,0:T(8,128)(2,1)} %key_ref.1) | copy-start | bytes 1572868
  7.6 20.2 %copy-start.3 = (bf16[256,8,128]{2,1,0:T(8,128)(2,1)S(1)}, bf16[256,8,128]{2,1,0:T(8,128)(2,1)}, u32[]{:S(2)}) copy-start(bf16[256,8,128]{2,1,0:T(8,128)(2,1)} %value_ref.1) | copy-start | bytes 1572868
  7.6 20.2 %copy-start.5 = (s32[128]{0:T(128)S(1)}, s32[128]{0:T(128)}, u32[]{:S(2)}) copy-start(s32[128]{0:T(128)} %param.11) | copy-start | bytes 1540
  7.6 24.7 %all-to-all-start = ((bf16[8,2,256,128]{3,2,1,0:T(8,128)(2,1)}), bf16[8,2,256,128]{3,2,1,0:T(8,128)(2,1)S(1)}, u32[]{:S(2)}, u32[]{:S(2)}) async-start(bf16[8,2,256,128]{3,2,1,0:T(8,128)(2,1)} %query_prepare_kernel.1.qd_all_ref.qd_here_ref), calls=%async_computation | async-start | bytes 2097152 | tf_op jit(solution)/shard_map/all_to_all | solution.py:265
  25.9 5.3 %collective-permute-start.1 = (bf16[8,256,128]{2,1,0:T(8,128)(2,1)S(1)}, bf16[8,256,128]{2,1,0:T(8,128)(2,1)S(1)}, u32[]{:S(2)}, u32[]{:S(2)}) collective-permute-start(bf16[8,256,128]{2,1,0:T(8,128)(2,1)S(1)} %collective-permute-done.here_ref), channel_id=1, source_target_pairs={{0,1},{1,0},{2,3},{3,2},{4,5},{5,4},{6,7},{7,6},{8,9},{9,8},{10,11... | collective-permute-start | bytes 1572872 | tf_op jit(solution)/shard_map/ppermute | solution.py:275
  35.3 7.9 %collective-permute-start.2 = (bf16[2,256,128]{2,1,0:T(8,128)(2,1)S(1)}, bf16[2,256,128]{2,1,0:T(8,128)(2,1)S(1)}, u32[]{:S(2)}, u32[]{:S(2)}) collective-permute-start(bf16[2,256,128]{2,1,0:T(8,128)(2,1)S(1)} %get-tuple-element.20), channel_id=1, source_target_pairs={{8,0},{16,8},{24,16},{32,24},{40,32},{48,40},{56,48},{64,56},{72,6... | collective-permute-start | bytes 393224 | tf_op jit(solution)/shard_map/ppermute | solution.py:33

commit v7 on v6

--- a/solution.py
+++ b/solution.py
@@ -59,7 +59,7 @@
     return middle, corners
 
 
-def pair_terms(query, dout, key, value, bias, scaling):
+def shifted_exps(query, key, bias, scaling):
     rows = query.shape[0]
     fold = scaling * math.log2(math.e)
     middle, corners = window_dots(key, query)
@@ -68,7 +68,12 @@
     row_max = jnp.maximum(jnp.max(middle, axis=0, keepdims=True), jnp.max(corners, axis=0, keepdims=True))
     middle = jnp.exp2(middle - row_max)
     corners = jnp.exp2(corners - row_max)
-    inverse = 1.0 / (jnp.sum(middle, axis=0, keepdims=True) + jnp.sum(corners, axis=0, keepdims=True))
+    total = jnp.sum(middle, axis=0, keepdims=True) + jnp.sum(corners, axis=0, keepdims=True)
+    return middle, corners, 1.0 / total
+
+
+def pair_terms(query, dout, key, value, bias, scaling):
+    middle, corners, inverse = shifted_exps(query, key, bias, scaling)
     middle = middle * inverse
     corners = corners * inverse
     grad_middle, grad_corners = window_dots(value, dout)
@@ -93,34 +98,41 @@
         qd_ref[:, 1, part] = jnp.swapaxes(grad_ref[part], 0, 1) * factor[b][:, None, None]
 
 
-def key_prepare_kernel(lengths_ref, key_ref, value_ref, kv_ref, bias_ref, bias):
+def key_prepare_kernel(lengths_ref, key_ref, value_ref, qd_ref, kv_ref, bias_ref, half_ref, bias, done):
+    half = half_ref.shape[0]
+    fetch = pltpu.make_async_copy(qd_ref.at[pl.ds((lax.axis_index("tp") & 1) * half, half)], half_ref, done)
+    fetch.start()
     fill_bias(bias, lengths_ref, lax.axis_index("seq") * bias.shape[1])
     bias_ref[...] = bias[...].astype(BF16)
     kv_ref[0] = jnp.swapaxes(key_ref[...], 0, 1)
     kv_ref[1] = jnp.swapaxes(value_ref[...], 0, 1)
+    fetch.wait()
 
 
 def query_grads(scaling, query, dout, key, value, bias):
     rows = query.shape[0]
     half = rows // 2
-    _, _, middle, corners = pair_terms(query, dout, key, value, bias, scaling)
+    middle, corners, inverse = shifted_exps(query, key, bias, scaling)
+    grad_middle, grad_corners = window_dots(value, dout)
+    row_delta = inverse * (
+        jnp.sum(middle * grad_middle, axis=0, keepdims=True) + jnp.sum(corners * grad_corners, axis=0, keepdims=True)
+    )
+    middle = (middle * (grad_middle - row_delta)).astype(BF16)
+    corners = (corners * (grad_corners - row_delta)).astype(BF16)
     key_t = key.T
     total = dot_nn(key_t[:, half : half + rows], middle) + jnp.concatenate(
         [dot_nn(key_t[:, :half], corners[:, :half]), dot_nn(key_t[:, half + rows :], corners[:, half:])],
         axis=1,
     )
-    return (total * scaling).astype(BF16).T
-
-
-def early_query_kernel(scaling, bias_ref, here_ref, kv_ref, qd_all_ref, out_ref, next_ref, qd_ref, done):
+    return (total * (inverse * scaling)).astype(BF16).T
+
+
+def early_query_kernel(scaling, bias_ref, here_ref, kv_ref, qd_ref, qd_all_ref, out_ref, next_ref, done):
     half = here_ref.shape[0] // 2
     first = (lax.axis_index("tp") & 1) * half
-    fetch = pltpu.make_async_copy(qd_all_ref.at[pl.ds(first, half)], qd_ref, done.at[0])
+    fetch = pltpu.make_async_copy(qd_all_ref.at[pl.ds(half - first, next_ref.shape[0])], next_ref, done)
     fetch.start()
-    fetch_next = pltpu.make_async_copy(qd_all_ref.at[pl.ds(half - first, next_ref.shape[0])], next_ref, done.at[1])
-    fetch_next.start()
     bias = bias_ref[...].astype(F32)
-    fetch.wait()
     for y in range(half):
         out_ref[y] = query_grads(
             scaling,
@@ -130,7 +142,7 @@
             jnp.concatenate([here_ref[half + y], kv_ref[1, first + y]], axis=0),
             bias,
         )
-    fetch_next.wait()
+    fetch.wait()
 
 
 def middle_query_kernel(scaling, bias_ref, here_ref, other_ref, kv_ref, early_ref, qd_ref, stash_ref):
@@ -265,20 +277,21 @@
     qd_group = lax.all_to_all(qd, "tp", split_axis=0, concat_axis=0, tiled=True)
     kv_shape = shape((2, groups, rows, width), BF16)
     bias_shape = (rows + rows // 2, rows)
-    kv, bias = call(
+    kv, bias, half_qd = call(
         key_prepare_kernel,
-        (lengths, keys, values),
-        [kv_shape, shape(bias_shape, BF16)],
-        [pltpu.VMEM(bias_shape, F32)],
+        (lengths, keys, values, qd),
+        [kv_shape, shape(bias_shape, BF16), shape((half, 2, rows, width), BF16)],
+        [pltpu.VMEM(bias_shape, F32), pltpu.SemaphoreType.DMA(())],
+        last=HBM,
         dots=20,
     )
     other = lax.ppermute(here, "tp", [(d, d ^ 1) for d in range(lax.axis_size("tp"))])
     middle = 2
     early, next_qd = call(
         functools.partial(early_query_kernel, scaling),
-        (bias, here, kv, qd),
+        (bias, here, kv, half_qd, qd),
         [shape((half, rows, width), BF16), shape((middle, 2, rows, width), BF16)],
-        [pltpu.VMEM((half, 2, rows, width), BF16), pltpu.SemaphoreType.DMA((2,))],
+        [pltpu.SemaphoreType.DMA(())],
         last=HBM,
         dots=1,
     )

time: 44.2 us -> 44.2 us (level)
  Pallas kernels: 11.4 us -> 10.8 us
  starting transfers between devices: 15.7 us -> 16.2 us
    pallas_call x7, Pallas kernels: 11.4 us -> 10.8 us  [call(): pl.pallas_call(kernel, in_specs=[VMEM] * (len(operands) - 1) + [last], ou...]
    ppermute x2, starting transfers between devices: 9.31 us -> 9.83 us  [shifted(): return lax.ppermute(block, axis, route)]
  transfers between devices with their start and end apart: 4 -> 4, of which waited for: 2 -> 2; matrix products, arithmetic and copies ran while one was open for 0% -> 0% of each run, Pallas kernels for 18% -> 16%
where the time goes in v7:
time: 44.2 us; the launch traced here: 43.9 us
  starting transfers between devices  16.2 us (37%)
  waiting for transfers between devices  14.5 us (33%)
  Pallas kernels  10.8 us (24%)
  local copies, waits for them, and re-layouts  1.58 us (4%)
  between operations  0.81 us (2%)
    ppermute x2, waiting for transfers between devices, shifted(): return lax.ppermute(block, axis, route)  14.5 us
    pallas_call x7, Pallas kernels, call(): pl.pallas_call(kernel, in_specs=[VMEM] * (len(operands) - 1) + [last], ou...  10.8 us
    ppermute x2, starting transfers between devices, shifted(): return lax.ppermute(block, axis, route)  9.83 us
    all_to_all x1, starting transfers between devices, per_device(): qd_group = lax.all_to_all(qd, 'tp', split_axis=0, concat_axis=0, tiled=True)  4.43 us
    ppermute x1, starting transfers between devices, per_device(): lax.ppermute(here, 'tp', [(d, d ^ 1) for d in range(lax.axis_size('tp'))])  1.91 us
    dynamic_slice x1, local copies, waits for them, and re-layouts, per_device(): lax.dynamic_slice(block, (0, (device & 1) * half, 0), (rows, half, width))  1.48 us
  transfers between devices with their start and end apart: 4, of which 2 were waited for; matrix products, arithmetic and copies ran while one was open for 0% of the time, Pallas kernels for 16%

profile of v7, /device:TPU:24, one launch (start us, length us, event | category | flops | bytes accessed | tf_op | source)
XLA Modules:
  0.0 43.9 jit_solution(3791434595554965927)
XLA Ops:
  0.6 1.5 %constant_dynamic-slice_fusion = (bf16[256,4,128]{2,1,0:T(4,128)(2,1)S(1)}, bf16[256,4,128]{2,1,0:T(4,128)(2,1)S(1)}) fusion(bf16[256,8,128]{2,1,0:T(8,128)(2,1)} %value_ref.1, s32[]{:T(128)S(6)} %select_n.4, bf16[256,8,128]{2,1,0:T(8,128)(2,1)} %key_ref.1), kind=kLoop, calls=%fused_computation.1 | loop fusion | bytes 1048580 | tf_op jit(solution)/shard_map/dynamic_slice | solution.py:267
  2.1 0.0 copy-start
  2.1 0.0 copy-start.1
  2.1 0.0 copy-start.4
  2.3 4.0 %collective-permute-start = (bf16[8,256,128]{2,1,0:T(8,128)(2,1)S(1)}, bf16[8,256,128]{2,1,0:T(8,128)(2,1)S(1)}, u32[]{:S(2)}, u32[]{:S(2)}) collective-permute-start(bf16[8,256,128]{2,1,0:T(8,128)(2,1)S(1)} %maximum_bitcast_fusion), channel_id=1, source_target_pairs={{0,8},{8,16},{16,24},{24,32},{32,40},{40,48},{48,56},{56,64},{64,7... | collective-permute-start | bytes 1572872 | tf_op jit(solution)/shard_map/ppermute | solution.py:33
  6.3 0.0 copy-done
  6.3 0.0 copy-done.1
  6.3 0.0 copy-done.4
  6.3 1.3 %query_prepare_kernel.1.qd_ref.qd_all_ref.qd_here_ref = bf16[8,2,256,128]{3,2,1,0:T(8,128)(2,1)} custom-call(s32[2,8]{1,0:T(2,128)S(1)} %bitcast.13, bf16[256,8,128]{2,1,0:T(8,128)(2,1)S(1)} %bitcast.11, bf16[256,8,128]{2,1,0:T(8,128)(2,1)S(1)} %bitcast.12), custom_call_target="tpu_custom_call" | custom-call | flops 1000000 | bytes 1048576 | tf_op jit(solution)/shard_map/query_prepare_kernel/pallas_call | solution.py:255
  7.6 0.0 copy-start.2
  7.6 0.0 copy-start.3
  7.6 0.0 copy-start.5
  7.6 4.4 %all-to-all-start = ((bf16[8,2,256,128]{3,2,1,0:T(8,128)(2,1)}), bf16[8,2,256,128]{3,2,1,0:T(8,128)(2,1)S(1)}, u32[]{:S(2)}, u32[]{:S(2)}) async-start(bf16[8,2,256,128]{3,2,1,0:T(8,128)(2,1)} %query_prepare_kernel.1.qd_ref.qd_all_ref.qd_here_ref), calls=%async_computation | async-start | bytes 2097152 | tf_op jit(solution)/shard_map/all_to_all | solution.py:277
  12.1 13.9 %collective-permute-done.here_ref = bf16[8,256,128]{2,1,0:T(8,128)(2,1)S(1)} collective-permute-done((bf16[8,256,128]{2,1,0:T(8,128)(2,1)S(1)}, bf16[8,256,128]{2,1,0:T(8,128)(2,1)S(1)}, u32[]{:S(2)}, u32[]{:S(2)}) %collective-permute-start) | collective-permute-done | bytes 524320 | tf_op jit(solution)/shard_map/ppermute | solution.py:33
  25.9 1.9 %collective-permute-start.1 = (bf16[8,256,128]{2,1,0:T(8,128)(2,1)S(1)}, bf16[8,256,128]{2,1,0:T(8,128)(2,1)S(1)}, u32[]{:S(2)}, u32[]{:S(2)}) collective-permute-start(bf16[8,256,128]{2,1,0:T(8,128)(2,1)S(1)} %collective-permute-done.here_ref), channel_id=1, source_target_pairs={{0,1},{1,0},{2,3},{3,2},{4,5},{5,4},{6,7},{7,6},{8,9},{9,8},{10,11... | collective-permute-start | bytes 1572872 | tf_op jit(solution)/shard_map/ppermute | solution.py:288
  27.8 0.0 copy-done.2
  27.9 0.0 copy-done.3
  27.9 0.0 copy-done.5
  27.9 1.1 %key_prepare_kernel.1 = (bf16[2,8,256,128]{3,2,1,0:T(8,128)(2,1)S(1)}, bf16[384,256]{1,0:T(8,128)(2,1)S(1)}, bf16[4,2,256,128]{3,2,1,0:T(8,128)(2,1)S(1)}) custom-call(s32[1,128]{1,0:T(1,128)S(1)} %bitcast.14, bf16[256,8,128]{2,1,0:T(8,128)(2,1)S(1)} %copy-done.2, bf16[256,8,128]{2,1,0:T(8,128)(2,1)S(1)} %copy-done.3, ...), custom_call_target="tpu_custom_call" | custom-call | flops 5369709056 | bytes 1048576 | tf_op jit(solution)/shard_map/key_prepare_kernel/pallas_call | solution.py:255
  28.9 1.8 %early_query_kernel.1 = (bf16[4,256,128]{2,1,0:T(8,128)(2,1)S(1)}, bf16[2,2,256,128]{3,2,1,0:T(8,128)(2,1)S(1)}) custom-call(bf16[384,256]{1,0:T(8,128)(2,1)S(1)} %get-tuple-element.15.bias_ref, bf16[8,256,128]{2,1,0:T(8,128)(2,1)S(1)} %collective-permute-done.here_ref, bf16[2,8,256,128]{3,2,1,0:T(8,128)(2,1)S(1)} %get-tuple-element.16.kv_ref, ...), custom_call_target="tpu_custom_call" | custom-call | flops 269435456 | bytes 1048576 | tf_op jit(solution)/shard_map/early_query_kernel/pallas_call | solution.py:255
  30.8 0.0 collective-permute-done.1.other_ref
  30.8 1.0 %middle_query_kernel.1.stash_ref = bf16[20,256,128]{2,1,0:T(8,128)(2,1)S(1)} custom-call(bf16[384,256]{1,0:T(8,128)(2,1)S(1)} %get-tuple-element.15.bias_ref, bf16[8,256,128]{2,1,0:T(8,128)(2,1)S(1)} %collective-permute-done.here_ref, bf16[8,256,128]{2,1,0:T(8,128)(2,1)S(1)} %collective-permute-done.1.other_ref, ...), custom_call_target="tpu_custom_call" | custom-call | flops 269435456 | bytes 1048576 | tf_op jit(solution)/shard_map/middle_query_kernel/pallas_call | solution.py:255
  31.8 0.0 all-to-all-done.qd_ref
  31.8 3.0 %key_side_kernel.1 = (bf16[2,256,128]{2,1,0:T(8,128)(2,1)S(1)}, f32[2,256,128]{2,1,0:T(8,128)S(1)}, bf16[2,2,256,128]{3,2,1,0:T(8,128)(2,1)S(1)}) custom-call(bf16[384,256]{1,0:T(8,128)(2,1)S(1)} %get-tuple-element.15.bias_ref, bf16[8,2,256,128]{3,2,1,0:T(8,128)(2,1)S(1)} %all-to-all-done.qd_ref, bf16[20,256,128]{2,1,0:T(8,128)(2,1)S(1)} %middle_query_kernel.1.stash_ref, ...), custom_call_target="tpu_custom_call" | custom-call | flops 1074741760 | bytes 1048576 | tf_op jit(solution)/shard_map/key_side_kernel/pallas_call | solution.py:255
  34.8 5.9 %collective-permute-start.2 = (bf16[2,256,128]{2,1,0:T(8,128)(2,1)S(1)}, bf16[2,256,128]{2,1,0:T(8,128)(2,1)S(1)}, u32[]{:S(2)}, u32[]{:S(2)}) collective-permute-start(bf16[2,256,128]{2,1,0:T(8,128)(2,1)S(1)} %get-tuple-element.22), channel_id=1, source_target_pairs={{8,0},{16,8},{24,16},{32,24},{40,32},{48,40},{56,48},{64,56},{72,6... | collective-permute-start | bytes 393224 | tf_op jit(solution)/shard_map/ppermute | solution.py:33
  40.7 1.9 %late_query_kernel.1 = bf16[256,8,128]{2,1,0:T(8,128)(2,1)} custom-call(bf16[384,256]{1,0:T(8,128)(2,1)S(1)} %get-tuple-element.15.bias_ref, bf16[20,256,128]{2,1,0:T(8,128)(2,1)S(1)} %middle_query_kernel.1.stash_ref, bf16[2,2,256,128]{3,2,1,0:T(8,128)(2,1)S(1)} %get-tuple-element.20.qd_ref), custom_call_target="tpu_custom_call" | custom-call | flops 806306368 | bytes 1048576 | tf_op jit(solution)/shard_map/late_query_kernel/pallas_call | solution.py:255
  42.6 0.6 %collective-permute-done.2.back_ref = bf16[2,256,128]{2,1,0:T(8,128)(2,1)S(1)} collective-permute-done((bf16[2,256,128]{2,1,0:T(8,128)(2,1)S(1)}, bf16[2,256,128]{2,1,0:T(8,128)(2,1)S(1)}, u32[]{:S(2)}, u32[]{:S(2)}) %collective-permute-start.2) | collective-permute-done | bytes 131104 | tf_op jit(solution)/shard_map/ppermute | solution.py:33
  43.2 0.7 %finish_kernel.1 = (bf16[256,128]{1,0:T(8,128)(2,1)}, bf16[256,128]{1,0:T(8,128)(2,1)}) custom-call(f32[2,256,128]{2,1,0:T(8,128)S(1)} %get-tuple-element.21.own_ref, bf16[2,256,128]{2,1,0:T(8,128)(2,1)S(1)} %collective-permute-done.2.back_ref), custom_call_target="tpu_custom_call" | custom-call | flops 1000000 | bytes 1048576 | tf_op jit(solution)/shard_map/finish_kernel/pallas_call | solution.py:255
  (3 shorter events, 0.1 us)
Async XLA Ops:
  2.1 4.2 %copy-start = (bf16[256,8,1,128]{3,1,2,0:T(8,128)(2,1)S(1)}, bf16[256,8,1,128]{3,1,2,0:T(8,128)(2,1)}, u32[]{:S(2)}) copy-start(bf16[256,8,1,128]{3,1,2,0:T(8,128)(2,1)} %param.6) | copy-start | bytes 1572868
  2.1 4.1 %copy-start.1 = (bf16[256,8,1,128]{3,1,2,0:T(8,128)(2,1)S(1)}, bf16[256,8,1,128]{3,1,2,0:T(8,128)(2,1)}, u32[]{:S(2)}) copy-start(bf16[256,8,1,128]{3,1,2,0:T(8,128)(2,1)} %param.9) | copy-start | bytes 1572868
  2.1 4.1 %copy-start.4 = (s32[2,8,1]{1,2,0:T(1,128)S(1)}, s32[2,8,1]{1,2,0:T(1,128)}, u32[]{:S(2)}) copy-start(s32[2,8,1]{1,2,0:T(1,128)} %param.10) | copy-start | bytes 196
  2.3 23.6 %collective-permute-start = (bf16[8,256,128]{2,1,0:T(8,128)(2,1)S(1)}, bf16[8,256,128]{2,1,0:T(8,128)(2,1)S(1)}, u32[]{:S(2)}, u32[]{:S(2)}) collective-permute-start(bf16[8,256,128]{2,1,0:T(8,128)(2,1)S(1)} %maximum_bitcast_fusion), channel_id=1, source_target_pairs={{0,8},{8,16},{16,24},{24,32},{32,40},{40,48},{48,56},{56,64},{64,7... | collective-permute-start | bytes 1572872 | tf_op jit(solution)/shard_map/ppermute | solution.py:33
  7.6 20.2 %copy-start.2 = (bf16[256,8,128]{2,1,0:T(8,128)(2,1)S(1)}, bf16[256,8,128]{2,1,0:T(8,128)(2,1)}, u32[]{:S(2)}) copy-start(bf16[256,8,128]{2,1,0:T(8,128)(2,1)} %key_ref.1) | copy-start | bytes 1572868
  7.6 20.2 %copy-start.3 = (bf16[256,8,128]{2,1,0:T(8,128)(2,1)S(1)}, bf16[256,8,128]{2,1,0:T(8,128)(2,1)}, u32[]{:S(2)}) copy-start(bf16[256,8,128]{2,1,0:T(8,128)(2,1)} %value_ref.1) | copy-start | bytes 1572868
  7.6 20.2 %copy-start.5 = (s32[128]{0:T(128)S(1)}, s32[128]{0:T(128)}, u32[]{:S(2)}) copy-start(s32[128]{0:T(128)} %param.11) | copy-start | bytes 1540
  7.6 24.2 %all-to-all-start = ((bf16[8,2,256,128]{3,2,1,0:T(8,128)(2,1)}), bf16[8,2,256,128]{3,2,1,0:T(8,128)(2,1)S(1)}, u32[]{:S(2)}, u32[]{:S(2)}) async-start(bf16[8,2,256,128]{3,2,1,0:T(8,128)(2,1)} %query_prepare_kernel.1.qd_ref.qd_all_ref.qd_here_ref), calls=%async_computation | async-start | bytes 2097152 | tf_op jit(solution)/shard_map/all_to_all | solution.py:277
  25.9 4.8 %collective-permute-start.1 = (bf16[8,256,128]{2,1,0:T(8,128)(2,1)S(1)}, bf16[8,256,128]{2,1,0:T(8,128)(2,1)S(1)}, u32[]{:S(2)}, u32[]{:S(2)}) collective-permute-start(bf16[8,256,128]{2,1,0:T(8,128)(2,1)S(1)} %collective-permute-done.here_ref), channel_id=1, source_target_pairs={{0,1},{1,0},{2,3},{3,2},{4,5},{5,4},{6,7},{7,6},{8,9},{9,8},{10,11... | collective-permute-start | bytes 1572872 | tf_op jit(solution)/shard_map/ppermute | solution.py:288
  34.8 8.4 %collective-permute-start.2 = (bf16[2,256,128]{2,1,0:T(8,128)(2,1)S(1)}, bf16[2,256,128]{2,1,0:T(8,128)(2,1)S(1)}, u32[]{:S(2)}, u32[]{:S(2)}) collective-permute-start(bf16[2,256,128]{2,1,0:T(8,128)(2,1)S(1)} %get-tuple-element.22), channel_id=1, source_target_pairs={{8,0},{16,8},{24,16},{32,24},{40,32},{48,40},{56,48},{64,56},{72,6... | collective-permute-start | bytes 393224 | tf_op jit(solution)/shard_map/ppermute | solution.py:33

commit v8 on v7

--- a/solution.py
+++ b/solution.py
@@ -72,30 +72,22 @@
     return middle, corners, 1.0 / total
 
 
-def pair_terms(query, dout, key, value, bias, scaling):
-    middle, corners, inverse = shifted_exps(query, key, bias, scaling)
-    middle = middle * inverse
-    corners = corners * inverse
-    grad_middle, grad_corners = window_dots(value, dout)
-    row_delta = jnp.sum(middle * grad_middle, axis=0, keepdims=True) + jnp.sum(
-        corners * grad_corners, axis=0, keepdims=True
-    )
-    return (
-        middle.astype(BF16),
-        corners.astype(BF16),
-        (middle * (grad_middle - row_delta)).astype(BF16),
-        (corners * (grad_corners - row_delta)).astype(BF16),
-    )
-
-
-def query_prepare_kernel(exp_ref, query_ref, grad_ref, qd_ref):
-    qd_ref[:, 0] = jnp.swapaxes(query_ref[...], 0, 1)
+def query_prepare_kernel(exp_ref, query_ref, grad_ref, out_ref, qd, done):
     blocks, groups = exp_ref.shape
     rows = grad_ref.shape[0] // blocks
     factor = jnp.exp2(exp_ref[...].astype(F32)).astype(BF16)
-    for b in range(blocks):
-        part = pl.ds(b * rows, rows)
-        qd_ref[:, 1, part] = jnp.swapaxes(grad_ref[part], 0, 1) * factor[b][:, None, None]
+    copies = []
+    for i, ref in enumerate((query_ref, grad_ref)):
+        for b in range(blocks):
+            part = pl.ds(b * rows, rows)
+            piece = jnp.swapaxes(ref[part], 0, 1)
+            qd[:, i, part] = piece * factor[b][:, None, None] if i else piece
+            copies.append(
+                pltpu.make_async_copy(qd.at[:, i, part], out_ref.at[:, i, part], done.at[i * blocks + b])
+            )
+            copies[-1].start()
+    for copy in copies:
+        copy.wait()
 
 
 def key_prepare_kernel(lengths_ref, key_ref, value_ref, qd_ref, kv_ref, bias_ref, half_ref, bias, done):
@@ -200,7 +192,7 @@
 
 
 def key_side_kernel(
-    scaling, bias_ref, qd_ref, stash_ref, qd_here_ref, cross_ref, own_ref, late_ref, mid_terms, left_terms, right_terms, done
+    scaling, bias_ref, qd_ref, stash_ref, qd_here_ref, cross_ref, own_ref, late_ref, terms, done
 ):
     heads, _, rows, width = qd_ref.shape
     half = rows // 2
@@ -214,25 +206,32 @@
         jnp.concatenate([jnp.where(came_here, stash_ref[at], stash_ref[at + 1]), stash_ref[at + 2]], axis=0)
         for at in (0, 3)
     )
-    bias = bias_ref[...].astype(F32)
-    for h in range(heads):
-        probs, probs_c, grads, grads_c = pair_terms(qd_ref[h, 0], qd_ref[h, 1], key, value, bias, scaling)
-        at, at_half = pl.ds(h * rows, rows), pl.ds(h * half, half)
-        mid_terms[0, :, at] = grads
-        mid_terms[1, :, at] = probs
-        left_terms[0, :, at_half] = grads_c[:, :half]
-        left_terms[1, :, at_half] = probs_c[:, :half]
-        right_terms[0, :, at_half] = grads_c[:, half:]
-        right_terms[1, :, at_half] = probs_c[:, half:]
+    for second in range(2):
+        lanes = slice(second * half, (second + 1) * half)
+        reach = slice(second * half, (second + 3) * half)
+        middle, corner = bias_ref[:rows, lanes], bias_ref[rows:, lanes]
+        bias = jnp.concatenate([middle, corner] if second else [corner, middle], axis=0).astype(F32)
+        bias = jnp.concatenate([bias, bias], axis=1)
+        for h in range(0, heads, 2):
+            query = qd_ref[h : h + 2, 0, lanes].reshape(rows, width)
+            dout = qd_ref[h : h + 2, 1, lanes].reshape(rows, width)
+            scores = dot_nt(key[reach], query) * (scaling * math.log2(math.e)) + bias
+            shifted_exp = jnp.exp2(scores - jnp.max(scores, axis=0, keepdims=True))
+            probs = shifted_exp * (1.0 / jnp.sum(shifted_exp, axis=0, keepdims=True))
+            grad_probs = dot_nt(value[reach], dout)
+            row_delta = jnp.sum(probs * grad_probs, axis=0, keepdims=True)
+            at = pl.ds(h * half, rows)
+            terms[second, 0, :, at] = (probs * (grad_probs - row_delta)).astype(BF16)
+            terms[second, 1, :, at] = probs.astype(BF16)
     for i, factor in ((0, scaling), (1, 1.0)):
-        both = qd_ref[:, i].reshape(heads * rows, width)
-        early = qd_ref[:, i, :half].reshape(heads * half, width)
-        late = qd_ref[:, i, half:].reshape(heads * half, width)
-        middle = dot_nn(mid_terms[i], both) * factor
-        cross_ref[i, :half] = (dot_nn(left_terms[i], early) * factor).astype(BF16)
-        cross_ref[i, half:] = middle[:half].astype(BF16)
-        own_ref[i, :half] = middle[half:]
-        own_ref[i, half:] = dot_nn(right_terms[i], late) * factor
+        first, last = (
+            dot_nn(terms[second, i], qd_ref[:, i, second * half : (second + 1) * half].reshape(heads * half, width)) * factor
+            for second in range(2)
+        )
+        cross_ref[i, :half] = first[:half].astype(BF16)
+        cross_ref[i, half:] = (first[half:rows] + last[:half]).astype(BF16)
+        own_ref[i, :half] = first[rows:] + last[half:rows]
+        own_ref[i, half:] = last[rows:]
     fetch.wait()
 
 
@@ -269,10 +268,13 @@
     exponents = exponents.reshape(-1, groups)
     here = shifted(half_kv, "seq", 1)
     queries, half_kv = lax.optimization_barrier((queries, half_kv))
+    qd_shape = (groups, 2, rows, width)
     qd = call(
         query_prepare_kernel,
         (exponents, queries.reshape(rows, groups, width), grad_out.reshape(rows, groups, width)),
-        shape((groups, 2, rows, width), BF16),
+        shape(qd_shape, BF16),
+        [pltpu.VMEM(qd_shape, BF16), pltpu.SemaphoreType.DMA((2 * exponents.shape[0],))],
+        out=HBM,
     )
     qd_group = lax.all_to_all(qd, "tp", split_axis=0, concat_axis=0, tiled=True)
     kv_shape = shape((2, groups, rows, width), BF16)
@@ -306,9 +308,7 @@
         (bias, qd_group, stash, qd),
         [shape((2, rows, width), BF16), shape((2, rows, width), F32), shape((half - middle, 2, rows, width), BF16)],
         [
-            pltpu.VMEM((2, rows, pairs * rows), BF16),
-            pltpu.VMEM((2, rows // 2, pairs * rows // 2), BF16),
-            pltpu.VMEM((2, rows // 2, pairs * rows // 2), BF16),
+            pltpu.VMEM((2, 2, rows + rows // 2, pairs * rows // 2), BF16),
             pltpu.SemaphoreType.DMA(()),
         ],
         last=HBM,

time: 44.2 us -> 43.6 us (0.986)
  Pallas kernels: 10.8 us -> 10.2 us
    pallas_call x7, Pallas kernels: 10.8 us -> 10.2 us  [call(): pl.pallas_call(kernel, in_specs=[VMEM] * (len(operands) - 1) + [last], ou...]
where the time goes in v8:
time: 43.6 us; the launch traced here: 43.4 us
  starting transfers between devices  16.1 us (37%)
  waiting for transfers between devices  14.6 us (33%)
  Pallas kernels  10.2 us (23%)
  local copies, waits for them, and re-layouts  1.59 us (4%)
  between operations  0.84 us (2%)
    ppermute x2, waiting for transfers between devices, shifted(): return lax.ppermute(block, axis, route)  14.6 us
    pallas_call x7, Pallas kernels, call(): pl.pallas_call(kernel, in_specs=[VMEM] * (len(operands) - 1) + [last], ou...  10.2 us
    ppermute x2, starting transfers between devices, shifted(): return lax.ppermute(block, axis, route)  9.7 us
    all_to_all x1, starting transfers between devices, per_device(): qd_group = lax.all_to_all(qd, 'tp', split_axis=0, concat_axis=0, tiled=True)  4.44 us
    ppermute x1, starting transfers between devices, per_device(): lax.ppermute(here, 'tp', [(d, d ^ 1) for d in range(lax.axis_size('tp'))])  1.91 us
    dynamic_slice x1, local copies, waits for them, and re-layouts, per_device(): lax.dynamic_slice(block, (0, (device & 1) * half, 0), (rows, half, width))  1.48 us
  transfers between devices with their start and end apart: 4, of which 2 were waited for; matrix products, arithmetic and copies ran while one was open for 0% of the time, Pallas kernels for 16%

profile of v8, /device:TPU:24, one launch (start us, length us, event | category | flops | bytes accessed | tf_op | source)
XLA Modules:
  0.0 43.4 jit_solution(16085920252278208053)
XLA Ops:
  0.6 1.5 %constant_dynamic-slice_fusion = (bf16[256,4,128]{2,1,0:T(4,128)(2,1)S(1)}, bf16[256,4,128]{2,1,0:T(4,128)(2,1)S(1)}) fusion(bf16[256,8,128]{2,1,0:T(8,128)(2,1)} %value_ref.1, s32[]{:T(128)S(6)} %select_n.4, bf16[256,8,128]{2,1,0:T(8,128)(2,1)} %key_ref.1), kind=kLoop, calls=%fused_computation.1 | loop fusion | bytes 1048580 | tf_op jit(solution)/shard_map/dynamic_slice | solution.py:266
  2.1 0.0 copy-start
  2.1 0.0 copy-start.1
  2.1 0.0 copy-start.4
  2.3 4.0 %collective-permute-start = (bf16[8,256,128]{2,1,0:T(8,128)(2,1)S(1)}, bf16[8,256,128]{2,1,0:T(8,128)(2,1)S(1)}, u32[]{:S(2)}, u32[]{:S(2)}) collective-permute-start(bf16[8,256,128]{2,1,0:T(8,128)(2,1)S(1)} %maximum_bitcast_fusion), channel_id=1, source_target_pairs={{0,8},{8,16},{16,24},{24,32},{32,40},{40,48},{48,56},{56,64},{64,7... | collective-permute-start | bytes 1572872 | tf_op jit(solution)/shard_map/ppermute | solution.py:33
  6.3 0.0 copy-done
  6.3 0.0 copy-done.1
  6.3 0.0 copy-done.4
  6.3 1.1 %query_prepare_kernel.1.qd_ref.qd_all_ref.qd_here_ref = bf16[8,2,256,128]{3,2,1,0:T(8,128)(2,1)} custom-call(s32[2,8]{1,0:T(2,128)S(1)} %bitcast.13, bf16[256,8,128]{2,1,0:T(8,128)(2,1)S(1)} %bitcast.11, bf16[256,8,128]{2,1,0:T(8,128)(2,1)S(1)} %bitcast.12), custom_call_target="tpu_custom_call" | custom-call | flops 1000000 | bytes 1048576 | tf_op jit(solution)/shard_map/query_prepare_kernel/pallas_call | solution.py:254
  7.4 0.0 copy-start.2
  7.5 0.0 copy-start.3
  7.5 0.0 copy-start.5
  7.5 4.4 %all-to-all-start = ((bf16[8,2,256,128]{3,2,1,0:T(8,128)(2,1)}), bf16[8,2,256,128]{3,2,1,0:T(8,128)(2,1)S(1)}, u32[]{:S(2)}, u32[]{:S(2)}) async-start(bf16[8,2,256,128]{3,2,1,0:T(8,128)(2,1)} %query_prepare_kernel.1.qd_ref.qd_all_ref.qd_here_ref), calls=%async_computation | async-start | bytes 2097152 | tf_op jit(solution)/shard_map/all_to_all | solution.py:279
  11.9 14.0 %collective-permute-done.here_ref = bf16[8,256,128]{2,1,0:T(8,128)(2,1)S(1)} collective-permute-done((bf16[8,256,128]{2,1,0:T(8,128)(2,1)S(1)}, bf16[8,256,128]{2,1,0:T(8,128)(2,1)S(1)}, u32[]{:S(2)}, u32[]{:S(2)}) %collective-permute-start) | collective-permute-done | bytes 524320 | tf_op jit(solution)/shard_map/ppermute | solution.py:33
  25.9 1.9 %collective-permute-start.1 = (bf16[8,256,128]{2,1,0:T(8,128)(2,1)S(1)}, bf16[8,256,128]{2,1,0:T(8,128)(2,1)S(1)}, u32[]{:S(2)}, u32[]{:S(2)}) collective-permute-start(bf16[8,256,128]{2,1,0:T(8,128)(2,1)S(1)} %collective-permute-done.here_ref), channel_id=1, source_target_pairs={{0,1},{1,0},{2,3},{3,2},{4,5},{5,4},{6,7},{7,6},{8,9},{9,8},{10,11... | collective-permute-start | bytes 1572872 | tf_op jit(solution)/shard_map/ppermute | solution.py:290
  27.8 0.0 copy-done.2
  27.9 0.0 copy-done.3
  27.9 0.0 copy-done.5
  27.9 1.1 %key_prepare_kernel.1 = (bf16[2,8,256,128]{3,2,1,0:T(8,128)(2,1)S(1)}, bf16[384,256]{1,0:T(8,128)(2,1)S(1)}, bf16[4,2,256,128]{3,2,1,0:T(8,128)(2,1)S(1)}) custom-call(s32[1,128]{1,0:T(1,128)S(1)} %bitcast.14, bf16[256,8,128]{2,1,0:T(8,128)(2,1)S(1)} %copy-done.2, bf16[256,8,128]{2,1,0:T(8,128)(2,1)S(1)} %copy-done.3, ...), custom_call_target="tpu_custom_call" | custom-call | flops 5369709056 | bytes 1048576 | tf_op jit(solution)/shard_map/key_prepare_kernel/pallas_call | solution.py:254
  28.9 1.8 %early_query_kernel.1 = (bf16[4,256,128]{2,1,0:T(8,128)(2,1)S(1)}, bf16[2,2,256,128]{3,2,1,0:T(8,128)(2,1)S(1)}) custom-call(bf16[384,256]{1,0:T(8,128)(2,1)S(1)} %get-tuple-element.15.bias_ref, bf16[8,256,128]{2,1,0:T(8,128)(2,1)S(1)} %collective-permute-done.here_ref, bf16[2,8,256,128]{3,2,1,0:T(8,128)(2,1)S(1)} %get-tuple-element.16.kv_ref, ...), custom_call_target="tpu_custom_call" | custom-call | flops 269435456 | bytes 1048576 | tf_op jit(solution)/shard_map/early_query_kernel/pallas_call | solution.py:254
  30.8 0.0 collective-permute-done.1.other_ref
  30.8 1.0 %middle_query_kernel.1.stash_ref = bf16[20,256,128]{2,1,0:T(8,128)(2,1)S(1)} custom-call(bf16[384,256]{1,0:T(8,128)(2,1)S(1)} %get-tuple-element.15.bias_ref, bf16[8,256,128]{2,1,0:T(8,128)(2,1)S(1)} %collective-permute-done.here_ref, bf16[8,256,128]{2,1,0:T(8,128)(2,1)S(1)} %collective-permute-done.1.other_ref, ...), custom_call_target="tpu_custom_call" | custom-call | flops 269435456 | bytes 1048576 | tf_op jit(solution)/shard_map/middle_query_kernel/pallas_call | solution.py:254
  31.8 0.0 all-to-all-done.qd_ref
  31.8 2.6 %key_side_kernel.1 = (bf16[2,256,128]{2,1,0:T(8,128)(2,1)S(1)}, f32[2,256,128]{2,1,0:T(8,128)S(1)}, bf16[2,2,256,128]{3,2,1,0:T(8,128)(2,1)S(1)}) custom-call(bf16[384,256]{1,0:T(8,128)(2,1)S(1)} %get-tuple-element.15.bias_ref, bf16[8,2,256,128]{3,2,1,0:T(8,128)(2,1)S(1)} %all-to-all-done.qd_ref, bf16[20,256,128]{2,1,0:T(8,128)(2,1)S(1)} %middle_query_kernel.1.stash_ref, ...), custom_call_target="tpu_custom_call" | custom-call | flops 1074741760 | bytes 1048576 | tf_op jit(solution)/shard_map/key_side_kernel/pallas_call | solution.py:254
  34.4 5.7 %collective-permute-start.2 = (bf16[2,256,128]{2,1,0:T(8,128)(2,1)S(1)}, bf16[2,256,128]{2,1,0:T(8,128)(2,1)S(1)}, u32[]{:S(2)}, u32[]{:S(2)}) collective-permute-start(bf16[2,256,128]{2,1,0:T(8,128)(2,1)S(1)} %get-tuple-element.22), channel_id=1, source_target_pairs={{8,0},{16,8},{24,16},{32,24},{40,32},{48,40},{56,48},{64,56},{72,6... | collective-permute-start | bytes 393224 | tf_op jit(solution)/shard_map/ppermute | solution.py:33
  40.2 1.9 %late_query_kernel.1 = bf16[256,8,128]{2,1,0:T(8,128)(2,1)} custom-call(bf16[384,256]{1,0:T(8,128)(2,1)S(1)} %get-tuple-element.15.bias_ref, bf16[20,256,128]{2,1,0:T(8,128)(2,1)S(1)} %middle_query_kernel.1.stash_ref, bf16[2,2,256,128]{3,2,1,0:T(8,128)(2,1)S(1)} %get-tuple-element.20.qd_ref), custom_call_target="tpu_custom_call" | custom-call | flops 806306368 | bytes 1048576 | tf_op jit(solution)/shard_map/late_query_kernel/pallas_call | solution.py:254
  42.1 0.6 %collective-permute-done.2.back_ref = bf16[2,256,128]{2,1,0:T(8,128)(2,1)S(1)} collective-permute-done((bf16[2,256,128]{2,1,0:T(8,128)(2,1)S(1)}, bf16[2,256,128]{2,1,0:T(8,128)(2,1)S(1)}, u32[]{:S(2)}, u32[]{:S(2)}) %collective-permute-start.2) | collective-permute-done | bytes 131104 | tf_op jit(solution)/shard_map/ppermute | solution.py:33
  42.7 0.7 %finish_kernel.1 = (bf16[256,128]{1,0:T(8,128)(2,1)}, bf16[256,128]{1,0:T(8,128)(2,1)}) custom-call(f32[2,256,128]{2,1,0:T(8,128)S(1)} %get-tuple-element.21.own_ref, bf16[2,256,128]{2,1,0:T(8,128)(2,1)S(1)} %collective-permute-done.2.back_ref), custom_call_target="tpu_custom_call" | custom-call | flops 1000000 | bytes 1048576 | tf_op jit(solution)/shard_map/finish_kernel/pallas_call | solution.py:254
  (3 shorter events, 0.1 us)
Async XLA Ops:
  2.1 4.2 %copy-start = (bf16[256,8,1,128]{3,1,2,0:T(8,128)(2,1)S(1)}, bf16[256,8,1,128]{3,1,2,0:T(8,128)(2,1)}, u32[]{:S(2)}) copy-start(bf16[256,8,1,128]{3,1,2,0:T(8,128)(2,1)} %param.6) | copy-start | bytes 1572868
  2.1 4.1 %copy-start.1 = (bf16[256,8,1,128]{3,1,2,0:T(8,128)(2,1)S(1)}, bf16[256,8,1,128]{3,1,2,0:T(8,128)(2,1)}, u32[]{:S(2)}) copy-start(bf16[256,8,1,128]{3,1,2,0:T(8,128)(2,1)} %param.9) | copy-start | bytes 1572868
  2.1 4.1 %copy-start.4 = (s32[2,8,1]{1,2,0:T(1,128)S(1)}, s32[2,8,1]{1,2,0:T(1,128)}, u32[]{:S(2)}) copy-start(s32[2,8,1]{1,2,0:T(1,128)} %param.10) | copy-start | bytes 196
  2.3 23.6 %collective-permute-start = (bf16[8,256,128]{2,1,0:T(8,128)(2,1)S(1)}, bf16[8,256,128]{2,1,0:T(8,128)(2,1)S(1)}, u32[]{:S(2)}, u32[]{:S(2)}) collective-permute-start(bf16[8,256,128]{2,1,0:T(8,128)(2,1)S(1)} %maximum_bitcast_fusion), channel_id=1, source_target_pairs={{0,8},{8,16},{16,24},{24,32},{32,40},{40,48},{48,56},{56,64},{64,7... | collective-permute-start | bytes 1572872 | tf_op jit(solution)/shard_map/ppermute | solution.py:33
  7.4 20.4 %copy-start.2 = (bf16[256,8,128]{2,1,0:T(8,128)(2,1)S(1)}, bf16[256,8,128]{2,1,0:T(8,128)(2,1)}, u32[]{:S(2)}) copy-start(bf16[256,8,128]{2,1,0:T(8,128)(2,1)} %key_ref.1) | copy-start | bytes 1572868
  7.5 20.4 %copy-start.3 = (bf16[256,8,128]{2,1,0:T(8,128)(2,1)S(1)}, bf16[256,8,128]{2,1,0:T(8,128)(2,1)}, u32[]{:S(2)}) copy-start(bf16[256,8,128]{2,1,0:T(8,128)(2,1)} %value_ref.1) | copy-start | bytes 1572868
  7.5 20.4 %copy-start.5 = (s32[128]{0:T(128)S(1)}, s32[128]{0:T(128)}, u32[]{:S(2)}) copy-start(s32[128]{0:T(128)} %param.11) | copy-start | bytes 1540
  7.5 24.3 %all-to-all-start = ((bf16[8,2,256,128]{3,2,1,0:T(8,128)(2,1)}), bf16[8,2,256,128]{3,2,1,0:T(8,128)(2,1)S(1)}, u32[]{:S(2)}, u32[]{:S(2)}) async-start(bf16[8,2,256,128]{3,2,1,0:T(8,128)(2,1)} %query_prepare_kernel.1.qd_ref.qd_all_ref.qd_here_ref), calls=%async_computation | async-start | bytes 2097152 | tf_op jit(solution)/shard_map/all_to_all | solution.py:279
  25.9 4.8 %collective-permute-start.1 = (bf16[8,256,128]{2,1,0:T(8,128)(2,1)S(1)}, bf16[8,256,128]{2,1,0:T(8,128)(2,1)S(1)}, u32[]{:S(2)}, u32[]{:S(2)}) collective-permute-start(bf16[8,256,128]{2,1,0:T(8,128)(2,1)S(1)} %collective-permute-done.here_ref), channel_id=1, source_target_pairs={{0,1},{1,0},{2,3},{3,2},{4,5},{5,4},{6,7},{7,6},{8,9},{9,8},{10,11... | collective-permute-start | bytes 1572872 | tf_op jit(solution)/shard_map/ppermute | solution.py:290
  34.4 8.3 %collective-permute-start.2 = (bf16[2,256,128]{2,1,0:T(8,128)(2,1)S(1)}, bf16[2,256,128]{2,1,0:T(8,128)(2,1)S(1)}, u32[]{:S(2)}, u32[]{:S(2)}) collective-permute-start(bf16[2,256,128]{2,1,0:T(8,128)(2,1)S(1)} %get-tuple-element.22), channel_id=1, source_target_pairs={{8,0},{16,8},{24,16},{32,24},{40,32},{48,40},{56,48},{64,56},{72,6... | collective-permute-start | bytes 393224 | tf_op jit(solution)/shard_map/ppermute | solution.py:33

commit v9 on v8

--- a/solution.py
+++ b/solution.py
@@ -211,16 +211,16 @@
         reach = slice(second * half, (second + 3) * half)
         middle, corner = bias_ref[:rows, lanes], bias_ref[rows:, lanes]
         bias = jnp.concatenate([middle, corner] if second else [corner, middle], axis=0).astype(F32)
-        bias = jnp.concatenate([bias, bias], axis=1)
-        for h in range(0, heads, 2):
-            query = qd_ref[h : h + 2, 0, lanes].reshape(rows, width)
-            dout = qd_ref[h : h + 2, 1, lanes].reshape(rows, width)
+        bias = jnp.concatenate([bias] * 4, axis=1)
+        for h in range(0, heads, 4):
+            query = qd_ref[h : h + 4, 0, lanes].reshape(2 * rows, width)
+            dout = qd_ref[h : h + 4, 1, lanes].reshape(2 * rows, width)
             scores = dot_nt(key[reach], query) * (scaling * math.log2(math.e)) + bias
             shifted_exp = jnp.exp2(scores - jnp.max(scores, axis=0, keepdims=True))
             probs = shifted_exp * (1.0 / jnp.sum(shifted_exp, axis=0, keepdims=True))
             grad_probs = dot_nt(value[reach], dout)
             row_delta = jnp.sum(probs * grad_probs, axis=0, keepdims=True)
-            at = pl.ds(h * half, rows)
+            at = pl.ds(h * half, 2 * rows)
             terms[second, 0, :, at] = (probs * (grad_probs - row_delta)).astype(BF16)
             terms[second, 1, :, at] = probs.astype(BF16)
     for i, factor in ((0, scaling), (1, 1.0)):

time: 43.6 us -> 43.6 us (level)
  no operation moved by 1% of the time
where the time goes in v9:
time: 43.6 us; the launch traced here: 43.3 us
  starting transfers between devices  16.1 us (37%)
  waiting for transfers between devices  14.6 us (33%)
  Pallas kernels  10.1 us (23%)
  local copies, waits for them, and re-layouts  1.59 us (4%)
  between operations  0.84 us (2%)
    ppermute x2, waiting for transfers between devices, shifted(): return lax.ppermute(block, axis, route)  14.6 us
    pallas_call x7, Pallas kernels, call(): pl.pallas_call(kernel, in_specs=[VMEM] * (len(operands) - 1) + [last], ou...  10.1 us
    ppermute x2, starting transfers between devices, shifted(): return lax.ppermute(block, axis, route)  9.7 us
    all_to_all x1, starting transfers between devices, per_device(): qd_group = lax.all_to_all(qd, 'tp', split_axis=0, concat_axis=0, tiled=True)  4.44 us
    ppermute x1, starting transfers between devices, per_device(): lax.ppermute(here, 'tp', [(d, d ^ 1) for d in range(lax.axis_size('tp'))])  1.91 us
    dynamic_slice x1, local copies, waits for them, and re-layouts, per_device(): lax.dynamic_slice(block, (0, (device & 1) * half, 0), (rows, half, width))  1.48 us
  transfers between devices with their start and end apart: 4, of which 2 were waited for; matrix products, arithmetic and copies ran while one was open for 0% of the time, Pallas kernels for 16%

profile of v9, /device:TPU:24, one launch (start us, length us, event | category | flops | bytes accessed | tf_op | source)
XLA Modules:
  0.0 43.3 jit_solution(4439469042540921993)
XLA Ops:
  0.6 1.5 %constant_dynamic-slice_fusion = (bf16[256,4,128]{2,1,0:T(4,128)(2,1)S(1)}, bf16[256,4,128]{2,1,0:T(4,128)(2,1)S(1)}) fusion(bf16[256,8,128]{2,1,0:T(8,128)(2,1)} %value_ref.1, s32[]{:T(128)S(6)} %select_n.4, bf16[256,8,128]{2,1,0:T(8,128)(2,1)} %key_ref.1), kind=kLoop, calls=%fused_computation.1 | loop fusion | bytes 1048580 | tf_op jit(solution)/shard_map/dynamic_slice | solution.py:266
  2.1 0.0 copy-start
  2.1 0.0 copy-start.1
  2.1 0.0 copy-start.4
  2.3 4.0 %collective-permute-start = (bf16[8,256,128]{2,1,0:T(8,128)(2,1)S(1)}, bf16[8,256,128]{2,1,0:T(8,128)(2,1)S(1)}, u32[]{:S(2)}, u32[]{:S(2)}) collective-permute-start(bf16[8,256,128]{2,1,0:T(8,128)(2,1)S(1)} %maximum_bitcast_fusion), channel_id=1, source_target_pairs={{0,8},{8,16},{16,24},{24,32},{32,40},{40,48},{48,56},{56,64},{64,7... | collective-permute-start | bytes 1572872 | tf_op jit(solution)/shard_map/ppermute | solution.py:33
  6.3 0.0 copy-done
  6.3 0.0 copy-done.1
  6.3 0.0 copy-done.4
  6.3 1.1 %query_prepare_kernel.1.qd_ref.qd_all_ref.qd_here_ref = bf16[8,2,256,128]{3,2,1,0:T(8,128)(2,1)} custom-call(s32[2,8]{1,0:T(2,128)S(1)} %bitcast.13, bf16[256,8,128]{2,1,0:T(8,128)(2,1)S(1)} %bitcast.11, bf16[256,8,128]{2,1,0:T(8,128)(2,1)S(1)} %bitcast.12), custom_call_target="tpu_custom_call" | custom-call | flops 1000000 | bytes 1048576 | tf_op jit(solution)/shard_map/query_prepare_kernel/pallas_call | solution.py:254
  7.4 0.0 copy-start.2
  7.5 0.0 copy-start.3
  7.5 0.0 copy-start.5
  7.5 4.4 %all-to-all-start = ((bf16[8,2,256,128]{3,2,1,0:T(8,128)(2,1)}), bf16[8,2,256,128]{3,2,1,0:T(8,128)(2,1)S(1)}, u32[]{:S(2)}, u32[]{:S(2)}) async-start(bf16[8,2,256,128]{3,2,1,0:T(8,128)(2,1)} %query_prepare_kernel.1.qd_ref.qd_all_ref.qd_here_ref), calls=%async_computation | async-start | bytes 2097152 | tf_op jit(solution)/shard_map/all_to_all | solution.py:279
  11.9 14.0 %collective-permute-done.here_ref = bf16[8,256,128]{2,1,0:T(8,128)(2,1)S(1)} collective-permute-done((bf16[8,256,128]{2,1,0:T(8,128)(2,1)S(1)}, bf16[8,256,128]{2,1,0:T(8,128)(2,1)S(1)}, u32[]{:S(2)}, u32[]{:S(2)}) %collective-permute-start) | collective-permute-done | bytes 524320 | tf_op jit(solution)/shard_map/ppermute | solution.py:33
  25.9 1.9 %collective-permute-start.1 = (bf16[8,256,128]{2,1,0:T(8,128)(2,1)S(1)}, bf16[8,256,128]{2,1,0:T(8,128)(2,1)S(1)}, u32[]{:S(2)}, u32[]{:S(2)}) collective-permute-start(bf16[8,256,128]{2,1,0:T(8,128)(2,1)S(1)} %collective-permute-done.here_ref), channel_id=1, source_target_pairs={{0,1},{1,0},{2,3},{3,2},{4,5},{5,4},{6,7},{7,6},{8,9},{9,8},{10,11... | collective-permute-start | bytes 1572872 | tf_op jit(solution)/shard_map/ppermute | solution.py:290
  27.8 0.0 copy-done.2
  27.9 0.0 copy-done.3
  27.9 0.0 copy-done.5
  27.9 1.1 %key_prepare_kernel.1 = (bf16[2,8,256,128]{3,2,1,0:T(8,128)(2,1)S(1)}, bf16[384,256]{1,0:T(8,128)(2,1)S(1)}, bf16[4,2,256,128]{3,2,1,0:T(8,128)(2,1)S(1)}) custom-call(s32[1,128]{1,0:T(1,128)S(1)} %bitcast.14, bf16[256,8,128]{2,1,0:T(8,128)(2,1)S(1)} %copy-done.2, bf16[256,8,128]{2,1,0:T(8,128)(2,1)S(1)} %copy-done.3, ...), custom_call_target="tpu_custom_call" | custom-call | flops 5369709056 | bytes 1048576 | tf_op jit(solution)/shard_map/key_prepare_kernel/pallas_call | solution.py:254
  28.9 1.8 %early_query_kernel.1 = (bf16[4,256,128]{2,1,0:T(8,128)(2,1)S(1)}, bf16[2,2,256,128]{3,2,1,0:T(8,128)(2,1)S(1)}) custom-call(bf16[384,256]{1,0:T(8,128)(2,1)S(1)} %get-tuple-element.15.bias_ref, bf16[8,256,128]{2,1,0:T(8,128)(2,1)S(1)} %collective-permute-done.here_ref, bf16[2,8,256,128]{3,2,1,0:T(8,128)(2,1)S(1)} %get-tuple-element.16.kv_ref, ...), custom_call_target="tpu_custom_call" | custom-call | flops 269435456 | bytes 1048576 | tf_op jit(solution)/shard_map/early_query_kernel/pallas_call | solution.py:254
  30.8 0.0 collective-permute-done.1.other_ref
  30.8 1.0 %middle_query_kernel.1.stash_ref = bf16[20,256,128]{2,1,0:T(8,128)(2,1)S(1)} custom-call(bf16[384,256]{1,0:T(8,128)(2,1)S(1)} %get-tuple-element.15.bias_ref, bf16[8,256,128]{2,1,0:T(8,128)(2,1)S(1)} %collective-permute-done.here_ref, bf16[8,256,128]{2,1,0:T(8,128)(2,1)S(1)} %collective-permute-done.1.other_ref, ...), custom_call_target="tpu_custom_call" | custom-call | flops 269435456 | bytes 1048576 | tf_op jit(solution)/shard_map/middle_query_kernel/pallas_call | solution.py:254
  31.8 0.0 all-to-all-done.qd_ref
  31.8 2.5 %key_side_kernel.1 = (bf16[2,256,128]{2,1,0:T(8,128)(2,1)S(1)}, f32[2,256,128]{2,1,0:T(8,128)S(1)}, bf16[2,2,256,128]{3,2,1,0:T(8,128)(2,1)S(1)}) custom-call(bf16[384,256]{1,0:T(8,128)(2,1)S(1)} %get-tuple-element.15.bias_ref, bf16[8,2,256,128]{3,2,1,0:T(8,128)(2,1)S(1)} %all-to-all-done.qd_ref, bf16[20,256,128]{2,1,0:T(8,128)(2,1)S(1)} %middle_query_kernel.1.stash_ref, ...), custom_call_target="tpu_custom_call" | custom-call | flops 1074741760 | bytes 1048576 | tf_op jit(solution)/shard_map/key_side_kernel/pallas_call | solution.py:254
  34.3 5.7 %collective-permute-start.2 = (bf16[2,256,128]{2,1,0:T(8,128)(2,1)S(1)}, bf16[2,256,128]{2,1,0:T(8,128)(2,1)S(1)}, u32[]{:S(2)}, u32[]{:S(2)}) collective-permute-start(bf16[2,256,128]{2,1,0:T(8,128)(2,1)S(1)} %get-tuple-element.22), channel_id=1, source_target_pairs={{8,0},{16,8},{24,16},{32,24},{40,32},{48,40},{56,48},{64,56},{72,6... | collective-permute-start | bytes 393224 | tf_op jit(solution)/shard_map/ppermute | solution.py:33
  40.1 1.9 %late_query_kernel.1 = bf16[256,8,128]{2,1,0:T(8,128)(2,1)} custom-call(bf16[384,256]{1,0:T(8,128)(2,1)S(1)} %get-tuple-element.15.bias_ref, bf16[20,256,128]{2,1,0:T(8,128)(2,1)S(1)} %middle_query_kernel.1.stash_ref, bf16[2,2,256,128]{3,2,1,0:T(8,128)(2,1)S(1)} %get-tuple-element.20.qd_ref), custom_call_target="tpu_custom_call" | custom-call | flops 806306368 | bytes 1048576 | tf_op jit(solution)/shard_map/late_query_kernel/pallas_call | solution.py:254
  42.0 0.6 %collective-permute-done.2.back_ref = bf16[2,256,128]{2,1,0:T(8,128)(2,1)S(1)} collective-permute-done((bf16[2,256,128]{2,1,0:T(8,128)(2,1)S(1)}, bf16[2,256,128]{2,1,0:T(8,128)(2,1)S(1)}, u32[]{:S(2)}, u32[]{:S(2)}) %collective-permute-start.2) | collective-permute-done | bytes 131104 | tf_op jit(solution)/shard_map/ppermute | solution.py:33
  42.6 0.7 %finish_kernel.1 = (bf16[256,128]{1,0:T(8,128)(2,1)}, bf16[256,128]{1,0:T(8,128)(2,1)}) custom-call(f32[2,256,128]{2,1,0:T(8,128)S(1)} %get-tuple-element.21.own_ref, bf16[2,256,128]{2,1,0:T(8,128)(2,1)S(1)} %collective-permute-done.2.back_ref), custom_call_target="tpu_custom_call" | custom-call | flops 1000000 | bytes 1048576 | tf_op jit(solution)/shard_map/finish_kernel/pallas_call | solution.py:254
  (3 shorter events, 0.1 us)
Async XLA Ops:
  2.1 4.2 %copy-start = (bf16[256,8,1,128]{3,1,2,0:T(8,128)(2,1)S(1)}, bf16[256,8,1,128]{3,1,2,0:T(8,128)(2,1)}, u32[]{:S(2)}) copy-start(bf16[256,8,1,128]{3,1,2,0:T(8,128)(2,1)} %param.6) | copy-start | bytes 1572868
  2.1 4.1 %copy-start.1 = (bf16[256,8,1,128]{3,1,2,0:T(8,128)(2,1)S(1)}, bf16[256,8,1,128]{3,1,2,0:T(8,128)(2,1)}, u32[]{:S(2)}) copy-start(bf16[256,8,1,128]{3,1,2,0:T(8,128)(2,1)} %param.9) | copy-start | bytes 1572868
  2.1 4.1 %copy-start.4 = (s32[2,8,1]{1,2,0:T(1,128)S(1)}, s32[2,8,1]{1,2,0:T(1,128)}, u32[]{:S(2)}) copy-start(s32[2,8,1]{1,2,0:T(1,128)} %param.10) | copy-start | bytes 196
  2.3 23.6 %collective-permute-start = (bf16[8,256,128]{2,1,0:T(8,128)(2,1)S(1)}, bf16[8,256,128]{2,1,0:T(8,128)(2,1)S(1)}, u32[]{:S(2)}, u32[]{:S(2)}) collective-permute-start(bf16[8,256,128]{2,1,0:T(8,128)(2,1)S(1)} %maximum_bitcast_fusion), channel_id=1, source_target_pairs={{0,8},{8,16},{16,24},{24,32},{32,40},{40,48},{48,56},{56,64},{64,7... | collective-permute-start | bytes 1572872 | tf_op jit(solution)/shard_map/ppermute | solution.py:33
  7.4 20.4 %copy-start.2 = (bf16[256,8,128]{2,1,0:T(8,128)(2,1)S(1)}, bf16[256,8,128]{2,1,0:T(8,128)(2,1)}, u32[]{:S(2)}) copy-start(bf16[256,8,128]{2,1,0:T(8,128)(2,1)} %key_ref.1) | copy-start | bytes 1572868
  7.5 20.4 %copy-start.3 = (bf16[256,8,128]{2,1,0:T(8,128)(2,1)S(1)}, bf16[256,8,128]{2,1,0:T(8,128)(2,1)}, u32[]{:S(2)}) copy-start(bf16[256,8,128]{2,1,0:T(8,128)(2,1)} %value_ref.1) | copy-start | bytes 1572868
  7.5 20.4 %copy-start.5 = (s32[128]{0:T(128)S(1)}, s32[128]{0:T(128)}, u32[]{:S(2)}) copy-start(s32[128]{0:T(128)} %param.11) | copy-start | bytes 1540
  7.5 24.3 %all-to-all-start = ((bf16[8,2,256,128]{3,2,1,0:T(8,128)(2,1)}), bf16[8,2,256,128]{3,2,1,0:T(8,128)(2,1)S(1)}, u32[]{:S(2)}, u32[]{:S(2)}) async-start(bf16[8,2,256,128]{3,2,1,0:T(8,128)(2,1)} %query_prepare_kernel.1.qd_ref.qd_all_ref.qd_here_ref), calls=%async_computation | async-start | bytes 2097152 | tf_op jit(solution)/shard_map/all_to_all | solution.py:279
  25.9 4.8 %collective-permute-start.1 = (bf16[8,256,128]{2,1,0:T(8,128)(2,1)S(1)}, bf16[8,256,128]{2,1,0:T(8,128)(2,1)S(1)}, u32[]{:S(2)}, u32[]{:S(2)}) collective-permute-start(bf16[8,256,128]{2,1,0:T(8,128)(2,1)S(1)} %collective-permute-done.here_ref), channel_id=1, source_target_pairs={{0,1},{1,0},{2,3},{3,2},{4,5},{5,4},{6,7},{7,6},{8,9},{9,8},{10,11... | collective-permute-start | bytes 1572872 | tf_op jit(solution)/shard_map/ppermute | solution.py:290
  34.3 8.3 %collective-permute-start.2 = (bf16[2,256,128]{2,1,0:T(8,128)(2,1)S(1)}, bf16[2,256,128]{2,1,0:T(8,128)(2,1)S(1)}, u32[]{:S(2)}, u32[]{:S(2)}) collective-permute-start(bf16[2,256,128]{2,1,0:T(8,128)(2,1)S(1)} %get-tuple-element.22), channel_id=1, source_target_pairs={{8,0},{16,8},{24,16},{32,24},{40,32},{48,40},{56,48},{64,56},{72,6... | collective-permute-start | bytes 393224 | tf_op jit(solution)/shard_map/ppermute | solution.py:33
